TPU v7x, 32 devices: a whole 2x2x4 slice. The times are simulated.
32 devices in a mesh: ctx: 8 (over z, x), ch: 4 (over y, core).
Axes of the slice: x: 2, y: 2, z: 4, core: 2. Of those that a mesh axis runs over, the one named last changes fastest.
Arguments:
- query: bfloat16 [1024, 8192], P('ctx', 'ch'), may hold values from -6 to 6
- key: bfloat16 [1024, 8192], P('ctx', 'ch'), may hold values from -6 to 6
- value: bfloat16 [1024, 8192], P('ctx', 'ch'), may hold values from -6 to 6
- filter_taps: bfloat16 [1024, 512], P('ctx', 'ch'), may hold values from -0.1875 to 0.1875
- skip: float32 [8192], P('ch'), may hold values from -1 to 1
Outputs:
- gated: bfloat16 [1024, 8192], P('ctx', 'ch')
All inputs are finite; a program needn't handle non-finite values.
Results may differ from a plain program's by a relative error of at most 0.0085.
Values may be sent and summed in bfloat16 or wider, within the bound.
No kernel may reach another device: no remote copies, remote signals or barrier semaphores. Data moves between devices by JAX's collectives and lax.ppermute only.
A program may use at most 192 MiB of HBM per device.

v0:
```python
import jax
import jax.numpy as jnp
from jax import lax
from jax.sharding import PartitionSpec as P

GROUP = 16
BLOCK = 128
LAGS = 8


def from_behind(value, axis, steps):
    count = lax.axis_size(axis)
    leading, last = (max(0, -steps), min(count, count - steps))
    return lax.ppermute(value, axis, [(source, source + steps) for source in range(leading, last)])


def all_toeplitz(padded, width, count):
    lag_part = jnp.arange(count, dtype=jnp.int32)[:, None, None] * width
    row_part = jnp.arange(width, dtype=jnp.int32)[None, :, None]
    col_part = jnp.arange(width, dtype=jnp.int32)[None, None, :]
    indices = lag_part + width + row_part - col_part
    return jnp.take(padded, indices, axis=1)


def per_device(query, key, value, filter_taps, skip):
    rows = query.shape[0]
    channels = query.shape[1]
    groups = channels // GROUP
    all_taps = lax.all_gather(filter_taps, "ctx", axis=0, tiled=True)
    mixed = (key.astype(jnp.float32) * value.astype(jnp.float32)).astype(jnp.bfloat16)
    mixed_cols = mixed.T.reshape(groups, GROUP, rows)
    padded = jnp.concatenate(
        [
            jnp.zeros((groups, BLOCK), jnp.bfloat16),
            all_taps.T,
            jnp.zeros((groups, BLOCK), jnp.bfloat16),
        ],
        axis=1,
    )
    toeplitz_all = all_toeplitz(padded, BLOCK, LAGS)

    def convolve(lag_index, source):
        return jnp.einsum(
            "gts,gcs->gct", toeplitz_all[:, lag_index], source, preferred_element_type=jnp.float32
        )

    summed = convolve(0, mixed_cols)
    moving = mixed_cols
    for lag_index in range(1, LAGS):
        moving = from_behind(moving, "ctx", 1)
        summed = summed + convolve(lag_index, moving)
    conv = summed.reshape(channels, rows).T
    gated = query.astype(jnp.float32) * (conv + skip[None, :] * mixed.astype(jnp.float32))
    return gated.astype(jnp.bfloat16)


def solution(mesh):
    placed = (P("ctx", "ch"), P("ctx", "ch"), P("ctx", "ch"), P("ctx", "ch"), P("ch"))
    return jax.shard_map(
        per_device, mesh=mesh, in_specs=placed, out_specs=P("ctx", "ch"), check_vma=False
    )
```

profile of v0, /device:TPU:0, one launch (start us, length us, event | category | flops | bytes accessed | tf_op | source)
XLA Modules:
  0.0 648.5 jit_solution(3448024036053329940)
XLA Ops:
  0.0 1.3 fusion.20
  1.3 0.3 copy.8
  1.6 4.9 collective-permute-start
  6.5 0.1 iota_add_fusion
  6.6 0.2 compare_select_fusion
  6.8 10.8 %collective-permute-done = bf16[128,16,128]{2,1,0:T(8,128)(2,1)S(1)} collective-permute-done((bf16[128,16,128]{2,1,0:T(8,128)(2,1)S(1)}, bf16[128,16,128]{2,1,0:T(8,128)(2,1)S(1)}, u32[]{:S(2)}, u32[]{:S(2)}) %collective-permute-start) | collective-permute-done | bytes 524320 | tf_op jit(solution)/shard_map/ppermute | solution.py:14
  17.6 4.4 collective-permute-start.1
  22.0 0.1 broadcast_clamp_fusion
  22.1 10.2 %collective-permute-done.1 = bf16[128,16,128]{2,1,0:T(8,128)(2,1)S(1)} collective-permute-done((bf16[128,16,128]{2,1,0:T(8,128)(2,1)S(1)}, bf16[128,16,128]{2,1,0:T(8,128)(2,1)S(1)}, u32[]{:S(2)}, u32[]{:S(2)}) %collective-permute-start.1) | collective-permute-done | bytes 524320 | tf_op jit(solution)/shard_map/ppermute | solution.py:14
  32.3 0.0 copy-start.2
  32.3 5.2 collective-permute-start.2
  37.5 37.2 %all_gather.3 = bf16[1024,128]{1,0:T(8,128)(2,1)S(1)} all-gather(bf16[128,128]{1,0:T(8,128)(2,1)} %param.8), channel_id=1, replica_groups=mesh['ctx'=8,'ch'=4] {'ctx'}, dimensions={0}, use_global_device_ids=true | all-gather | bytes 294912 | tf_op jit(solution)/shard_map/all_gather | solution.py:29
  74.8 453.9 %gather_fusion = bf16[131072,128]{1,0:T(8,128)(2,1)} fusion(bf16[128,1280]{0,1:T(8,128)(2,1)S(1)} %pad_maximum_fusion, s32[131072]{0:T(1024)S(1)} %broadcast_clamp_fusion), kind=kCustom, calls=%fused_computation | custom fusion | bytes 67633152 | tf_op jit(solution)/shard_map/jit(_take)/gather | solution.py:22
  528.7 0.0 copy-done.2
  528.7 46.0 %copy.9 = bf16[8,128,128,128]{2,1,3,0:T(8,128)(2,1)} copy(bf16[8,128,128,128]{3,2,1,0:T(8,128)(2,1)} %bitcast.61) | data formatting | bytes 67108864 | tf_op jit(solution)/shard_map/jit(_take)/gather | solution.py:22
  574.7 0.2 fusion.19
  574.9 0.0 copy-start.3
  574.9 0.0 collective-permute-done.2
  574.9 2.5 collective-permute-start.3
  577.4 22.9 %select_bitcast_fusion = bf16[128,8,128,128]{3,2,0,1:T(8,128)(2,1)} fusion(bf16[8,128,128,128]{2,1,3,0:T(8,128)(2,1)} %copy.9, pred[8,128,128]{2,1,0:T(8,128)(4,1)S(1)} %fusion.19), kind=kLoop, calls=%fused_computation.1 | loop fusion | flops 16777216 | bytes 67239936 | tf_op jit(solution)/shard_map/jit(_take)/select_n | solution.py:22
  600.4 0.0 copy-start
  600.4 0.0 copy-start.1
  600.4 0.0 copy-start.4
  600.4 4.5 fusion.7
  605.0 0.0 collective-permute-done.3
  605.0 1.9 collective-permute-start.4
  606.9 4.5 fusion.8
  611.4 0.0 copy-done.3
  611.4 4.5 fusion.9
  615.9 0.0 collective-permute-done.4
  615.9 3.8 collective-permute-start.5
  619.6 4.6 fusion.10
  624.3 4.7 fusion.11
  628.9 0.0 collective-permute-done.5
  628.9 3.7 collective-permute-start.6
  632.6 4.5 fusion.12
  637.0 4.5 fusion.13
  641.5 0.0 collective-permute-done.6
  641.5 4.5 fusion.14
  646.0 0.4 copy.10
  646.4 0.0 copy-done
  646.4 0.0 copy-done.1
  646.4 0.0 copy-done.4
  646.4 2.1 fusion.16
  (3 shorter events, 0.0 us)
Async XLA Ops:
  1.6 16.0 %collective-permute-start = (bf16[128,16,128]{2,1,0:T(8,128)(2,1)S(1)}, bf16[128,16,128]{2,1,0:T(8,128)(2,1)S(1)}, u32[]{:S(2)}, u32[]{:S(2)}) collective-permute-start(bf16[128,16,128]{2,1,0:T(8,128)(2,1)S(1)} %bitcast.64), channel_id=1, source_target_pairs={{0,4},{4,8},{8,12},{12,16},{16,20},{20,24},{24,28},{1,5},{5,9},{9,... | collective-permute-start | bytes 1572872 | tf_op jit(solution)/shard_map/ppermute | solution.py:14
  17.6 14.7 %collective-permute-start.1 = (bf16[128,16,128]{2,1,0:T(8,128)(2,1)S(1)}, bf16[128,16,128]{2,1,0:T(8,128)(2,1)S(1)}, u32[]{:S(2)}, u32[]{:S(2)}) collective-permute-start(bf16[128,16,128]{2,1,0:T(8,128)(2,1)S(1)} %collective-permute-done), channel_id=1, source_target_pairs={{0,4},{4,8},{8,12},{12,16},{16,20},{20,24},{24,28},{1,5},{5,9},{9,... | collective-permute-start | bytes 1572872 | tf_op jit(solution)/shard_map/ppermute | solution.py:14
  32.3 496.4 %copy-start.2 = (bf16[128,16,128]{2,1,0:T(8,128)(2,1)}, bf16[128,16,128]{2,1,0:T(8,128)(2,1)S(1)}, u32[]{:S(2)}) copy-start(bf16[128,16,128]{2,1,0:T(8,128)(2,1)S(1)} %collective-permute-done.1) | copy-start | bytes 1572868
  32.3 542.6 %collective-permute-start.2 = (bf16[128,16,128]{2,1,0:T(8,128)(2,1)S(1)}, bf16[128,16,128]{2,1,0:T(8,128)(2,1)}, u32[]{:S(2)}, u32[]{:S(2)}) collective-permute-start(bf16[128,16,128]{2,1,0:T(8,128)(2,1)S(1)} %collective-permute-done.1), channel_id=1, source_target_pairs={{0,4},{4,8},{8,12},{12,16},{16,20},{20,24},{24,28},{1,5},{5,9},{9,... | collective-permute-start | bytes 1572872 | tf_op jit(solution)/shard_map/ppermute | solution.py:14
  574.9 36.5 %copy-start.3 = (bf16[128,16,128]{2,1,0:T(8,128)(2,1)S(1)}, bf16[128,16,128]{2,1,0:T(8,128)(2,1)}, u32[]{:S(2)}) copy-start(bf16[128,16,128]{2,1,0:T(8,128)(2,1)} %copy-done.2) | copy-start | bytes 1572868
  574.9 30.0 %collective-permute-start.3 = (bf16[128,16,128]{2,1,0:T(8,128)(2,1)}, bf16[128,16,128]{2,1,0:T(8,128)(2,1)}, u32[]{:S(2)}, u32[]{:S(2)}) collective-permute-start(bf16[128,16,128]{2,1,0:T(8,128)(2,1)} %collective-permute-done.2), channel_id=1, source_target_pairs={{0,4},{4,8},{8,12},{12,16},{16,20},{20,24},{24,28},{1,5},{5,9},{9,... | collective-permute-start | bytes 1572872 | tf_op jit(solution)/shard_map/ppermute | solution.py:14
  600.4 46.0 %copy-start = (bf16[128,2048]{1,0:T(8,128)(2,1)S(1)}, bf16[128,2048]{1,0:T(8,128)(2,1)}, u32[]{:S(2)}) copy-start(bf16[128,2048]{1,0:T(8,128)(2,1)} %param.7) | copy-start | bytes 1572868
  600.4 46.0 %copy-start.1 = (bf16[128,2048]{1,0:T(8,128)(2,1)S(1)}, bf16[128,2048]{1,0:T(8,128)(2,1)}, u32[]{:S(2)}) copy-start(bf16[128,2048]{1,0:T(8,128)(2,1)} %param.6) | copy-start | bytes 1572868
  600.4 46.0 %copy-start.4 = (f32[2048]{0:T(1024)S(1)}, f32[2048]{0:T(1024)}, u32[]{:S(2)}) copy-start(f32[2048]{0:T(1024)} %param.9) | copy-start | bytes 24580
  605.0 10.9 %collective-permute-start.4 = (bf16[128,16,128]{2,1,0:T(8,128)(2,1)}, bf16[128,16,128]{2,1,0:T(8,128)(2,1)S(1)}, u32[]{:S(2)}, u32[]{:S(2)}) collective-permute-start(bf16[128,16,128]{2,1,0:T(8,128)(2,1)} %collective-permute-done.3), channel_id=1, source_target_pairs={{0,4},{4,8},{8,12},{12,16},{16,20},{20,24},{24,28},{1,5},{5,9},{9,... | collective-permute-start | bytes 1572872 | tf_op jit(solution)/shard_map/ppermute | solution.py:14
  615.9 13.1 %collective-permute-start.5 = (bf16[128,16,128]{2,1,0:T(8,128)(2,1)S(1)}, bf16[128,16,128]{2,1,0:T(8,128)(2,1)S(1)}, u32[]{:S(2)}, u32[]{:S(2)}) collective-permute-start(bf16[128,16,128]{2,1,0:T(8,128)(2,1)S(1)} %collective-permute-done.4), channel_id=1, source_target_pairs={{0,4},{4,8},{8,12},{12,16},{16,20},{20,24},{24,28},{1,5},{5,9},{9,... | collective-permute-start | bytes 1572872 | tf_op jit(solution)/shard_map/ppermute | solution.py:14
  628.9 12.6 %collective-permute-start.6 = (bf16[128,16,128]{2,1,0:T(8,128)(2,1)S(1)}, bf16[128,16,128]{2,1,0:T(8,128)(2,1)S(1)}, u32[]{:S(2)}, u32[]{:S(2)}) collective-permute-start(bf16[128,16,128]{2,1,0:T(8,128)(2,1)S(1)} %collective-permute-done.5), channel_id=1, source_target_pairs={{0,4},{4,8},{8,12},{12,16},{16,20},{20,24},{24,28},{1,5},{5,9},{9,... | collective-permute-start | bytes 1572872 | tf_op jit(solution)/shard_map/ppermute | solution.py:14
where the time goes:
time: 656 us; the launch traced here: 649 us
  local copies, waits for them, and re-layouts  501 us (76%)
  blocking collectives  37.2 us (6%)
  matrix products  36.2 us (6%)
  other arithmetic  27 us (4%)
  starting transfers between devices  26.3 us (4%)
  waiting for transfers between devices  21 us (3%)
    gather x2, local copies, waits for them, and re-layouts, all_toeplitz(): return jnp.take(padded, indices, axis=1)  500 us
    all_gather x1, blocking collectives, per_device(): all_taps = lax.all_gather(filter_taps, 'ctx', axis=0, tiled=True)  37.2 us
    dot_general x8, matrix products, convolve(): jnp.einsum('gts,gcs->gct', toeplitz_all[:, lag_index], source, preferred_...  36.2 us
    ppermute x7, starting transfers between devices, from_behind(): lax.ppermute(value, axis, [(source, source + steps) for source in range(l...  26.3 us
    select_n x2, other arithmetic, all_toeplitz(): return jnp.take(padded, indices, axis=1)  23.2 us
    ppermute x7, waiting for transfers between devices, from_behind(): lax.ppermute(value, axis, [(source, source + steps) for source in range(l...  21 us
  transfers between devices with their start and end apart: 7, of which 2 were waited for; matrix products, arithmetic and copies ran while one was open for 86% of the time, Pallas kernels for 0%

commit v1 on v0

v1 whole, which is shorter than its diff:
```python
import jax
import jax.numpy as jnp
from jax import lax
from jax.experimental import pallas as pl
from jax.experimental.pallas import tpu as pltpu
from jax.sharding import PartitionSpec as P

GROUP = 16
BLOCK = 128
LAGS = 8
LANES = 128
TILE = 16
SIDE = LANES // GROUP


def swap_granules(tiles):
    granule = lax.broadcasted_iota(jnp.int32, tiles[0].shape, 1) // GROUP
    tiles = list(tiles)
    for bit in (1, 2, 4):
        high = (granule & bit) != 0
        swapped = list(tiles)
        for low_index in range(SIDE):
            if low_index & bit:
                continue
            low, top = tiles[low_index], tiles[low_index | bit]
            swapped[low_index] = jnp.where(high, pltpu.roll(top, bit * GROUP, 1), low)
            swapped[low_index | bit] = jnp.where(high, top, pltpu.roll(low, LANES - bit * GROUP, 1))
        tiles = swapped
    return tiles


def mix_kernel(parts, key_ref, value_ref, taps_ref, sent_ref):
    width = sent_ref.shape[2]
    tap = lax.broadcasted_iota(jnp.int32, (BLOCK, LANES), 0)
    place = lax.broadcasted_iota(jnp.int32, (BLOCK, LANES), 1)
    mirror = jnp.where((tap + place) % BLOCK == 0, 1.0, 0.0).astype(jnp.bfloat16)
    mirrored = lax.dot_general(
        taps_ref[...], mirror, (((0,), (0,)), ((), ())), preferred_element_type=jnp.float32
    ).astype(jnp.bfloat16)
    for part in range(parts):
        columns = slice(part * width, (part + 1) * width)
        sent_ref[part, 0:BLOCK, :] = (
            key_ref[:, columns].astype(jnp.float32) * value_ref[:, columns].astype(jnp.float32)
        ).astype(jnp.bfloat16)
        own = mirrored[part * TILE : (part + 1) * TILE]
        for start in range(0, width, LANES):
            sent_ref[part, BLOCK : BLOCK + TILE, start : start + LANES] = own


def conv_kernel(sources, *refs):
    got_refs, (conv_ref, *all_gathered, results) = refs[:sources], refs[sources:]
    got_ref, gathered = got_refs[0], all_gathered[0]
    halves = conv_ref.shape[2] // LANES
    for half in range(halves):
        columns = slice(half * LANES, (half + 1) * LANES)

        @pl.loop(0, BLOCK // TILE)
        def _(step):
            rows = pl.ds(pl.multiple_of(step * TILE, TILE), TILE)
            for from_ref, to_ref in zip(got_refs, all_gathered):
                tiles = swap_granules([from_ref[block, rows, columns] for block in range(LAGS)])
                for index in range(SIDE):
                    to_ref[half * SIDE + index, rows, :] = tiles[index]

    lane = lax.broadcasted_iota(jnp.int32, (BLOCK, LANES), 1)
    row = lax.broadcasted_iota(jnp.int32, (BLOCK, LANES), 0)
    causal = row >= lane

    @pl.loop(0, halves * SIDE)
    def _(group):
        source = gathered[group]
        earlier = all_gathered[1][group] if sources > 1 else None
        before = jnp.zeros((BLOCK, LANES), jnp.float32)
        total = None
        filters, shifted = [], []
        for lag in range(LAGS):
            taps = got_ref[lag, BLOCK : BLOCK + TILE, 0:LANES].astype(jnp.float32)
            pick = lax.broadcasted_iota(jnp.int32, (TILE, LANES), 0) == group
            own = jnp.sum(jnp.where(pick, taps, 0.0), axis=0, keepdims=True)
            turned = pltpu.roll(jnp.broadcast_to(own, (BLOCK, LANES)), 0, 1, stride=1, stride_axis=0)
            filters.append(jnp.where(causal, turned, before).astype(jnp.bfloat16))
            before = turned
            if lag:
                moved = pltpu.roll(source, lag * GROUP, 1)
                carried = pltpu.roll(earlier, lag * GROUP, 1) if sources > 1 else jnp.zeros_like(moved)
                shifted.append(jnp.where(lane >= lag * GROUP, moved, carried))
            else:
                shifted.append(source)
        total = jnp.dot(
            jnp.concatenate(filters, axis=1),
            jnp.concatenate(shifted, axis=0),
            preferred_element_type=jnp.float32,
        )
        results[group] = total.astype(jnp.bfloat16)

    for half in range(halves):
        columns = slice(half * LANES, (half + 1) * LANES)

        @pl.loop(0, BLOCK // TILE)
        def _(step):
            rows = pl.ds(pl.multiple_of(step * TILE, TILE), TILE)
            tiles = swap_granules([results[half * SIDE + index, rows, :] for index in range(SIDE)])
            for block in range(LAGS):
                conv_ref[block, rows, columns] = tiles[block]


def gate_kernel(parts, query_ref, sent_ref, conv_ref, skip_ref, gated_ref):
    width = sent_ref.shape[2]
    for part in range(parts):
        columns = slice(part * width, (part + 1) * width)
        mixed = sent_ref[part, 0:BLOCK, :].astype(jnp.float32)
        summed = conv_ref[part].astype(jnp.float32) + skip_ref[:, columns] * mixed
        gated_ref[:, columns] = (query_ref[:, columns].astype(jnp.float32) * summed).astype(jnp.bfloat16)


def per_device(query, key, value, filter_taps, skip):
    rows, channels = query.shape
    parts = LAGS
    width = channels // parts
    count = lax.axis_size("ctx")
    windows = None
    if count > LAGS:
        windows = [list(range(first, first + LAGS)) for first in range(0, count, LAGS)]
        all_taps = lax.all_gather(filter_taps, "ctx", axis=0, tiled=True)
        first_tap = lax.axis_index("ctx") % LAGS * BLOCK
        filter_taps = lax.dynamic_slice_in_dim(all_taps, first_tap, BLOCK, axis=0)
    sent = pl.pallas_call(
        lambda *refs: mix_kernel(parts, *refs),
        out_shape=jax.ShapeDtypeStruct((parts, BLOCK + TILE, width), jnp.bfloat16),
    )(key, value, filter_taps)
    got = [lax.all_to_all(sent, "ctx", 0, 0, tiled=True, axis_index_groups=windows)]
    if count > LAGS:
        onward = [(source, source + LAGS) for source in range(count - LAGS)]
        got.append(lax.ppermute(got[0], "ctx", onward))
    conv = pl.pallas_call(
        lambda *refs: conv_kernel(len(got), *refs),
        out_shape=jax.ShapeDtypeStruct((parts, BLOCK, width), jnp.bfloat16),
        scratch_shapes=[pltpu.VMEM((width // GROUP, BLOCK, LANES), jnp.bfloat16)] * (len(got) + 1),
    )(*got)
    back = lax.all_to_all(conv, "ctx", 0, 0, tiled=True, axis_index_groups=windows)
    return pl.pallas_call(
        lambda *refs: gate_kernel(parts, *refs),
        out_shape=jax.ShapeDtypeStruct((rows, channels), jnp.bfloat16),
    )(query, sent, back, skip.reshape(1, channels))


def solution(mesh):
    placed = (P("ctx", "ch"), P("ctx", "ch"), P("ctx", "ch"), P("ctx", "ch"), P("ch"))
    return jax.shard_map(
        per_device, mesh=mesh, in_specs=placed, out_specs=P("ctx", "ch"), check_vma=False
    )
```

time: 656 us -> 61 us (0.09); the launches traced: 649 us -> 60.6 us
  local copies, waits for them, and re-layouts: 501 us -> 0 us
  matrix products: 36.2 us -> 0 us
  other arithmetic: 27 us -> 0 us
  starting transfers between devices: 26.3 us -> 0 us
  waiting for transfers between devices: 21 us -> 0 us
  Pallas kernels: 0 us -> 19 us
    gather x2 -> x0, local copies, waits for them, and re-layouts: 500 us -> none  [all_toeplitz(): return jnp.take(padded, indices, axis=1)]
    all_to_all x0 -> x2, blocking collectives: none -> 41.7 us  [the longest x1 23.9 us: per_device(): lax.all_to_all(sent, 'ctx', 0, 0, tiled=True, axis_index_groups=windows)]
    all_gather x1 -> x0, blocking collectives: 37.2 us -> none  [per_device(): all_taps = lax.all_gather(filter_taps, 'ctx', axis=0, tiled=True)]
    dot_general x8 -> x0, matrix products: 36.2 us -> none  [convolve(): jnp.einsum('gts,gcs->gct', toeplitz_all[:, lag_index], source, preferred_...]
    ppermute x7 -> x0, starting transfers between devices: 26.3 us -> none  [from_behind(): lax.ppermute(value, axis, [(source, source + steps) for source in range(l...]
    select_n x2 -> x0, other arithmetic: 23.2 us -> none  [all_toeplitz(): return jnp.take(padded, indices, axis=1)]
    ppermute x7 -> x0, waiting for transfers between devices: 21 us -> none  [from_behind(): lax.ppermute(value, axis, [(source, source + steps) for source in range(l...]
    pallas_call x0 -> x3, Pallas kernels: none -> 19 us  [the longest x1 14.3 us: per_device(): pl.pallas_call(lambda *refs: conv_kernel(len(got), *refs), out_shape=jax....]
  transfers between devices with their start and end apart: 7 -> 0, of which waited for: 2 -> 0; matrix products, arithmetic and copies ran while one was open for 86% -> 0% of each run, Pallas kernels for 0% -> 0%
where the time goes in v1:
time: 61 us; the launch traced here: 60.6 us
  blocking collectives  41.7 us (68%)
  Pallas kernels  19 us (31%)
    all_to_all x1, blocking collectives, per_device(): lax.all_to_all(sent, 'ctx', 0, 0, tiled=True, axis_index_groups=windows)  23.9 us
    all_to_all x1, blocking collectives, per_device(): lax.all_to_all(conv, 'ctx', 0, 0, tiled=True, axis_index_groups=windows)  17.7 us
    pallas_call x1, Pallas kernels, per_device(): pl.pallas_call(lambda *refs: conv_kernel(len(got), *refs), out_shape=jax....  14.3 us
    pallas_call x1, Pallas kernels, per_device(): pl.pallas_call(lambda *refs: gate_kernel(parts, *refs), out_shape=jax.Sha...  2.39 us
    pallas_call x1, Pallas kernels, per_device(): pl.pallas_call(lambda *refs: mix_kernel(parts, *refs), out_shape=jax.Shap...  2.26 us

profile of v1, /device:TPU:0, one launch (start us, length us, event | category | flops | bytes accessed | tf_op | source)
XLA Modules:
  0.0 60.6 jit_solution(16336323531431684670)
XLA Ops:
  0.0 2.3 %shard_map.55.refs_1_ = bf16[8,144,256]{2,1,0:T(8,128)(2,1)} custom-call(bf16[128,2048]{1,0:T(8,128)(2,1)} %refs_0_.2, bf16[128,2048]{1,0:T(8,128)(2,1)} %refs_1_.1, bf16[128,128]{1,0:T(8,128)(2,1)} %refs_2_.1), custom_call_target="tpu_custom_call" | custom-call | tf_op jit(solution)/shard_map/pallas_call | solution.py:127
  2.3 23.9 %all_to_all.10.refs_0_ = bf16[8,144,256]{2,1,0:T(8,128)(2,1)} all-to-all(bf16[8,144,256]{2,1,0:T(8,128)(2,1)} %shard_map.55.refs_1_), channel_id=1, replica_groups=mesh['ctx'=8,'ch'=4] {'ctx'}, dimensions={0} | all-to-all | bytes 1179648 | tf_op jit(solution)/shard_map/all_to_all | solution.py:131
  26.2 14.3 %shard_map.56 = bf16[8,128,256]{2,1,0:T(8,128)(2,1)} custom-call(bf16[8,144,256]{2,1,0:T(8,128)(2,1)} %all_to_all.10.refs_0_), custom_call_target="tpu_custom_call" | custom-call | tf_op jit(solution)/shard_map/pallas_call | solution.py:135
  40.5 17.7 %all_to_all.11.refs_2_ = bf16[8,128,256]{2,1,0:T(8,128)(2,1)} all-to-all(bf16[8,128,256]{2,1,0:T(8,128)(2,1)} %shard_map.56), channel_id=1, replica_groups=mesh['ctx'=8,'ch'=4] {'ctx'}, dimensions={0} | all-to-all | bytes 1048576 | tf_op jit(solution)/shard_map/all_to_all | solution.py:140
  58.2 2.4 %shard_map.57 = bf16[128,2048]{1,0:T(8,128)(2,1)} custom-call(bf16[128,2048]{1,0:T(8,128)(2,1)} %refs_0_.3, bf16[8,144,256]{2,1,0:T(8,128)(2,1)} %shard_map.55.refs_1_, bf16[8,128,256]{2,1,0:T(8,128)(2,1)} %all_to_all.11.refs_2_, f32[1,2048]{1,0:T(1,128)} %bitcast.1), custom_call_target="tpu_custom_call" | custom-call | tf_op jit(solution)/shard_map/pallas_call | solution.py:141

commit v2 on v1

v2 whole, which is shorter than its diff:
```python
import jax
import jax.numpy as jnp
from jax import lax
from jax.experimental import pallas as pl
from jax.experimental.pallas import tpu as pltpu
from jax.sharding import PartitionSpec as P

GROUP = 16
BLOCK = 128
LAGS = 8
LANES = 128
TILE = 16
SIDE = LANES // GROUP
CHUNKS = 4
SMALL = pltpu.CompilerParams(vmem_limit_bytes=16 * 1024 * 1024)


def mix_kernel(parts, chunks, key_hbm, value_hbm, taps_hbm, sent_hbm, key_ref, value_ref, taps_ref, sent_ref, arrived, left):
    width = sent_ref.shape[2]
    step = parts // chunks
    taps_copy = pltpu.make_async_copy(taps_hbm, taps_ref, arrived.at[2 * chunks])
    taps_copy.start()
    copies = []
    for chunk in range(chunks):
        columns = slice(chunk * step * width, (chunk + 1) * step * width)
        pair = [
            pltpu.make_async_copy(key_hbm.at[:, columns], key_ref.at[:, columns], arrived.at[2 * chunk]),
            pltpu.make_async_copy(value_hbm.at[:, columns], value_ref.at[:, columns], arrived.at[2 * chunk + 1]),
        ]
        for copy in pair:
            copy.start()
        copies.append(pair)
    tap = lax.broadcasted_iota(jnp.int32, (BLOCK, LANES), 0)
    place = lax.broadcasted_iota(jnp.int32, (BLOCK, LANES), 1)
    mirror = jnp.where((tap + place) % BLOCK == 0, 1.0, 0.0).astype(jnp.bfloat16)
    taps_copy.wait()
    mirrored = lax.dot_general(
        taps_ref[...], mirror, (((0,), (0,)), ((), ())), preferred_element_type=jnp.float32
    ).astype(jnp.bfloat16)
    for part in range(parts):
        own = mirrored[part * TILE : (part + 1) * TILE]
        for start in range(0, width, LANES):
            sent_ref[part, BLOCK : BLOCK + TILE, start : start + LANES] = own
    outs = []
    for chunk in range(chunks):
        for copy in copies[chunk]:
            copy.wait()
        mine = slice(chunk * step, (chunk + 1) * step)
        for part in range(chunk * step, (chunk + 1) * step):
            columns = slice(part * width, (part + 1) * width)
            sent_ref[part, 0:BLOCK, :] = (
                key_ref[:, columns].astype(jnp.float32) * value_ref[:, columns].astype(jnp.float32)
            ).astype(jnp.bfloat16)
        out = pltpu.make_async_copy(sent_ref.at[mine], sent_hbm.at[mine], left.at[chunk])
        out.start()
        outs.append(out)
    for out in outs:
        out.wait()


def conv_kernel(sources, *refs):
    got_refs, (conv_ref, taps, results) = refs[:sources], refs[sources : sources + 3]
    turned_refs = refs[sources + 3 :]
    halves = conv_ref.shape[2] // LANES
    for lag in range(LAGS):
        taps[lag] = got_refs[0][lag, BLOCK : BLOCK + TILE, 0:LANES].astype(jnp.float32)
    lane = lax.broadcasted_iota(jnp.int32, (BLOCK, LANES), 1)
    row = lax.broadcasted_iota(jnp.int32, (BLOCK, LANES), 0)
    causal = row >= lane

    @pl.loop(0, halves)
    def _(half):
        columns = pl.ds(pl.multiple_of(half * LANES, LANES), LANES)
        for got_ref, turned_ref in zip(got_refs, turned_refs):
            for block in range(LAGS):
                tile = got_ref[block, 0:BLOCK, columns]
                turned_ref[block] = pltpu.roll(tile, block * GROUP, 1) if block else tile
        for side in range(SIDE):
            holds = (lane // GROUP + (SIDE - side)) % SIDE
            sources_here = []
            for turned_ref in turned_refs:
                source = turned_ref[0]
                for block in range(1, LAGS):
                    source = jnp.where(holds == block, turned_ref[block], source)
                sources_here.append(source)
            before = jnp.zeros((BLOCK, LANES), jnp.float32)
            filters, shifted = [], []
            for lag in range(LAGS):
                own = taps[lag, pl.ds(half * SIDE + side, 1), :]
                turned = pltpu.roll(jnp.broadcast_to(own, (BLOCK, LANES)), 0, 1, stride=1, stride_axis=0)
                filters.append(jnp.where(causal, turned, before).astype(jnp.bfloat16))
                before = turned
                moved = [pltpu.roll(source, lag * GROUP, 1) if lag else source for source in sources_here]
                if lag:
                    carried = moved[1] if sources > 1 else jnp.zeros_like(moved[0])
                    moved[0] = jnp.where(holds >= lag, moved[0], carried)
                shifted.append(moved[0])
            total = jnp.dot(
                jnp.concatenate(filters, axis=1),
                jnp.concatenate(shifted, axis=0),
                preferred_element_type=jnp.float32,
            )
            results[half * SIDE + side] = total.astype(jnp.bfloat16)

    tall = 4 * TILE
    granule = lax.broadcasted_iota(jnp.int32, (tall, LANES), 1) // GROUP
    for half in range(halves):

        @pl.loop(0, BLOCK // tall)
        def _(step):
            rows = pl.ds(pl.multiple_of(step * tall, tall), tall)
            tiles = [results[half * SIDE + side, rows, :] for side in range(SIDE)]
            for block in range(LAGS):
                total = tiles[0]
                for side in range(1, SIDE):
                    total = jnp.where(granule == (side + block) % SIDE, tiles[side], total)
                turned = pltpu.roll(total, (SIDE - block) * GROUP, 1) if block else total
                conv_ref[block, rows, half * LANES : (half + 1) * LANES] = turned


def gate_kernel(parts, query_ref, key_ref, value_ref, conv_ref, skip_ref, gated_ref):
    width = conv_ref.shape[2]
    for part in range(parts):
        for start in range(0, width, LANES):
            columns = slice(part * width + start, part * width + start + LANES)
            mixed = (
                key_ref[:, columns].astype(jnp.float32) * value_ref[:, columns].astype(jnp.float32)
            ).astype(jnp.bfloat16).astype(jnp.float32)
            conv = conv_ref[part, :, start : start + LANES].astype(jnp.float32)
            summed = conv + skip_ref[:, columns] * mixed
            gated_ref[:, columns] = (query_ref[:, columns].astype(jnp.float32) * summed).astype(jnp.bfloat16)


def per_device(query, key, value, filter_taps, skip):
    rows, channels = query.shape
    parts = LAGS
    width = channels // parts
    count = lax.axis_size("ctx")
    windows = None
    if count > LAGS:
        windows = [list(range(first, first + LAGS)) for first in range(0, count, LAGS)]
        all_taps = lax.all_gather(filter_taps, "ctx", axis=0, tiled=True)
        filter_taps = lax.dynamic_slice_in_dim(all_taps, lax.axis_index("ctx") % LAGS * BLOCK, BLOCK, axis=0)
    sent = pl.pallas_call(
        lambda *refs: mix_kernel(parts, CHUNKS, *refs),
        out_shape=jax.ShapeDtypeStruct((parts, BLOCK + TILE, width), jnp.bfloat16),
        in_specs=[pl.BlockSpec(memory_space=pl.ANY)] * 3,
        out_specs=pl.BlockSpec(memory_space=pl.ANY),
        scratch_shapes=[
            pltpu.VMEM(key.shape, key.dtype),
            pltpu.VMEM(value.shape, value.dtype),
            pltpu.VMEM(filter_taps.shape, filter_taps.dtype),
            pltpu.VMEM((parts, BLOCK + TILE, width), jnp.bfloat16),
            pltpu.SemaphoreType.DMA((2 * CHUNKS + 1,)),
            pltpu.SemaphoreType.DMA((CHUNKS,)),
        ],
    )(key, value, filter_taps)
    got = [lax.all_to_all(sent, "ctx", 0, 0, tiled=True, axis_index_groups=windows)]
    if count > LAGS:
        onward = [(source, source + LAGS) for source in range(count - LAGS)]
        got.append(lax.ppermute(got[0], "ctx", onward))
    conv = pl.pallas_call(
        lambda *refs: conv_kernel(len(got), *refs),
        out_shape=jax.ShapeDtypeStruct((parts, BLOCK, width), jnp.bfloat16),
        scratch_shapes=[
            pltpu.VMEM((LAGS, TILE, LANES), jnp.float32),
            pltpu.VMEM((width // GROUP, BLOCK, LANES), jnp.bfloat16),
        ]
        + [pltpu.VMEM((LAGS, BLOCK, LANES), jnp.bfloat16)] * len(got),
        compiler_params=SMALL,
    )(*got)
    back = lax.all_to_all(conv, "ctx", 0, 0, tiled=True, axis_index_groups=windows)
    return pl.pallas_call(
        lambda *refs: gate_kernel(parts, *refs),
        out_shape=jax.ShapeDtypeStruct((rows, channels), jnp.bfloat16),
        compiler_params=SMALL,
    )(query, key, value, back, skip.reshape(1, channels))


def solution(mesh):
    placed = (P("ctx", "ch"), P("ctx", "ch"), P("ctx", "ch"), P("ctx", "ch"), P("ch"))
    return jax.shard_map(
        per_device, mesh=mesh, in_specs=placed, out_specs=P("ctx", "ch"), check_vma=False
    )
```

time: 61 us -> 48.2 us (0.79)
  Pallas kernels: 19 us -> 6.77 us
    pallas_call x1, Pallas kernels: 14.3 us -> 3.5 us  [per_device(): pl.pallas_call(lambda *refs: conv_kernel(len(got), *refs), out_shape=jax....]
    pallas_call x1, Pallas kernels: 2.39 us -> 1.17 us  [per_device(): pl.pallas_call(lambda *refs: gate_kernel(parts, *refs), out_shape=jax.Sha...]
where the time goes in v2:
time: 48.2 us; the launch traced here: 47.9 us
  blocking collectives  41.1 us (85%)
  Pallas kernels  6.77 us (14%)
    all_to_all x1, blocking collectives, per_device(): lax.all_to_all(sent, 'ctx', 0, 0, tiled=True, axis_index_groups=windows)  23.8 us
    all_to_all x1, blocking collectives, per_device(): lax.all_to_all(conv, 'ctx', 0, 0, tiled=True, axis_index_groups=windows)  17.2 us
    pallas_call x1, Pallas kernels, per_device(): pl.pallas_call(lambda *refs: conv_kernel(len(got), *refs), out_shape=jax....  3.5 us
    pallas_call x1, Pallas kernels, per_device(): pl.pallas_call(lambda *refs: mix_kernel(parts, CHUNKS, *refs), out_shape=...  2.1 us
    pallas_call x1, Pallas kernels, per_device(): pl.pallas_call(lambda *refs: gate_kernel(parts, *refs), out_shape=jax.Sha...  1.17 us

profile of v2, /device:TPU:0, one launch (start us, length us, event | category | flops | bytes accessed | tf_op | source)
XLA Modules:
  0.0 47.9 jit_solution(12806117576217239500)
XLA Ops:
  0.0 2.1 %shard_map.55 = bf16[8,144,256]{2,1,0:T(8,128)(2,1)} custom-call(bf16[128,2048]{1,0:T(8,128)(2,1)} %refs_1_.3, bf16[128,2048]{1,0:T(8,128)(2,1)} %refs_2_.3, bf16[128,128]{1,0:T(8,128)(2,1)} %refs_2_.2), custom_call_target="tpu_custom_call" | custom-call | tf_op jit(solution)/shard_map/pallas_call | solution.py:144
  2.1 23.8 %all_to_all.10.refs_0_ = bf16[8,144,256]{2,1,0:T(8,128)(2,1)S(1)} all-to-all(bf16[8,144,256]{2,1,0:T(8,128)(2,1)} %shard_map.55), channel_id=1, replica_groups=mesh['ctx'=8,'ch'=4] {'ctx'}, dimensions={0} | all-to-all | bytes 1179648 | tf_op jit(solution)/shard_map/all_to_all | solution.py:158
  25.9 0.0 copy-start.2
  25.9 0.0 copy-start.3
  25.9 3.5 %shard_map.56 = bf16[8,128,256]{2,1,0:T(8,128)(2,1)S(1)} custom-call(bf16[8,144,256]{2,1,0:T(8,128)(2,1)S(1)} %all_to_all.10.refs_0_), custom_call_target="tpu_custom_call" | custom-call | tf_op jit(solution)/shard_map/pallas_call | solution.py:162
  29.4 0.0 copy-start
  29.5 0.0 copy-start.1
  29.5 17.2 %all_to_all.11.refs_3_ = bf16[8,128,256]{2,1,0:T(8,128)(2,1)S(1)} all-to-all(bf16[8,128,256]{2,1,0:T(8,128)(2,1)S(1)} %shard_map.56), channel_id=1, replica_groups=mesh['ctx'=8,'ch'=4] {'ctx'}, dimensions={0} | all-to-all | bytes 1048576 | tf_op jit(solution)/shard_map/all_to_all | solution.py:172
  46.7 0.0 copy-done.2
  46.7 0.0 copy-done.3
  46.7 0.0 copy-done
  46.7 0.0 copy-done.1
  46.7 1.2 %shard_map.57 = bf16[128,2048]{1,0:T(8,128)(2,1)} custom-call(bf16[128,2048]{1,0:T(8,128)(2,1)S(1)} %copy-done.2, bf16[128,2048]{1,0:T(8,128)(2,1)S(1)} %copy-done, bf16[128,2048]{1,0:T(8,128)(2,1)S(1)} %copy-done.1, bf16[8,128,256]{2,1,0:T(8,128)(2,1)S(1)} %all_to_all.11.refs_3_, f32[1,2048]{1,0:T(1,128)S(1)} %bitcast.1), custom_call_target="tpu_custom_call" | custom-call | tf_op jit(solution)/shard_map/pallas_call | solution.py:173
Async XLA Ops:
  25.9 20.8 %copy-start.2 = (bf16[128,2048]{1,0:T(8,128)(2,1)S(1)}, bf16[128,2048]{1,0:T(8,128)(2,1)}, u32[]{:S(2)}) copy-start(bf16[128,2048]{1,0:T(8,128)(2,1)} %refs_0_.3) | copy-start | bytes 1572868
  25.9 20.8 %copy-start.3 = (f32[2048]{0:T(1024)S(1)}, f32[2048]{0:T(1024)}, u32[]{:S(2)}) copy-start(f32[2048]{0:T(1024)} %param.9) | copy-start | bytes 24580
  29.4 17.3 %copy-start = (bf16[128,2048]{1,0:T(8,128)(2,1)S(1)}, bf16[128,2048]{1,0:T(8,128)(2,1)}, u32[]{:S(2)}) copy-start(bf16[128,2048]{1,0:T(8,128)(2,1)} %refs_1_.3) | copy-start | bytes 1572868
  29.5 17.3 %copy-start.1 = (bf16[128,2048]{1,0:T(8,128)(2,1)S(1)}, bf16[128,2048]{1,0:T(8,128)(2,1)}, u32[]{:S(2)}) copy-start(bf16[128,2048]{1,0:T(8,128)(2,1)} %refs_2_.3) | copy-start | bytes 1572868

commit v3 on v2

v3 whole, which is shorter than its diff:
```python
import jax
import jax.numpy as jnp
from jax import lax
from jax.experimental import pallas as pl
from jax.experimental.pallas import tpu as pltpu
from jax.sharding import PartitionSpec as P

GROUP = 16
BLOCK = 128
LAGS = 8
LANES = 128
TILE = 16
SIDE = LANES // GROUP
ORDER = (4, 1, 5, 2, 6, 3, 7)
STEPS = (0,) + ORDER
CHUNKS = 2
SMALL = pltpu.CompilerParams(vmem_limit_bytes=16 * 1024 * 1024)


def partner(step):
    return (lax.axis_index("ctx") % LAGS) ^ step


def exchange(blocks):
    pairs = lambda step: [(source, source ^ step) for source in range(lax.axis_size("ctx"))]
    return [blocks[0]] + [lax.ppermute(block, "ctx", pairs(step)) for block, step in zip(blocks[1:], ORDER)]


def turned_back(block):
    return pltpu.roll(block, (SIDE - partner(0)) % SIDE * GROUP, 1)


def mix_kernel(key_hbm, value_hbm, taps_hbm, *refs):
    sent_refs, (key_ref, value_ref, taps_ref, mirrored_ref, arrived) = refs[:LAGS], refs[LAGS:]
    halves = sent_refs[0].shape[0] // BLOCK
    rows = BLOCK // CHUNKS
    taps_copy = pltpu.make_async_copy(taps_hbm, taps_ref, arrived.at[2 * CHUNKS])
    taps_copy.start()
    copies = []
    for chunk in range(CHUNKS):
        here = slice(chunk * rows, (chunk + 1) * rows)
        pair = [
            pltpu.make_async_copy(key_hbm.at[here], key_ref.at[here], arrived.at[2 * chunk]),
            pltpu.make_async_copy(value_hbm.at[here], value_ref.at[here], arrived.at[2 * chunk + 1]),
        ]
        for copy in pair:
            copy.start()
        copies.append(pair)
    tap = lax.broadcasted_iota(jnp.int32, (BLOCK, LANES), 0)
    place = lax.broadcasted_iota(jnp.int32, (BLOCK, LANES), 1)
    mirror = jnp.where((tap + place) % BLOCK == 0, 1.0, 0.0).astype(jnp.bfloat16)
    taps_copy.wait()
    mirrored_ref[...] = lax.dot_general(
        taps_ref[...], mirror, (((0,), (0,)), ((), ())), preferred_element_type=jnp.float32
    ).astype(jnp.bfloat16)
    for step, sent_ref in zip(STEPS, sent_refs):
        first = pl.multiple_of(partner(step) * TILE, TILE)
        sent_ref[halves * BLOCK : halves * BLOCK + TILE, :] = mirrored_ref[pl.ds(first, TILE), :]
    for chunk in range(CHUNKS):
        for copy in copies[chunk]:
            copy.wait()
        here = slice(chunk * rows, (chunk + 1) * rows)
        for step, sent_ref in zip(STEPS, sent_refs):
            for half in range(halves):
                columns = pl.ds(pl.multiple_of((partner(step) * halves + half) * LANES, LANES), LANES)
                mixed = (
                    key_ref[here, columns].astype(jnp.float32) * value_ref[here, columns].astype(jnp.float32)
                ).astype(jnp.bfloat16)
                there = slice(half * BLOCK + chunk * rows, half * BLOCK + (chunk + 1) * rows)
                sent_ref[there, :] = pltpu.roll(mixed, partner(0) * GROUP, 1)


def conv_kernel(sources, *refs):
    inputs = sources * LAGS
    got_refs = [refs[first : first + LAGS] for first in range(0, inputs, LAGS)]
    conv_refs = refs[inputs : inputs + LAGS]
    taps, results = refs[inputs + LAGS :]
    halves = conv_refs[0].shape[0] // BLOCK
    for step, got_ref in zip(STEPS, got_refs[0]):
        taps[partner(step)] = got_ref[halves * BLOCK : halves * BLOCK + TILE, :].astype(jnp.float32)
    lane = lax.broadcasted_iota(jnp.int32, (BLOCK, LANES), 1)
    row = lax.broadcasted_iota(jnp.int32, (BLOCK, LANES), 0)
    causal = row >= lane

    @pl.loop(0, halves)
    def _(half):
        rows = pl.ds(pl.multiple_of(half * BLOCK, BLOCK), BLOCK)
        for side in range(SIDE):
            holds = (lane // GROUP + (SIDE - side)) % SIDE
            sources_here = []
            for window in got_refs:
                source = window[0][rows, :]
                for step, got_ref in zip(ORDER, window[1:]):
                    source = jnp.where(holds == partner(step), got_ref[rows, :], source)
                sources_here.append(source)
            before = jnp.zeros((BLOCK, LANES), jnp.float32)
            filters, shifted = [], []
            for lag in range(LAGS):
                own = taps[lag, pl.ds(half * SIDE + side, 1), :]
                turned = pltpu.roll(jnp.broadcast_to(own, (BLOCK, LANES)), 0, 1, stride=1, stride_axis=0)
                filters.append(jnp.where(causal, turned, before).astype(jnp.bfloat16))
                before = turned
                moved = [pltpu.roll(source, lag * GROUP, 1) if lag else source for source in sources_here]
                if lag:
                    carried = moved[1] if sources > 1 else jnp.zeros_like(moved[0])
                    moved[0] = jnp.where(holds >= lag, moved[0], carried)
                shifted.append(moved[0])
            total = jnp.dot(
                jnp.concatenate(filters, axis=1),
                jnp.concatenate(shifted, axis=0),
                preferred_element_type=jnp.float32,
            )
            results[half * SIDE + side] = total.astype(jnp.bfloat16)

    tall = 4 * TILE
    granule = lax.broadcasted_iota(jnp.int32, (tall, LANES), 1) // GROUP
    for half in range(halves):

        @pl.loop(0, BLOCK // tall)
        def _(part):
            tiles = [results[half * SIDE + side, pl.ds(part * tall, tall), :] for side in range(SIDE)]
            for step, conv_ref in zip(STEPS, conv_refs):
                total = tiles[0]
                for side in range(1, SIDE):
                    total = jnp.where(granule == (side + partner(step)) % SIDE, tiles[side], total)
                conv_ref[pl.ds(half * BLOCK + part * tall, tall), :] = total


def gate_kernel(query_ref, skip_ref, *refs):
    sent_refs, conv_refs, (gated_hbm, gated_ref, left) = refs[:LAGS], refs[LAGS : 2 * LAGS], refs[2 * LAGS :]
    halves = conv_refs[0].shape[0] // BLOCK
    width = halves * LANES
    copies = []
    for index, step in enumerate(STEPS):
        for half in range(halves):
            columns = pl.ds(pl.multiple_of((partner(step) * halves + half) * LANES, LANES), LANES)
            rows = slice(half * BLOCK, (half + 1) * BLOCK)
            mixed = turned_back(sent_refs[index][rows, :]).astype(jnp.float32)
            conv = turned_back(conv_refs[index][rows, :]).astype(jnp.float32)
            summed = conv + skip_ref[:, columns] * mixed
            gated_ref[:, columns] = (query_ref[:, columns].astype(jnp.float32) * summed).astype(jnp.bfloat16)
        columns = pl.ds(pl.multiple_of(partner(step) * width, width), width)
        copy = pltpu.make_async_copy(gated_ref.at[:, columns], gated_hbm.at[:, columns], left.at[index])
        copy.start()
        copies.append(copy)
    for copy in copies:
        copy.wait()


def per_device(query, key, value, filter_taps, skip):
    rows, channels = query.shape
    halves = channels // LAGS // LANES
    count = lax.axis_size("ctx")
    if count > LAGS:
        all_taps = lax.all_gather(filter_taps, "ctx", axis=0, tiled=True)
        first_tap = lax.axis_index("ctx") % LAGS * BLOCK
        filter_taps = lax.dynamic_slice_in_dim(all_taps, first_tap, BLOCK, axis=0)
    in_hbm = [pltpu.with_memory_space_constraint(array, pltpu.HBM) for array in (key, value, filter_taps)]
    sent = pl.pallas_call(
        mix_kernel,
        out_shape=[jax.ShapeDtypeStruct((halves * BLOCK + TILE, LANES), jnp.bfloat16)] * LAGS,
        in_specs=[pl.BlockSpec(memory_space=pl.ANY)] * 3,
        scratch_shapes=[
            pltpu.VMEM(key.shape, key.dtype),
            pltpu.VMEM(value.shape, value.dtype),
            pltpu.VMEM(filter_taps.shape, filter_taps.dtype),
            pltpu.VMEM((LANES, BLOCK), jnp.bfloat16),
            pltpu.SemaphoreType.DMA((2 * CHUNKS + 1,)),
        ],
        compiler_params=SMALL,
    )(*in_hbm)
    got = exchange(sent)
    sources = 1
    if count > LAGS:
        sources = 2
        onward = [(source, source + LAGS) for source in range(count - LAGS)]
        got = got + [lax.ppermute(block, "ctx", onward) for block in got]
    conv = pl.pallas_call(
        lambda *refs: conv_kernel(sources, *refs),
        out_shape=[jax.ShapeDtypeStruct((halves * BLOCK, LANES), jnp.bfloat16)] * LAGS,
        scratch_shapes=[
            pltpu.VMEM((LAGS, TILE, LANES), jnp.float32),
            pltpu.VMEM((halves * SIDE, BLOCK, LANES), jnp.bfloat16),
        ],
        compiler_params=SMALL,
    )(*got)
    back = exchange(conv)
    whole = pl.BlockSpec(memory_space=pltpu.VMEM)
    return pl.pallas_call(
        gate_kernel,
        out_shape=jax.ShapeDtypeStruct((rows, channels), jnp.bfloat16),
        in_specs=[whole] * (2 + 2 * LAGS),
        out_specs=pl.BlockSpec(memory_space=pl.ANY),
        scratch_shapes=[pltpu.VMEM((rows, channels), jnp.bfloat16), pltpu.SemaphoreType.DMA((LAGS,))],
        compiler_params=SMALL,
    )(query, skip.reshape(1, channels), *sent, *back)


def solution(mesh):
    placed = (P("ctx", "ch"), P("ctx", "ch"), P("ctx", "ch"), P("ctx", "ch"), P("ch"))
    return jax.shard_map(
        per_device, mesh=mesh, in_specs=placed, out_specs=P("ctx", "ch"), check_vma=False
    )
```

time: 48.2 us -> 40.1 us (0.83)
  blocking collectives: 41.1 us -> 0 us
  starting transfers between devices: 0 us -> 24.6 us
  waiting for transfers between devices: 0 us -> 9.45 us
  Pallas kernels: 6.77 us -> 5.8 us
    all_to_all x2 -> x0, blocking collectives: 41.1 us -> none  [the longest x1 23.8 us: per_device(): lax.all_to_all(sent, 'ctx', 0, 0, tiled=True, axis_index_groups=windows)]
    ppermute x0 -> x14, starting transfers between devices: none -> 24.6 us  [exchange(): lax.ppermute(block, 'ctx', pairs(step))]
    ppermute x0 -> x14, waiting for transfers between devices: none -> 9.45 us  [exchange(): lax.ppermute(block, 'ctx', pairs(step))]
    pallas_call x3, Pallas kernels: 6.77 us -> 5.8 us  [the longest x1 3.21 us: per_device(): pl.pallas_call(lambda *refs: conv_kernel(sources, *refs), out_shape=[jax....]
  transfers between devices with their start and end apart: 0 -> 14, of which waited for: 0 -> 7; matrix products, arithmetic and copies ran while one was open for 0% -> 0% of each run, Pallas kernels for 0% -> 0%
where the time goes in v3:
time: 40.1 us; the launch traced here: 39.9 us
  starting transfers between devices  24.6 us (61%)
  waiting for transfers between devices  9.45 us (24%)
  Pallas kernels  5.8 us (14%)
    ppermute x14, starting transfers between devices, exchange(): lax.ppermute(block, 'ctx', pairs(step))  24.6 us
    ppermute x14, waiting for transfers between devices, exchange(): lax.ppermute(block, 'ctx', pairs(step))  9.45 us
    pallas_call x1, Pallas kernels, per_device(): pl.pallas_call(lambda *refs: conv_kernel(sources, *refs), out_shape=[jax....  3.21 us
    pallas_call x1, Pallas kernels, per_device(): pl.pallas_call(mix_kernel, out_shape=[jax.ShapeDtypeStruct((halves * BLOC...  1.51 us
    pallas_call x1, Pallas kernels, per_device(): pl.pallas_call(gate_kernel, out_shape=jax.ShapeDtypeStruct((rows, channel...  1.08 us
  transfers between devices with their start and end apart: 14, of which 7 were waited for; matrix products, arithmetic and copies ran while one was open for 0% of the time, Pallas kernels for 0%

profile of v3, /device:TPU:0, one launch (start us, length us, event | category | flops | bytes accessed | tf_op | source)
XLA Modules:
  0.0 39.9 jit_solution(8404957481701881252)
XLA Ops:
  0.0 1.5 %shard_map.55 = (bf16[272,128]{1,0:T(8,128)(2,1)S(1)}, bf16[272,128]{1,0:T(8,128)(2,1)S(1)}, bf16[272,128]{1,0:T(8,128)(2,1)S(1)}, bf16[272,128]{1,0:T(8,128)(2,...) custom-call(bf16[128,2048]{1,0:T(8,128)(2,1)} %key_hbm.1, ...), custom_call_target="tpu_custom_call" | custom-call | tf_op jit(solution)/shard_map/pallas_call | solution.py:159
  1.5 0.0 copy-start
  1.5 4.1 %collective-permute-start = (bf16[272,128]{1,0:T(8,128)(2,1)S(1)}, bf16[272,128]{1,0:T(8,128)(2,1)S(1)}, u32[]{:S(2)}, u32[]{:S(2)}) collective-permute-start(bf16[272,128]{1,0:T(8,128)(2,1)S(1)} %get-tuple-element.22.refs_1_), channel_id=1, source_target_pairs={{0,16},{4,20},{8,24},{12,28},{16,0},{20,4},{24,8},{28,12},{1,17},{... | collective-permute-start | bytes 208904 | tf_op jit(solution)/shard_map/ppermute | solution.py:26
  5.6 1.5 %collective-permute-start.1 = (bf16[272,128]{1,0:T(8,128)(2,1)S(1)}, bf16[272,128]{1,0:T(8,128)(2,1)S(1)}, u32[]{:S(2)}, u32[]{:S(2)}) collective-permute-start(bf16[272,128]{1,0:T(8,128)(2,1)S(1)} %get-tuple-element.23.refs_2_), channel_id=1, source_target_pairs={{0,4},{4,0},{8,12},{12,8},{16,20},{20,16},{24,28},{28,24},{1,5},{5... | collective-permute-start | bytes 208904 | tf_op jit(solution)/shard_map/ppermute | solution.py:26
  7.1 0.0 collective-permute-start.2
  7.2 1.8 %collective-permute-start.3 = (bf16[272,128]{1,0:T(8,128)(2,1)S(1)}, bf16[272,128]{1,0:T(8,128)(2,1)S(1)}, u32[]{:S(2)}, u32[]{:S(2)}) collective-permute-start(bf16[272,128]{1,0:T(8,128)(2,1)S(1)} %get-tuple-element.25.refs_4_), channel_id=1, source_target_pairs={{0,8},{4,12},{8,0},{12,4},{16,24},{20,28},{24,16},{28,20},{1,9},{5... | collective-permute-start | bytes 208904 | tf_op jit(solution)/shard_map/ppermute | solution.py:26
  9.0 2.5 %collective-permute-start.4 = (bf16[272,128]{1,0:T(8,128)(2,1)S(1)}, bf16[272,128]{1,0:T(8,128)(2,1)S(1)}, u32[]{:S(2)}, u32[]{:S(2)}) collective-permute-start(bf16[272,128]{1,0:T(8,128)(2,1)S(1)} %get-tuple-element.26.refs_5_), channel_id=1, source_target_pairs={{0,24},{4,28},{8,16},{12,20},{16,8},{20,12},{24,0},{28,4},{1,25},{... | collective-permute-start | bytes 208904 | tf_op jit(solution)/shard_map/ppermute | solution.py:26
  11.5 0.0 collective-permute-done.refs_1_
  11.5 1.6 %collective-permute-start.5 = (bf16[272,128]{1,0:T(8,128)(2,1)S(1)}, bf16[272,128]{1,0:T(8,128)(2,1)S(1)}, u32[]{:S(2)}, u32[]{:S(2)}) collective-permute-start(bf16[272,128]{1,0:T(8,128)(2,1)S(1)} %get-tuple-element.27.refs_6_), channel_id=1, source_target_pairs={{0,12},{4,8},{8,4},{12,0},{16,28},{20,24},{24,20},{28,16},{1,13},{... | collective-permute-start | bytes 208904 | tf_op jit(solution)/shard_map/ppermute | solution.py:26
  13.1 0.0 collective-permute-done.1.refs_2_
  13.1 2.7 %collective-permute-start.6 = (bf16[272,128]{1,0:T(8,128)(2,1)S(1)}, bf16[272,128]{1,0:T(8,128)(2,1)S(1)}, u32[]{:S(2)}, u32[]{:S(2)}) collective-permute-start(bf16[272,128]{1,0:T(8,128)(2,1)S(1)} %get-tuple-element.28.refs_7_), channel_id=1, source_target_pairs={{0,28},{4,24},{8,20},{12,16},{16,12},{20,8},{24,4},{28,0},{1,29},{... | collective-permute-start | bytes 208904 | tf_op jit(solution)/shard_map/ppermute | solution.py:26
  15.8 0.0 collective-permute-done.2.refs_3_
  15.8 0.0 collective-permute-done.3.refs_4_
  15.8 0.1 collective-permute-done.4.refs_5_
  16.0 1.9 %collective-permute-done.5.refs_6_ = bf16[272,128]{1,0:T(8,128)(2,1)S(1)} collective-permute-done((bf16[272,128]{1,0:T(8,128)(2,1)S(1)}, bf16[272,128]{1,0:T(8,128)(2,1)S(1)}, u32[]{:S(2)}, u32[]{:S(2)}) %collective-permute-start.5) | collective-permute-done | bytes 69664 | tf_op jit(solution)/shard_map/ppermute | solution.py:26
  17.9 2.2 %collective-permute-done.6.refs_7_ = bf16[272,128]{1,0:T(8,128)(2,1)S(1)} collective-permute-done((bf16[272,128]{1,0:T(8,128)(2,1)S(1)}, bf16[272,128]{1,0:T(8,128)(2,1)S(1)}, u32[]{:S(2)}, u32[]{:S(2)}) %collective-permute-start.6) | collective-permute-done | bytes 69664 | tf_op jit(solution)/shard_map/ppermute | solution.py:26
  20.1 3.2 %shard_map.56 = (bf16[256,128]{1,0:T(8,128)(2,1)S(1)}, bf16[256,128]{1,0:T(8,128)(2,1)S(1)}, bf16[256,128]{1,0:T(8,128)(2,1)S(1)}, bf16[256,128]{1,0:T(8,128)(2,...) custom-call(bf16[272,128]{1,0:T(8,128)(2,1)S(1)} %get-tuple-element., ...), custom_call_target="tpu_custom_call" | custom-call | tf_op jit(solution)/shard_map/pallas_call | solution.py:178
  23.3 0.0 copy-start.1
  23.3 1.8 %collective-permute-start.7 = (bf16[256,128]{1,0:T(8,128)(2,1)S(1)}, bf16[256,128]{1,0:T(8,128)(2,1)S(1)}, u32[]{:S(2)}, u32[]{:S(2)}) collective-permute-start(bf16[256,128]{1,0:T(8,128)(2,1)S(1)} %get-tuple-element.30), channel_id=1, source_target_pairs={{0,16},{4,20},{8,24},{12,28},{16,0},{20,4},{24,8},{28,12},{1,17},{... | collective-permute-start | bytes 196616 | tf_op jit(solution)/shard_map/ppermute | solution.py:26
  25.1 1.1 %collective-permute-start.8 = (bf16[256,128]{1,0:T(8,128)(2,1)S(1)}, bf16[256,128]{1,0:T(8,128)(2,1)S(1)}, u32[]{:S(2)}, u32[]{:S(2)}) collective-permute-start(bf16[256,128]{1,0:T(8,128)(2,1)S(1)} %get-tuple-element.31), channel_id=1, source_target_pairs={{0,4},{4,0},{8,12},{12,8},{16,20},{20,16},{24,28},{28,24},{1,5},{5... | collective-permute-start | bytes 196616 | tf_op jit(solution)/shard_map/ppermute | solution.py:26
  26.2 1.6 %collective-permute-start.9 = (bf16[256,128]{1,0:T(8,128)(2,1)S(1)}, bf16[256,128]{1,0:T(8,128)(2,1)S(1)}, u32[]{:S(2)}, u32[]{:S(2)}) collective-permute-start(bf16[256,128]{1,0:T(8,128)(2,1)S(1)} %get-tuple-element.32), channel_id=1, source_target_pairs={{0,20},{4,16},{8,28},{12,24},{16,4},{20,0},{24,12},{28,8},{1,21},{... | collective-permute-start | bytes 196616 | tf_op jit(solution)/shard_map/ppermute | solution.py:26
  27.8 0.0 collective-permute-start.10
  27.8 3.2 %collective-permute-start.11 = (bf16[256,128]{1,0:T(8,128)(2,1)S(1)}, bf16[256,128]{1,0:T(8,128)(2,1)S(1)}, u32[]{:S(2)}, u32[]{:S(2)}) collective-permute-start(bf16[256,128]{1,0:T(8,128)(2,1)S(1)} %get-tuple-element.34), channel_id=1, source_target_pairs={{0,24},{4,28},{8,16},{12,20},{16,8},{20,12},{24,0},{28,4},{1,25},{... | collective-permute-start | bytes 196616 | tf_op jit(solution)/shard_map/ppermute | solution.py:26
  31.0 0.0 collective-permute-done.7.refs_9_
  31.0 0.8 %collective-permute-start.12 = (bf16[256,128]{1,0:T(8,128)(2,1)S(1)}, bf16[256,128]{1,0:T(8,128)(2,1)S(1)}, u32[]{:S(2)}, u32[]{:S(2)}) collective-permute-start(bf16[256,128]{1,0:T(8,128)(2,1)S(1)} %get-tuple-element.35), channel_id=1, source_target_pairs={{0,12},{4,8},{8,4},{12,0},{16,28},{20,24},{24,20},{28,16},{1,13},{... | collective-permute-start | bytes 196616 | tf_op jit(solution)/shard_map/ppermute | solution.py:26
  31.8 0.0 collective-permute-done.8.refs_10_
  31.8 1.9 %collective-permute-start.13 = (bf16[256,128]{1,0:T(8,128)(2,1)S(1)}, bf16[256,128]{1,0:T(8,128)(2,1)S(1)}, u32[]{:S(2)}, u32[]{:S(2)}) collective-permute-start(bf16[256,128]{1,0:T(8,128)(2,1)S(1)} %get-tuple-element.36), channel_id=1, source_target_pairs={{0,28},{4,24},{8,20},{12,16},{16,12},{20,8},{24,4},{28,0},{1,29},{... | collective-permute-start | bytes 196616 | tf_op jit(solution)/shard_map/ppermute | solution.py:26
  33.6 0.5 %collective-permute-done.9.refs_11_ = bf16[256,128]{1,0:T(8,128)(2,1)S(1)} collective-permute-done((bf16[256,128]{1,0:T(8,128)(2,1)S(1)}, bf16[256,128]{1,0:T(8,128)(2,1)S(1)}, u32[]{:S(2)}, u32[]{:S(2)}) %collective-permute-start.9) | collective-permute-done | bytes 65568 | tf_op jit(solution)/shard_map/ppermute | solution.py:26
  34.2 0.0 collective-permute-done.10.refs_12_
  34.2 0.5 %collective-permute-done.11.refs_13_ = bf16[256,128]{1,0:T(8,128)(2,1)S(1)} collective-permute-done((bf16[256,128]{1,0:T(8,128)(2,1)S(1)}, bf16[256,128]{1,0:T(8,128)(2,1)S(1)}, u32[]{:S(2)}, u32[]{:S(2)}) %collective-permute-start.11) | collective-permute-done | bytes 65568 | tf_op jit(solution)/shard_map/ppermute | solution.py:26
  34.7 1.5 %collective-permute-done.12.refs_14_ = bf16[256,128]{1,0:T(8,128)(2,1)S(1)} collective-permute-done((bf16[256,128]{1,0:T(8,128)(2,1)S(1)}, bf16[256,128]{1,0:T(8,128)(2,1)S(1)}, u32[]{:S(2)}, u32[]{:S(2)}) %collective-permute-start.12) | collective-permute-done | bytes 65568 | tf_op jit(solution)/shard_map/ppermute | solution.py:26
  36.1 2.7 %collective-permute-done.13.refs_15_ = bf16[256,128]{1,0:T(8,128)(2,1)S(1)} collective-permute-done((bf16[256,128]{1,0:T(8,128)(2,1)S(1)}, bf16[256,128]{1,0:T(8,128)(2,1)S(1)}, u32[]{:S(2)}, u32[]{:S(2)}) %collective-permute-start.13) | collective-permute-done | bytes 65568 | tf_op jit(solution)/shard_map/ppermute | solution.py:26
  38.8 0.0 copy-done
  38.8 0.0 copy-done.1
  38.8 1.1 %shard_map.57 = bf16[128,2048]{1,0:T(8,128)(2,1)} custom-call(bf16[128,2048]{1,0:T(8,128)(2,1)S(1)} %copy-done, f32[1,2048]{1,0:T(1,128)S(1)} %bitcast.1, bf16[272,128]{1,0:T(8,128)(2,1)S(1)} %get-tuple-element.21.refs_0_, bf16[272,128]{1,0:T(8,128)(2,1)S(1)} %get-tuple-element.22.refs_1_, bf16[272,128]{1,0:T(8,128)(2,1)S(1)} %get-tuple-element.23.refs_2_, ...), custom_call_target="tpu_custom_call" | custom-call | tf_op jit(solution)/shard_map/pallas_call | solution.py:189
Async XLA Ops:
  1.5 37.3 %copy-start = (bf16[128,2048]{1,0:T(8,128)(2,1)S(1)}, bf16[128,2048]{1,0:T(8,128)(2,1)}, u32[]{:S(2)}) copy-start(bf16[128,2048]{1,0:T(8,128)(2,1)} %query_ref.1) | copy-start | bytes 1572868
  1.5 10.0 %collective-permute-start = (bf16[272,128]{1,0:T(8,128)(2,1)S(1)}, bf16[272,128]{1,0:T(8,128)(2,1)S(1)}, u32[]{:S(2)}, u32[]{:S(2)}) collective-permute-start(bf16[272,128]{1,0:T(8,128)(2,1)S(1)} %get-tuple-element.22.refs_1_), channel_id=1, source_target_pairs={{0,16},{4,20},{8,24},{12,28},{16,0},{20,4},{24,8},{28,12},{1,17},{... | collective-permute-start | bytes 208904 | tf_op jit(solution)/shard_map/ppermute | solution.py:26
  5.6 7.5 %collective-permute-start.1 = (bf16[272,128]{1,0:T(8,128)(2,1)S(1)}, bf16[272,128]{1,0:T(8,128)(2,1)S(1)}, u32[]{:S(2)}, u32[]{:S(2)}) collective-permute-start(bf16[272,128]{1,0:T(8,128)(2,1)S(1)} %get-tuple-element.23.refs_2_), channel_id=1, source_target_pairs={{0,4},{4,0},{8,12},{12,8},{16,20},{20,16},{24,28},{28,24},{1,5},{5... | collective-permute-start | bytes 208904 | tf_op jit(solution)/shard_map/ppermute | solution.py:26
  7.1 8.7 %collective-permute-start.2 = (bf16[272,128]{1,0:T(8,128)(2,1)S(1)}, bf16[272,128]{1,0:T(8,128)(2,1)S(1)}, u32[]{:S(2)}, u32[]{:S(2)}) collective-permute-start(bf16[272,128]{1,0:T(8,128)(2,1)S(1)} %get-tuple-element.24.refs_3_), channel_id=1, source_target_pairs={{0,20},{4,16},{8,28},{12,24},{16,4},{20,0},{24,12},{28,8},{1,21},{... | collective-permute-start | bytes 208904 | tf_op jit(solution)/shard_map/ppermute | solution.py:26
  7.2 8.7 %collective-permute-start.3 = (bf16[272,128]{1,0:T(8,128)(2,1)S(1)}, bf16[272,128]{1,0:T(8,128)(2,1)S(1)}, u32[]{:S(2)}, u32[]{:S(2)}) collective-permute-start(bf16[272,128]{1,0:T(8,128)(2,1)S(1)} %get-tuple-element.25.refs_4_), channel_id=1, source_target_pairs={{0,8},{4,12},{8,0},{12,4},{16,24},{20,28},{24,16},{28,20},{1,9},{5... | collective-permute-start | bytes 208904 | tf_op jit(solution)/shard_map/ppermute | solution.py:26
  9.0 7.0 %collective-permute-start.4 = (bf16[272,128]{1,0:T(8,128)(2,1)S(1)}, bf16[272,128]{1,0:T(8,128)(2,1)S(1)}, u32[]{:S(2)}, u32[]{:S(2)}) collective-permute-start(bf16[272,128]{1,0:T(8,128)(2,1)S(1)} %get-tuple-element.26.refs_5_), channel_id=1, source_target_pairs={{0,24},{4,28},{8,16},{12,20},{16,8},{20,12},{24,0},{28,4},{1,25},{... | collective-permute-start | bytes 208904 | tf_op jit(solution)/shard_map/ppermute | solution.py:26
  11.5 6.4 %collective-permute-start.5 = (bf16[272,128]{1,0:T(8,128)(2,1)S(1)}, bf16[272,128]{1,0:T(8,128)(2,1)S(1)}, u32[]{:S(2)}, u32[]{:S(2)}) collective-permute-start(bf16[272,128]{1,0:T(8,128)(2,1)S(1)} %get-tuple-element.27.refs_6_), channel_id=1, source_target_pairs={{0,12},{4,8},{8,4},{12,0},{16,28},{20,24},{24,20},{28,16},{1,13},{... | collective-permute-start | bytes 208904 | tf_op jit(solution)/shard_map/ppermute | solution.py:26
  13.1 7.0 %collective-permute-start.6 = (bf16[272,128]{1,0:T(8,128)(2,1)S(1)}, bf16[272,128]{1,0:T(8,128)(2,1)S(1)}, u32[]{:S(2)}, u32[]{:S(2)}) collective-permute-start(bf16[272,128]{1,0:T(8,128)(2,1)S(1)} %get-tuple-element.28.refs_7_), channel_id=1, source_target_pairs={{0,28},{4,24},{8,20},{12,16},{16,12},{20,8},{24,4},{28,0},{1,29},{... | collective-permute-start | bytes 208904 | tf_op jit(solution)/shard_map/ppermute | solution.py:26
  23.3 15.5 %copy-start.1 = (f32[2048]{0:T(1024)S(1)}, f32[2048]{0:T(1024)}, u32[]{:S(2)}) copy-start(f32[2048]{0:T(1024)} %param.9) | copy-start | bytes 24580
  23.3 7.6 %collective-permute-start.7 = (bf16[256,128]{1,0:T(8,128)(2,1)S(1)}, bf16[256,128]{1,0:T(8,128)(2,1)S(1)}, u32[]{:S(2)}, u32[]{:S(2)}) collective-permute-start(bf16[256,128]{1,0:T(8,128)(2,1)S(1)} %get-tuple-element.30), channel_id=1, source_target_pairs={{0,16},{4,20},{8,24},{12,28},{16,0},{20,4},{24,8},{28,12},{1,17},{... | collective-permute-start | bytes 196616 | tf_op jit(solution)/shard_map/ppermute | solution.py:26
  25.1 6.6 %collective-permute-start.8 = (bf16[256,128]{1,0:T(8,128)(2,1)S(1)}, bf16[256,128]{1,0:T(8,128)(2,1)S(1)}, u32[]{:S(2)}, u32[]{:S(2)}) collective-permute-start(bf16[256,128]{1,0:T(8,128)(2,1)S(1)} %get-tuple-element.31), channel_id=1, source_target_pairs={{0,4},{4,0},{8,12},{12,8},{16,20},{20,16},{24,28},{28,24},{1,5},{5... | collective-permute-start | bytes 196616 | tf_op jit(solution)/shard_map/ppermute | solution.py:26
  26.2 8.0 %collective-permute-start.9 = (bf16[256,128]{1,0:T(8,128)(2,1)S(1)}, bf16[256,128]{1,0:T(8,128)(2,1)S(1)}, u32[]{:S(2)}, u32[]{:S(2)}) collective-permute-start(bf16[256,128]{1,0:T(8,128)(2,1)S(1)} %get-tuple-element.32), channel_id=1, source_target_pairs={{0,20},{4,16},{8,28},{12,24},{16,4},{20,0},{24,12},{28,8},{1,21},{... | collective-permute-start | bytes 196616 | tf_op jit(solution)/shard_map/ppermute | solution.py:26
  27.8 6.4 %collective-permute-start.10 = (bf16[256,128]{1,0:T(8,128)(2,1)S(1)}, bf16[256,128]{1,0:T(8,128)(2,1)S(1)}, u32[]{:S(2)}, u32[]{:S(2)}) collective-permute-start(bf16[256,128]{1,0:T(8,128)(2,1)S(1)} %get-tuple-element.33), channel_id=1, source_target_pairs={{0,8},{4,12},{8,0},{12,4},{16,24},{20,28},{24,16},{28,20},{1,9},{5... | collective-permute-start | bytes 196616 | tf_op jit(solution)/shard_map/ppermute | solution.py:26
  27.8 6.9 %collective-permute-start.11 = (bf16[256,128]{1,0:T(8,128)(2,1)S(1)}, bf16[256,128]{1,0:T(8,128)(2,1)S(1)}, u32[]{:S(2)}, u32[]{:S(2)}) collective-permute-start(bf16[256,128]{1,0:T(8,128)(2,1)S(1)} %get-tuple-element.34), channel_id=1, source_target_pairs={{0,24},{4,28},{8,16},{12,20},{16,8},{20,12},{24,0},{28,4},{1,25},{... | collective-permute-start | bytes 196616 | tf_op jit(solution)/shard_map/ppermute | solution.py:26
  31.0 5.2 %collective-permute-start.12 = (bf16[256,128]{1,0:T(8,128)(2,1)S(1)}, bf16[256,128]{1,0:T(8,128)(2,1)S(1)}, u32[]{:S(2)}, u32[]{:S(2)}) collective-permute-start(bf16[256,128]{1,0:T(8,128)(2,1)S(1)} %get-tuple-element.35), channel_id=1, source_target_pairs={{0,12},{4,8},{8,4},{12,0},{16,28},{20,24},{24,20},{28,16},{1,13},{... | collective-permute-start | bytes 196616 | tf_op jit(solution)/shard_map/ppermute | solution.py:26
  31.8 7.1 %collective-permute-start.13 = (bf16[256,128]{1,0:T(8,128)(2,1)S(1)}, bf16[256,128]{1,0:T(8,128)(2,1)S(1)}, u32[]{:S(2)}, u32[]{:S(2)}) collective-permute-start(bf16[256,128]{1,0:T(8,128)(2,1)S(1)} %get-tuple-element.36), channel_id=1, source_target_pairs={{0,28},{4,24},{8,20},{12,16},{16,12},{20,8},{24,4},{28,0},{1,29},{... | collective-permute-start | bytes 196616 | tf_op jit(solution)/shard_map/ppermute | solution.py:26

commit v4 on v3

v4 whole, which is shorter than its diff:
```python
import jax
import jax.numpy as jnp
from jax import lax
from jax.experimental import pallas as pl
from jax.experimental.pallas import tpu as pltpu
from jax.sharding import PartitionSpec as P

GROUP = 16
BLOCK = 128
LAGS = 8
LANES = 128
TILE = 16
SIDE = LANES // GROUP
GATHER = ((6, 1, 4, 2, 5, 3, 7), (6, 1, 4, 2, 5, 3, 7))
RETURN = ((4, 1, 5, 2, 6, 3, 7), (4, 1, 5, 2, 6, 3, 7))
CHUNKS = 2
EARLY = 7
SMALL = pltpu.CompilerParams(vmem_limit_bytes=16 * 1024 * 1024)


def place():
    return lax.axis_index("ctx") % LAGS


def partners(orders):
    core = lax.axis_index("ch") % 2
    return [place()] + [place() ^ jnp.where(core == 0, first, second) for first, second in zip(*orders)]


def exchange(blocks, orders):
    size = lax.axis_size("ch")
    devices = range(lax.axis_size("ctx") * size)
    got = [blocks[0]]
    for block, steps in zip(blocks[1:], zip(*orders)):
        pairs = [(one, (one // size ^ steps[one % size % 2]) * size + one % size) for one in devices]
        got.append(lax.ppermute(block, ("ctx", "ch"), pairs))
    return got


def turned_back(block):
    return pltpu.roll(block, (SIDE - place()) % SIDE * GROUP, 1)


def mix_kernel(key_hbm, value_hbm, taps_hbm, *refs):
    sent_refs, (mixed_ref, key_ref, value_ref, taps_ref, mirrored_ref, arrived) = refs[:LAGS], refs[LAGS:]
    halves = sent_refs[0].shape[0] // BLOCK
    rows = BLOCK // CHUNKS
    taps_copy = pltpu.make_async_copy(taps_hbm, taps_ref, arrived.at[2 * CHUNKS])
    taps_copy.start()
    copies = []
    for chunk in range(CHUNKS):
        here = slice(chunk * rows, (chunk + 1) * rows)
        pair = [
            pltpu.make_async_copy(key_hbm.at[here], key_ref.at[here], arrived.at[2 * chunk]),
            pltpu.make_async_copy(value_hbm.at[here], value_ref.at[here], arrived.at[2 * chunk + 1]),
        ]
        for copy in pair:
            copy.start()
        copies.append(pair)
    tap = lax.broadcasted_iota(jnp.int32, (BLOCK, LANES), 0)
    column = lax.broadcasted_iota(jnp.int32, (BLOCK, LANES), 1)
    mirror = jnp.where((tap + column) % BLOCK == 0, 1.0, 0.0).astype(jnp.bfloat16)
    taps_copy.wait()
    mirrored_ref[...] = lax.dot_general(
        taps_ref[...], mirror, (((0,), (0,)), ((), ())), preferred_element_type=jnp.float32
    ).astype(jnp.bfloat16)
    for partner, sent_ref in zip(partners(GATHER), sent_refs):
        first = pl.multiple_of(partner * TILE, TILE)
        sent_ref[halves * BLOCK : halves * BLOCK + TILE, :] = mirrored_ref[pl.ds(first, TILE), :]
    for chunk in range(CHUNKS):
        for copy in copies[chunk]:
            copy.wait()
        here = slice(chunk * rows, (chunk + 1) * rows)
        for partner, sent_ref in zip(partners(GATHER), sent_refs):
            for half in range(halves):
                columns = pl.ds(pl.multiple_of((partner * halves + half) * LANES, LANES), LANES)
                mixed = (
                    key_ref[here, columns].astype(jnp.float32) * value_ref[here, columns].astype(jnp.float32)
                ).astype(jnp.bfloat16)
                mixed_ref[here, columns] = mixed
                there = slice(half * BLOCK + chunk * rows, half * BLOCK + (chunk + 1) * rows)
                sent_ref[there, :] = pltpu.roll(mixed, place() * GROUP, 1)


def add_circulants(where, got_refs, circulants, taps):
    rows = got_refs[0].shape[0]
    for index, got_ref in enumerate(got_refs):
        taps[index] = got_ref[rows - TILE : rows, :].astype(jnp.float32)

    @pl.loop(0, TILE, unroll=8)
    def _(group):
        for index, partner in enumerate(where):
            own = jnp.broadcast_to(taps[index, pl.ds(group, 1), :], (BLOCK, LANES))
            circulants[partner, group] = pltpu.roll(own, 0, 1, stride=1, stride_axis=0).astype(jnp.bfloat16)


def early_kernel(*refs):
    *got_refs, circulants, taps = refs
    add_circulants(partners(GATHER)[:EARLY], got_refs, circulants, taps)


def conv_kernel(sources, *refs):
    inputs = sources * LAGS
    got_refs = [refs[first : first + LAGS] for first in range(0, inputs, LAGS)]
    _, *conv_refs, circulants, taps, results = refs[inputs:]
    halves = conv_refs[0].shape[0] // BLOCK
    add_circulants(partners(GATHER)[EARLY:], got_refs[0][EARLY:], circulants, taps)
    lane = lax.broadcasted_iota(jnp.int32, (BLOCK, LANES), 1)
    row = lax.broadcasted_iota(jnp.int32, (BLOCK, LANES), 0)
    causal = row.astype(jnp.int16) >= lane.astype(jnp.int16)
    granule = lane // GROUP
    for group in range(halves * SIDE):
        half, side = divmod(group, SIDE)
        rows = slice(half * BLOCK, (half + 1) * BLOCK)
        holds = (granule + (SIDE - side)) % SIDE
        sources_here = []
        for window in got_refs:
            source = window[0][rows, :]
            for partner, got_ref in zip(partners(GATHER)[1:], window[1:]):
                source = jnp.where(holds == partner, got_ref[rows, :], source)
            sources_here.append(source)
        before = jnp.zeros((BLOCK, LANES), jnp.bfloat16)
        filters, shifted = [], []
        for lag in range(LAGS):
            turned = circulants[lag, group]
            filters.append(jnp.where(causal, turned, before))
            before = turned
            moved = [pltpu.roll(source, lag * GROUP, 1) if lag else source for source in sources_here]
            if lag:
                carried = moved[1] if sources > 1 else jnp.zeros_like(moved[0])
                moved[0] = jnp.where(holds >= lag, moved[0], carried)
            shifted.append(moved[0])
        total = jnp.dot(
            jnp.concatenate(filters, axis=1),
            jnp.concatenate(shifted, axis=0),
            preferred_element_type=jnp.float32,
        )
        results[group] = total.astype(jnp.bfloat16)
    for half in range(halves):
        tiles = [results[half * SIDE + side] for side in range(SIDE)]
        for partner, conv_ref in zip(partners(RETURN), conv_refs):
            total = tiles[0]
            for side in range(1, SIDE):
                total = jnp.where(granule == (side + partner) % SIDE, tiles[side], total)
            conv_ref[half * BLOCK : (half + 1) * BLOCK, :] = total


def gate_kernel(query_ref, skip_ref, mixed_ref, *refs):
    conv_refs, (gated_hbm, gated_ref, left) = refs[:LAGS], refs[LAGS:]
    halves = conv_refs[0].shape[0] // BLOCK
    width = halves * LANES
    copies = []
    for index, partner in enumerate(partners(RETURN)):
        for half in range(halves):
            columns = pl.ds(pl.multiple_of((partner * halves + half) * LANES, LANES), LANES)
            rows = slice(half * BLOCK, (half + 1) * BLOCK)
            mixed = mixed_ref[:, columns].astype(jnp.float32)
            conv = turned_back(conv_refs[index][rows, :]).astype(jnp.float32)
            summed = conv + skip_ref[:, columns] * mixed
            gated_ref[:, columns] = (query_ref[:, columns].astype(jnp.float32) * summed).astype(jnp.bfloat16)
        columns = pl.ds(pl.multiple_of(partner * width, width), width)
        copy = pltpu.make_async_copy(gated_ref.at[:, columns], gated_hbm.at[:, columns], left.at[index])
        copy.start()
        copies.append(copy)
    for copy in copies:
        copy.wait()


def per_device(query, key, value, filter_taps, skip):
    rows, channels = query.shape
    halves = channels // LAGS // LANES
    count = lax.axis_size("ctx")
    if count > LAGS:
        all_taps = lax.all_gather(filter_taps, "ctx", axis=0, tiled=True)
        first_tap = lax.axis_index("ctx") % LAGS * BLOCK
        filter_taps = lax.dynamic_slice_in_dim(all_taps, first_tap, BLOCK, axis=0)
    in_hbm = [pltpu.with_memory_space_constraint(array, pltpu.HBM) for array in (key, value, filter_taps)]
    *sent, mixed = pl.pallas_call(
        mix_kernel,
        out_shape=[jax.ShapeDtypeStruct((halves * BLOCK + TILE, LANES), jnp.bfloat16)] * LAGS
        + [jax.ShapeDtypeStruct(key.shape, jnp.bfloat16)],
        in_specs=[pl.BlockSpec(memory_space=pl.ANY)] * 3,
        scratch_shapes=[
            pltpu.VMEM(key.shape, key.dtype),
            pltpu.VMEM(value.shape, value.dtype),
            pltpu.VMEM(filter_taps.shape, filter_taps.dtype),
            pltpu.VMEM((LANES, BLOCK), jnp.bfloat16),
            pltpu.SemaphoreType.DMA((2 * CHUNKS + 1,)),
        ],
        compiler_params=SMALL,
    )(*in_hbm)
    got = exchange(sent, GATHER)
    sources = 1
    if count > LAGS:
        sources = 2
        onward = [(source, source + LAGS) for source in range(count - LAGS)]
        got = got + [lax.ppermute(block, "ctx", onward) for block in got]
    whole = pl.BlockSpec(memory_space=pltpu.VMEM)
    every = jax.ShapeDtypeStruct((LAGS, TILE, BLOCK, LANES), jnp.bfloat16)
    circulants = pl.pallas_call(
        early_kernel,
        out_shape=every,
        in_specs=[whole] * EARLY,
        out_specs=whole,
        scratch_shapes=[pltpu.VMEM((EARLY, TILE, LANES), jnp.float32)],
        cost_estimate=pl.CostEstimate(flops=0, bytes_accessed=8 * 1024 * 1024, transcendentals=0),
        compiler_params=SMALL,
    )(*got[:EARLY])
    *conv, _ = pl.pallas_call(
        lambda *refs: conv_kernel(sources, *refs),
        out_shape=[jax.ShapeDtypeStruct((halves * BLOCK, LANES), jnp.bfloat16)] * LAGS + [every],
        in_specs=[whole] * (len(got) + 1),
        out_specs=[whole] * (LAGS + 1),
        scratch_shapes=[
            pltpu.VMEM((LAGS - EARLY, TILE, LANES), jnp.float32),
            pltpu.VMEM((halves * SIDE, BLOCK, LANES), jnp.bfloat16),
        ],
        input_output_aliases={len(got): LAGS},
        compiler_params=SMALL,
    )(*got, circulants)
    back = exchange(conv, RETURN)
    return pl.pallas_call(
        gate_kernel,
        out_shape=jax.ShapeDtypeStruct((rows, channels), jnp.bfloat16),
        in_specs=[whole] * (3 + LAGS),
        out_specs=pl.BlockSpec(memory_space=pl.ANY),
        scratch_shapes=[pltpu.VMEM((rows, channels), jnp.bfloat16), pltpu.SemaphoreType.DMA((LAGS,))],
        compiler_params=SMALL,
    )(query, skip.reshape(1, channels), mixed, *back)


def solution(mesh):
    placed = (P("ctx", "ch"), P("ctx", "ch"), P("ctx", "ch"), P("ctx", "ch"), P("ch"))
    return jax.shard_map(
        per_device, mesh=mesh, in_specs=placed, out_specs=P("ctx", "ch"), check_vma=False
    )
```

time: 40.1 us -> 38 us (0.948)
  starting transfers between devices: 24.6 us -> 22.6 us
    ppermute x14, starting transfers between devices: 24.6 us -> 22.6 us  [exchange(): got.append(lax.ppermute(block, ('ctx', 'ch'), pairs))]
    pallas_call x0 -> x1, Pallas kernels: none -> 1.09 us  [per_device(): pl.pallas_call(early_kernel, out_shape=every, in_specs=[whole] * EARLY, o...]
    pallas_call x1, Pallas kernels: 3.21 us -> 2.16 us  [per_device(): pl.pallas_call(lambda *refs: conv_kernel(sources, *refs), out_shape=[jax....]
  transfers between devices with their start and end apart: 14 -> 14, of which waited for: 7 -> 7; matrix products, arithmetic and copies ran while one was open for 0% -> 0% of each run, Pallas kernels for 0% -> 3%
where the time goes in v4:
time: 38 us; the launch traced here: 37.9 us
  starting transfers between devices  22.6 us (59%)
  waiting for transfers between devices  9.41 us (25%)
  Pallas kernels  5.84 us (15%)
    ppermute x14, starting transfers between devices, exchange(): got.append(lax.ppermute(block, ('ctx', 'ch'), pairs))  22.6 us
    ppermute x14, waiting for transfers between devices, exchange(): got.append(lax.ppermute(block, ('ctx', 'ch'), pairs))  9.41 us
    pallas_call x1, Pallas kernels, per_device(): pl.pallas_call(lambda *refs: conv_kernel(sources, *refs), out_shape=[jax....  2.16 us
    pallas_call x1, Pallas kernels, per_device(): pl.pallas_call(mix_kernel, out_shape=[jax.ShapeDtypeStruct((halves * BLOC...  1.51 us
    pallas_call x1, Pallas kernels, per_device(): pl.pallas_call(early_kernel, out_shape=every, in_specs=[whole] * EARLY, o...  1.09 us
    pallas_call x1, Pallas kernels, per_device(): pl.pallas_call(gate_kernel, out_shape=jax.ShapeDtypeStruct((rows, channel...  1.07 us
  transfers between devices with their start and end apart: 14, of which 7 were waited for; matrix products, arithmetic and copies ran while one was open for 0% of the time, Pallas kernels for 3%

profile of v4, /device:TPU:0, one launch (start us, length us, event | category | flops | bytes accessed | tf_op | source)
XLA Modules:
  0.0 37.9 jit_solution(10717549984718560423)
XLA Ops:
  0.0 1.5 %shard_map.55 = (bf16[272,128]{1,0:T(8,128)(2,1)S(1)}, bf16[272,128]{1,0:T(8,128)(2,1)S(1)}, bf16[272,128]{1,0:T(8,128)(2,1)S(1)}, bf16[272,128]{1,0:T(8,128)(2,...) custom-call(bf16[128,2048]{1,0:T(8,128)(2,1)} %key_hbm.1, ...), custom_call_target="tpu_custom_call" | custom-call | tf_op jit(solution)/shard_map/pallas_call | solution.py:178
  1.5 5.1 %collective-permute-start = (bf16[272,128]{1,0:T(8,128)(2,1)S(1)}, bf16[272,128]{1,0:T(8,128)(2,1)S(1)}, u32[]{:S(2)}, u32[]{:S(2)}) collective-permute-start(bf16[272,128]{1,0:T(8,128)(2,1)S(1)} %get-tuple-element.24), channel_id=1, source_target_pairs={{0,24},{1,25},{2,26},{3,27},{4,28},{5,29},{6,30},{7,31},{8,16},{9,... | collective-permute-start | bytes 208904 | tf_op jit(solution)/shard_map/ppermute | solution.py:36
  6.6 1.5 %collective-permute-start.1 = (bf16[272,128]{1,0:T(8,128)(2,1)S(1)}, bf16[272,128]{1,0:T(8,128)(2,1)S(1)}, u32[]{:S(2)}, u32[]{:S(2)}) collective-permute-start(bf16[272,128]{1,0:T(8,128)(2,1)S(1)} %get-tuple-element.25), channel_id=1, source_target_pairs={{0,4},{1,5},{2,6},{3,7},{4,0},{5,1},{6,2},{7,3},{8,12},{9,13},{10,... | collective-permute-start | bytes 208904 | tf_op jit(solution)/shard_map/ppermute | solution.py:36
  8.1 0.0 collective-permute-start.2
  8.1 0.8 %collective-permute-start.3 = (bf16[272,128]{1,0:T(8,128)(2,1)S(1)}, bf16[272,128]{1,0:T(8,128)(2,1)S(1)}, u32[]{:S(2)}, u32[]{:S(2)}) collective-permute-start(bf16[272,128]{1,0:T(8,128)(2,1)S(1)} %get-tuple-element.27), channel_id=1, source_target_pairs={{0,8},{1,9},{2,10},{3,11},{4,12},{5,13},{6,14},{7,15},{8,0},{9,1},... | collective-permute-start | bytes 208904 | tf_op jit(solution)/shard_map/ppermute | solution.py:36
  8.9 2.1 %collective-permute-start.4 = (bf16[272,128]{1,0:T(8,128)(2,1)S(1)}, bf16[272,128]{1,0:T(8,128)(2,1)S(1)}, u32[]{:S(2)}, u32[]{:S(2)}) collective-permute-start(bf16[272,128]{1,0:T(8,128)(2,1)S(1)} %get-tuple-element.28), channel_id=1, source_target_pairs={{0,20},{1,21},{2,22},{3,23},{4,16},{5,17},{6,18},{7,19},{8,28},{9,... | collective-permute-start | bytes 208904 | tf_op jit(solution)/shard_map/ppermute | solution.py:36
  11.0 0.0 collective-permute-done.refs_1_
  11.0 3.0 %collective-permute-start.5 = (bf16[272,128]{1,0:T(8,128)(2,1)S(1)}, bf16[272,128]{1,0:T(8,128)(2,1)S(1)}, u32[]{:S(2)}, u32[]{:S(2)}) collective-permute-start(bf16[272,128]{1,0:T(8,128)(2,1)S(1)} %get-tuple-element.29), channel_id=1, source_target_pairs={{0,12},{1,13},{2,14},{3,15},{4,8},{5,9},{6,10},{7,11},{8,4},{9,5},... | collective-permute-start | bytes 208904 | tf_op jit(solution)/shard_map/ppermute | solution.py:36
  14.0 0.0 collective-permute-done.1.refs_2_
  14.0 0.5 %collective-permute-start.6 = (bf16[272,128]{1,0:T(8,128)(2,1)S(1)}, bf16[272,128]{1,0:T(8,128)(2,1)S(1)}, u32[]{:S(2)}, u32[]{:S(2)}) collective-permute-start(bf16[272,128]{1,0:T(8,128)(2,1)S(1)} %get-tuple-element.30), channel_id=1, source_target_pairs={{0,28},{1,29},{2,30},{3,31},{4,24},{5,25},{6,26},{7,27},{8,20},{9,... | collective-permute-start | bytes 208904 | tf_op jit(solution)/shard_map/ppermute | solution.py:36
  14.4 0.3 collective-permute-done.2.refs_3_
  14.7 0.0 collective-permute-done.3.refs_4_
  14.7 2.1 %collective-permute-done.4.refs_5_ = bf16[272,128]{1,0:T(8,128)(2,1)S(1)} collective-permute-done((bf16[272,128]{1,0:T(8,128)(2,1)S(1)}, bf16[272,128]{1,0:T(8,128)(2,1)S(1)}, u32[]{:S(2)}, u32[]{:S(2)}) %collective-permute-start.4) | collective-permute-done | bytes 69664 | tf_op jit(solution)/shard_map/ppermute | solution.py:36
  16.8 0.0 collective-permute-done.5.refs_6_
  16.8 0.0 copy-start
  16.9 0.0 copy-start.1
  16.9 1.1 %shard_map.56.refs_8_ = bf16[8,16,128,128]{3,2,1,0:T(8,128)(2,1)S(1)} custom-call(bf16[272,128]{1,0:T(8,128)(2,1)S(1)} %get-tuple-element.23.refs_0_, bf16[272,128]{1,0:T(8,128)(2,1)S(1)} %collective-permute-done.refs_1_, bf16[272,128]{1,0:T(8,128)(2,1)S(1)} %collective-permute-done.1.refs_2_, bf16[272,128]{1,0:T(8,128)(2,1)S(1)} %collective-permute-done.2.refs_3_, ...), custom_call_target="tpu_custom_call" | custom-call | bytes 8388608 | tf_op jit(solution)/shard_map/pallas_call | solution.py:200
  18.0 3.0 %collective-permute-done.6.refs_7_ = bf16[272,128]{1,0:T(8,128)(2,1)S(1)} collective-permute-done((bf16[272,128]{1,0:T(8,128)(2,1)S(1)}, bf16[272,128]{1,0:T(8,128)(2,1)S(1)}, u32[]{:S(2)}, u32[]{:S(2)}) %collective-permute-start.6) | collective-permute-done | bytes 69664 | tf_op jit(solution)/shard_map/ppermute | solution.py:36
  21.0 2.2 %shard_map.57 = (bf16[256,128]{1,0:T(8,128)(2,1)S(1)}, bf16[256,128]{1,0:T(8,128)(2,1)S(1)}, bf16[256,128]{1,0:T(8,128)(2,1)S(1)}, bf16[256,128]{1,0:T(8,128)(2,...) custom-call(bf16[272,128]{1,0:T(8,128)(2,1)S(1)} %get-tuple-element., ...), custom_call_target="tpu_custom_call", output_to_operand_aliasing={{8}: (8, {})} | custom-call | tf_op jit(solution)/shard_map/pallas_call | solution.py:209
  23.2 0.1 collective-permute-start.7
  23.2 0.9 %collective-permute-start.8 = (bf16[256,128]{1,0:T(8,128)(2,1)S(1)}, bf16[256,128]{1,0:T(8,128)(2,1)S(1)}, u32[]{:S(2)}, u32[]{:S(2)}) collective-permute-start(bf16[256,128]{1,0:T(8,128)(2,1)S(1)} %get-tuple-element.33), channel_id=1, source_target_pairs={{0,4},{1,5},{2,6},{3,7},{4,0},{5,1},{6,2},{7,3},{8,12},{9,13},{10,... | collective-permute-start | bytes 196616 | tf_op jit(solution)/shard_map/ppermute | solution.py:36
  24.1 3.5 %collective-permute-start.9 = (bf16[256,128]{1,0:T(8,128)(2,1)S(1)}, bf16[256,128]{1,0:T(8,128)(2,1)S(1)}, u32[]{:S(2)}, u32[]{:S(2)}) collective-permute-start(bf16[256,128]{1,0:T(8,128)(2,1)S(1)} %get-tuple-element.34), channel_id=1, source_target_pairs={{0,20},{1,21},{2,22},{3,23},{4,16},{5,17},{6,18},{7,19},{8,28},{9,... | collective-permute-start | bytes 196616 | tf_op jit(solution)/shard_map/ppermute | solution.py:36
  27.6 0.0 collective-permute-start.10
  27.6 1.5 %collective-permute-start.11 = (bf16[256,128]{1,0:T(8,128)(2,1)S(1)}, bf16[256,128]{1,0:T(8,128)(2,1)S(1)}, u32[]{:S(2)}, u32[]{:S(2)}) collective-permute-start(bf16[256,128]{1,0:T(8,128)(2,1)S(1)} %get-tuple-element.36), channel_id=1, source_target_pairs={{0,24},{1,25},{2,26},{3,27},{4,28},{5,29},{6,30},{7,31},{8,16},{9,... | collective-permute-start | bytes 196616 | tf_op jit(solution)/shard_map/ppermute | solution.py:36
  29.2 0.6 %collective-permute-done.7.refs_1_ = bf16[256,128]{1,0:T(8,128)(2,1)S(1)} collective-permute-done((bf16[256,128]{1,0:T(8,128)(2,1)S(1)}, bf16[256,128]{1,0:T(8,128)(2,1)S(1)}, u32[]{:S(2)}, u32[]{:S(2)}) %collective-permute-start.7) | collective-permute-done | bytes 65568 | tf_op jit(solution)/shard_map/ppermute | solution.py:36
  29.8 0.0 collective-permute-start.12
  29.8 0.0 collective-permute-done.8.refs_2_
  29.8 3.7 %collective-permute-start.13 = (bf16[256,128]{1,0:T(8,128)(2,1)S(1)}, bf16[256,128]{1,0:T(8,128)(2,1)S(1)}, u32[]{:S(2)}, u32[]{:S(2)}) collective-permute-start(bf16[256,128]{1,0:T(8,128)(2,1)S(1)} %get-tuple-element.38), channel_id=1, source_target_pairs={{0,28},{1,29},{2,30},{3,31},{4,24},{5,25},{6,26},{7,27},{8,20},{9,... | collective-permute-start | bytes 196616 | tf_op jit(solution)/shard_map/ppermute | solution.py:36
  33.5 0.3 collective-permute-done.9.refs_3_
  33.8 0.0 collective-permute-done.10.refs_4_
  33.8 0.0 collective-permute-done.11.refs_5_
  33.8 1.2 %collective-permute-done.12.refs_6_ = bf16[256,128]{1,0:T(8,128)(2,1)S(1)} collective-permute-done((bf16[256,128]{1,0:T(8,128)(2,1)S(1)}, bf16[256,128]{1,0:T(8,128)(2,1)S(1)}, u32[]{:S(2)}, u32[]{:S(2)}) %collective-permute-start.12) | collective-permute-done | bytes 65568 | tf_op jit(solution)/shard_map/ppermute | solution.py:36
  35.0 1.8 %collective-permute-done.13.refs_7_ = bf16[256,128]{1,0:T(8,128)(2,1)S(1)} collective-permute-done((bf16[256,128]{1,0:T(8,128)(2,1)S(1)}, bf16[256,128]{1,0:T(8,128)(2,1)S(1)}, u32[]{:S(2)}, u32[]{:S(2)}) %collective-permute-start.13) | collective-permute-done | bytes 65568 | tf_op jit(solution)/shard_map/ppermute | solution.py:36
  36.8 0.0 copy-done
  36.8 0.0 copy-done.1
  36.8 1.1 %shard_map.58 = bf16[128,2048]{1,0:T(8,128)(2,1)} custom-call(bf16[128,2048]{1,0:T(8,128)(2,1)S(1)} %copy-done, f32[1,2048]{1,0:T(1,128)S(1)} %bitcast.1, bf16[128,2048]{1,0:T(8,128)(2,1)S(1)} %get-tuple-element.22.mixed_ref, bf16[256,128]{1,0:T(8,128)(2,1)S(1)} %get-tuple-element.31.refs_0_, bf16[256,128]{1,0:T(8,128)(2,1)S(1)} %collective-permute-done.7.refs_1_, ...), custom_call_target="tpu_custom_call" | custom-call | tf_op jit(solution)/shard_map/pallas_call | solution.py:222
Async XLA Ops:
  1.5 9.5 %collective-permute-start = (bf16[272,128]{1,0:T(8,128)(2,1)S(1)}, bf16[272,128]{1,0:T(8,128)(2,1)S(1)}, u32[]{:S(2)}, u32[]{:S(2)}) collective-permute-start(bf16[272,128]{1,0:T(8,128)(2,1)S(1)} %get-tuple-element.24), channel_id=1, source_target_pairs={{0,24},{1,25},{2,26},{3,27},{4,28},{5,29},{6,30},{7,31},{8,16},{9,... | collective-permute-start | bytes 208904 | tf_op jit(solution)/shard_map/ppermute | solution.py:36
  6.6 7.3 %collective-permute-start.1 = (bf16[272,128]{1,0:T(8,128)(2,1)S(1)}, bf16[272,128]{1,0:T(8,128)(2,1)S(1)}, u32[]{:S(2)}, u32[]{:S(2)}) collective-permute-start(bf16[272,128]{1,0:T(8,128)(2,1)S(1)} %get-tuple-element.25), channel_id=1, source_target_pairs={{0,4},{1,5},{2,6},{3,7},{4,0},{5,1},{6,2},{7,3},{8,12},{9,13},{10,... | collective-permute-start | bytes 208904 | tf_op jit(solution)/shard_map/ppermute | solution.py:36
  8.1 6.6 %collective-permute-start.2 = (bf16[272,128]{1,0:T(8,128)(2,1)S(1)}, bf16[272,128]{1,0:T(8,128)(2,1)S(1)}, u32[]{:S(2)}, u32[]{:S(2)}) collective-permute-start(bf16[272,128]{1,0:T(8,128)(2,1)S(1)} %get-tuple-element.26), channel_id=1, source_target_pairs={{0,16},{1,17},{2,18},{3,19},{4,20},{5,21},{6,22},{7,23},{8,24},{9,... | collective-permute-start | bytes 208904 | tf_op jit(solution)/shard_map/ppermute | solution.py:36
  8.1 6.6 %collective-permute-start.3 = (bf16[272,128]{1,0:T(8,128)(2,1)S(1)}, bf16[272,128]{1,0:T(8,128)(2,1)S(1)}, u32[]{:S(2)}, u32[]{:S(2)}) collective-permute-start(bf16[272,128]{1,0:T(8,128)(2,1)S(1)} %get-tuple-element.27), channel_id=1, source_target_pairs={{0,8},{1,9},{2,10},{3,11},{4,12},{5,13},{6,14},{7,15},{8,0},{9,1},... | collective-permute-start | bytes 208904 | tf_op jit(solution)/shard_map/ppermute | solution.py:36
  8.9 7.9 %collective-permute-start.4 = (bf16[272,128]{1,0:T(8,128)(2,1)S(1)}, bf16[272,128]{1,0:T(8,128)(2,1)S(1)}, u32[]{:S(2)}, u32[]{:S(2)}) collective-permute-start(bf16[272,128]{1,0:T(8,128)(2,1)S(1)} %get-tuple-element.28), channel_id=1, source_target_pairs={{0,20},{1,21},{2,22},{3,23},{4,16},{5,17},{6,18},{7,19},{8,28},{9,... | collective-permute-start | bytes 208904 | tf_op jit(solution)/shard_map/ppermute | solution.py:36
  11.0 5.8 %collective-permute-start.5 = (bf16[272,128]{1,0:T(8,128)(2,1)S(1)}, bf16[272,128]{1,0:T(8,128)(2,1)S(1)}, u32[]{:S(2)}, u32[]{:S(2)}) collective-permute-start(bf16[272,128]{1,0:T(8,128)(2,1)S(1)} %get-tuple-element.29), channel_id=1, source_target_pairs={{0,12},{1,13},{2,14},{3,15},{4,8},{5,9},{6,10},{7,11},{8,4},{9,5},... | collective-permute-start | bytes 208904 | tf_op jit(solution)/shard_map/ppermute | solution.py:36
  14.0 7.0 %collective-permute-start.6 = (bf16[272,128]{1,0:T(8,128)(2,1)S(1)}, bf16[272,128]{1,0:T(8,128)(2,1)S(1)}, u32[]{:S(2)}, u32[]{:S(2)}) collective-permute-start(bf16[272,128]{1,0:T(8,128)(2,1)S(1)} %get-tuple-element.30), channel_id=1, source_target_pairs={{0,28},{1,29},{2,30},{3,31},{4,24},{5,25},{6,26},{7,27},{8,20},{9,... | collective-permute-start | bytes 208904 | tf_op jit(solution)/shard_map/ppermute | solution.py:36
  16.8 19.9 %copy-start = (bf16[128,2048]{1,0:T(8,128)(2,1)S(1)}, bf16[128,2048]{1,0:T(8,128)(2,1)}, u32[]{:S(2)}) copy-start(bf16[128,2048]{1,0:T(8,128)(2,1)} %query_ref.1) | copy-start | bytes 1572868
  16.9 19.9 %copy-start.1 = (f32[2048]{0:T(1024)S(1)}, f32[2048]{0:T(1024)}, u32[]{:S(2)}) copy-start(f32[2048]{0:T(1024)} %param.9) | copy-start | bytes 24580
  23.2 6.6 %collective-permute-start.7 = (bf16[256,128]{1,0:T(8,128)(2,1)S(1)}, bf16[256,128]{1,0:T(8,128)(2,1)S(1)}, u32[]{:S(2)}, u32[]{:S(2)}) collective-permute-start(bf16[256,128]{1,0:T(8,128)(2,1)S(1)} %get-tuple-element.32), channel_id=1, source_target_pairs={{0,16},{1,17},{2,18},{3,19},{4,20},{5,21},{6,22},{7,23},{8,24},{9,... | collective-permute-start | bytes 196616 | tf_op jit(solution)/shard_map/ppermute | solution.py:36
  23.2 6.6 %collective-permute-start.8 = (bf16[256,128]{1,0:T(8,128)(2,1)S(1)}, bf16[256,128]{1,0:T(8,128)(2,1)S(1)}, u32[]{:S(2)}, u32[]{:S(2)}) collective-permute-start(bf16[256,128]{1,0:T(8,128)(2,1)S(1)} %get-tuple-element.33), channel_id=1, source_target_pairs={{0,4},{1,5},{2,6},{3,7},{4,0},{5,1},{6,2},{7,3},{8,12},{9,13},{10,... | collective-permute-start | bytes 196616 | tf_op jit(solution)/shard_map/ppermute | solution.py:36
  24.1 9.7 %collective-permute-start.9 = (bf16[256,128]{1,0:T(8,128)(2,1)S(1)}, bf16[256,128]{1,0:T(8,128)(2,1)S(1)}, u32[]{:S(2)}, u32[]{:S(2)}) collective-permute-start(bf16[256,128]{1,0:T(8,128)(2,1)S(1)} %get-tuple-element.34), channel_id=1, source_target_pairs={{0,20},{1,21},{2,22},{3,23},{4,16},{5,17},{6,18},{7,19},{8,28},{9,... | collective-permute-start | bytes 196616 | tf_op jit(solution)/shard_map/ppermute | solution.py:36
  27.6 6.1 %collective-permute-start.10 = (bf16[256,128]{1,0:T(8,128)(2,1)S(1)}, bf16[256,128]{1,0:T(8,128)(2,1)S(1)}, u32[]{:S(2)}, u32[]{:S(2)}) collective-permute-start(bf16[256,128]{1,0:T(8,128)(2,1)S(1)} %get-tuple-element.35), channel_id=1, source_target_pairs={{0,8},{1,9},{2,10},{3,11},{4,12},{5,13},{6,14},{7,15},{8,0},{9,1},... | collective-permute-start | bytes 196616 | tf_op jit(solution)/shard_map/ppermute | solution.py:36
  27.6 6.2 %collective-permute-start.11 = (bf16[256,128]{1,0:T(8,128)(2,1)S(1)}, bf16[256,128]{1,0:T(8,128)(2,1)S(1)}, u32[]{:S(2)}, u32[]{:S(2)}) collective-permute-start(bf16[256,128]{1,0:T(8,128)(2,1)S(1)} %get-tuple-element.36), channel_id=1, source_target_pairs={{0,24},{1,25},{2,26},{3,27},{4,28},{5,29},{6,30},{7,31},{8,16},{9,... | collective-permute-start | bytes 196616 | tf_op jit(solution)/shard_map/ppermute | solution.py:36
  29.8 5.2 %collective-permute-start.12 = (bf16[256,128]{1,0:T(8,128)(2,1)S(1)}, bf16[256,128]{1,0:T(8,128)(2,1)S(1)}, u32[]{:S(2)}, u32[]{:S(2)}) collective-permute-start(bf16[256,128]{1,0:T(8,128)(2,1)S(1)} %get-tuple-element.37), channel_id=1, source_target_pairs={{0,12},{1,13},{2,14},{3,15},{4,8},{5,9},{6,10},{7,11},{8,4},{9,5},... | collective-permute-start | bytes 196616 | tf_op jit(solution)/shard_map/ppermute | solution.py:36
  29.8 7.0 %collective-permute-start.13 = (bf16[256,128]{1,0:T(8,128)(2,1)S(1)}, bf16[256,128]{1,0:T(8,128)(2,1)S(1)}, u32[]{:S(2)}, u32[]{:S(2)}) collective-permute-start(bf16[256,128]{1,0:T(8,128)(2,1)S(1)} %get-tuple-element.38), channel_id=1, source_target_pairs={{0,28},{1,29},{2,30},{3,31},{4,24},{5,25},{6,26},{7,27},{8,20},{9,... | collective-permute-start | bytes 196616 | tf_op jit(solution)/shard_map/ppermute | solution.py:36

commit v5 on v4

--- a/solution.py
+++ b/solution.py
@@ -1,3 +1,5 @@
+import functools
+
 import jax
 import jax.numpy as jnp
 from jax import lax
@@ -11,10 +13,12 @@
 LANES = 128
 TILE = 16
 SIDE = LANES // GROUP
-GATHER = ((6, 1, 4, 2, 5, 3, 7), (6, 1, 4, 2, 5, 3, 7))
+GATHER = ((6, 2, 4, 1, 5, 3, 7), (6, 2, 4, 1, 5, 3, 7))
 RETURN = ((4, 1, 5, 2, 6, 3, 7), (4, 1, 5, 2, 6, 3, 7))
 CHUNKS = 2
 EARLY = 7
+AHEAD = 2
+FIRST = 7
 SMALL = pltpu.CompilerParams(vmem_limit_bytes=16 * 1024 * 1024)
 
 
@@ -82,21 +86,20 @@
                 sent_ref[there, :] = pltpu.roll(mixed, place() * GROUP, 1)
 
 
-def add_circulants(where, got_refs, circulants, taps):
+def circulant(row):
+    return pltpu.roll(jnp.broadcast_to(row, (BLOCK, LANES)), 0, 1, stride=1, stride_axis=0).astype(jnp.bfloat16)
+
+
+def early_kernel(*refs):
+    *got_refs, circulants, taps = refs
     rows = got_refs[0].shape[0]
     for index, got_ref in enumerate(got_refs):
         taps[index] = got_ref[rows - TILE : rows, :].astype(jnp.float32)
 
     @pl.loop(0, TILE, unroll=8)
     def _(group):
-        for index, partner in enumerate(where):
-            own = jnp.broadcast_to(taps[index, pl.ds(group, 1), :], (BLOCK, LANES))
-            circulants[partner, group] = pltpu.roll(own, 0, 1, stride=1, stride_axis=0).astype(jnp.bfloat16)
-
-
-def early_kernel(*refs):
-    *got_refs, circulants, taps = refs
-    add_circulants(partners(GATHER)[:EARLY], got_refs, circulants, taps)
+        for index, partner in enumerate(partners(GATHER)[:EARLY]):
+            circulants[partner, group] = circulant(taps[index, pl.ds(group, 1), :])
 
 
 def conv_kernel(sources, *refs):
@@ -104,12 +107,23 @@
     got_refs = [refs[first : first + LAGS] for first in range(0, inputs, LAGS)]
     _, *conv_refs, circulants, taps, results = refs[inputs:]
     halves = conv_refs[0].shape[0] // BLOCK
-    add_circulants(partners(GATHER)[EARLY:], got_refs[0][EARLY:], circulants, taps)
+    late = list(zip(partners(GATHER), got_refs[0]))[EARLY:]
+    for index, (_, got_ref) in enumerate(late):
+        taps[index] = got_ref[halves * BLOCK : halves * BLOCK + TILE, :].astype(jnp.float32)
+
+    def add_late(group):
+        for index, (partner, _) in enumerate(late):
+            circulants[partner, group] = circulant(taps[index, group : group + 1, :])
+
+    for group in range(AHEAD):
+        add_late(group)
     lane = lax.broadcasted_iota(jnp.int32, (BLOCK, LANES), 1)
     row = lax.broadcasted_iota(jnp.int32, (BLOCK, LANES), 0)
     causal = row.astype(jnp.int16) >= lane.astype(jnp.int16)
     granule = lane // GROUP
     for group in range(halves * SIDE):
+        if group + AHEAD < halves * SIDE:
+            add_late(group + AHEAD)
         half, side = divmod(group, SIDE)
         rows = slice(half * BLOCK, (half + 1) * BLOCK)
         holds = (granule + (SIDE - side)) % SIDE
@@ -145,12 +159,12 @@
             conv_ref[half * BLOCK : (half + 1) * BLOCK, :] = total
 
 
-def gate_kernel(query_ref, skip_ref, mixed_ref, *refs):
-    conv_refs, (gated_hbm, gated_ref, left) = refs[:LAGS], refs[LAGS:]
+def gate_kernel(rounds, query_ref, skip_ref, mixed_ref, *refs):
+    conv_refs, (gated_hbm, gated_ref, left) = refs[: rounds.stop - rounds.start], refs[-3:]
     halves = conv_refs[0].shape[0] // BLOCK
     width = halves * LANES
     copies = []
-    for index, partner in enumerate(partners(RETURN)):
+    for index, partner in enumerate(partners(RETURN)[rounds]):
         for half in range(halves):
             columns = pl.ds(pl.multiple_of((partner * halves + half) * LANES, LANES), LANES)
             rows = slice(half * BLOCK, (half + 1) * BLOCK)
@@ -219,14 +233,24 @@
         compiler_params=SMALL,
     )(*got, circulants)
     back = exchange(conv, RETURN)
-    return pl.pallas_call(
-        gate_kernel,
-        out_shape=jax.ShapeDtypeStruct((rows, channels), jnp.bfloat16),
-        in_specs=[whole] * (3 + LAGS),
-        out_specs=pl.BlockSpec(memory_space=pl.ANY),
-        scratch_shapes=[pltpu.VMEM((rows, channels), jnp.bfloat16), pltpu.SemaphoreType.DMA((LAGS,))],
-        compiler_params=SMALL,
-    )(query, skip.reshape(1, channels), mixed, *back)
+    gated = None
+    for rounds in (slice(0, FIRST), slice(FIRST, LAGS)):
+        size = rounds.stop - rounds.start
+        inputs = [query, skip.reshape(1, channels), mixed, *back[rounds]]
+        specs = [whole] * len(inputs)
+        if gated is not None:
+            inputs.append(gated)
+            specs.append(pl.BlockSpec(memory_space=pl.ANY))
+        gated = pl.pallas_call(
+            functools.partial(gate_kernel, rounds),
+            out_shape=jax.ShapeDtypeStruct((rows, channels), jnp.bfloat16),
+            in_specs=specs,
+            out_specs=pl.BlockSpec(memory_space=pl.ANY),
+            scratch_shapes=[pltpu.VMEM((rows, channels), jnp.bfloat16), pltpu.SemaphoreType.DMA((size,))],
+            input_output_aliases={} if gated is None else {len(inputs) - 1: 0},
+            compiler_params=SMALL,
+        )(*inputs)
+    return gated
 
 
 def solution(mesh):

time: 38 us -> 37.4 us (0.984)
  waiting for transfers between devices: 9.41 us -> 7.71 us
  starting transfers between devices: 22.6 us -> 23.2 us
  Pallas kernels: 5.84 us -> 6.31 us
    ppermute x14, waiting for transfers between devices: 9.41 us -> 7.71 us  [exchange(): got.append(lax.ppermute(block, ('ctx', 'ch'), pairs))]
    pallas_call x1 -> x2, Pallas kernels: 1.07 us -> 1.76 us  [per_device(): pl.pallas_call(functools.partial(gate_kernel, rounds), out_shape=jax.Shap...]
    ppermute x14, starting transfers between devices: 22.6 us -> 23.2 us  [exchange(): got.append(lax.ppermute(block, ('ctx', 'ch'), pairs))]
  transfers between devices with their start and end apart: 14 -> 14, of which waited for: 7 -> 6; matrix products, arithmetic and copies ran while one was open for 0% -> 0% of each run, Pallas kernels for 3% -> 6%
where the time goes in v5:
time: 37.4 us; the launch traced here: 37.3 us
  starting transfers between devices  23.2 us (62%)
  waiting for transfers between devices  7.71 us (21%)
  Pallas kernels  6.31 us (17%)
    ppermute x14, starting transfers between devices, exchange(): got.append(lax.ppermute(block, ('ctx', 'ch'), pairs))  23.2 us
    ppermute x14, waiting for transfers between devices, exchange(): got.append(lax.ppermute(block, ('ctx', 'ch'), pairs))  7.71 us
    pallas_call x1, Pallas kernels, per_device(): pl.pallas_call(lambda *refs: conv_kernel(sources, *refs), out_shape=[jax....  1.95 us
    pallas_call x2, Pallas kernels, per_device(): pl.pallas_call(functools.partial(gate_kernel, rounds), out_shape=jax.Shap...  1.76 us
    pallas_call x1, Pallas kernels, per_device(): pl.pallas_call(mix_kernel, out_shape=[jax.ShapeDtypeStruct((halves * BLOC...  1.51 us
    pallas_call x1, Pallas kernels, per_device(): pl.pallas_call(early_kernel, out_shape=every, in_specs=[whole] * EARLY, o...  1.09 us
  transfers between devices with their start and end apart: 14, of which 6 were waited for; matrix products, arithmetic and copies ran while one was open for 0% of the time, Pallas kernels for 6%

profile of v5, /device:TPU:0, one launch (start us, length us, event | category | flops | bytes accessed | tf_op | source)
XLA Modules:
  0.0 37.3 jit_solution(2976838487483911320)
XLA Ops:
  0.0 1.5 %shard_map.55 = (bf16[272,128]{1,0:T(8,128)(2,1)S(1)}, bf16[272,128]{1,0:T(8,128)(2,1)S(1)}, bf16[272,128]{1,0:T(8,128)(2,1)S(1)}, bf16[272,128]{1,0:T(8,128)(2,...) custom-call(bf16[128,2048]{1,0:T(8,128)(2,1)} %key_hbm.1, ...), custom_call_target="tpu_custom_call" | custom-call | tf_op jit(solution)/shard_map/pallas_call | solution.py:192
  1.5 5.1 %collective-permute-start = (bf16[272,128]{1,0:T(8,128)(2,1)S(1)}, bf16[272,128]{1,0:T(8,128)(2,1)S(1)}, u32[]{:S(2)}, u32[]{:S(2)}) collective-permute-start(bf16[272,128]{1,0:T(8,128)(2,1)S(1)} %get-tuple-element.24), channel_id=1, source_target_pairs={{0,24},{1,25},{2,26},{3,27},{4,28},{5,29},{6,30},{7,31},{8,16},{9,... | collective-permute-start | bytes 208904 | tf_op jit(solution)/shard_map/ppermute | solution.py:40
  6.6 0.0 collective-permute-start.1
  6.6 0.6 %collective-permute-start.2 = (bf16[272,128]{1,0:T(8,128)(2,1)S(1)}, bf16[272,128]{1,0:T(8,128)(2,1)S(1)}, u32[]{:S(2)}, u32[]{:S(2)}) collective-permute-start(bf16[272,128]{1,0:T(8,128)(2,1)S(1)} %get-tuple-element.26), channel_id=1, source_target_pairs={{0,16},{1,17},{2,18},{3,19},{4,20},{5,21},{6,22},{7,23},{8,24},{9,... | collective-permute-start | bytes 208904 | tf_op jit(solution)/shard_map/ppermute | solution.py:40
  7.3 1.6 %collective-permute-start.3 = (bf16[272,128]{1,0:T(8,128)(2,1)S(1)}, bf16[272,128]{1,0:T(8,128)(2,1)S(1)}, u32[]{:S(2)}, u32[]{:S(2)}) collective-permute-start(bf16[272,128]{1,0:T(8,128)(2,1)S(1)} %get-tuple-element.27), channel_id=1, source_target_pairs={{0,4},{1,5},{2,6},{3,7},{4,0},{5,1},{6,2},{7,3},{8,12},{9,13},{10,... | collective-permute-start | bytes 208904 | tf_op jit(solution)/shard_map/ppermute | solution.py:40
  8.9 2.1 %collective-permute-start.4 = (bf16[272,128]{1,0:T(8,128)(2,1)S(1)}, bf16[272,128]{1,0:T(8,128)(2,1)S(1)}, u32[]{:S(2)}, u32[]{:S(2)}) collective-permute-start(bf16[272,128]{1,0:T(8,128)(2,1)S(1)} %get-tuple-element.28), channel_id=1, source_target_pairs={{0,20},{1,21},{2,22},{3,23},{4,16},{5,17},{6,18},{7,19},{8,28},{9,... | collective-permute-start | bytes 208904 | tf_op jit(solution)/shard_map/ppermute | solution.py:40
  11.0 0.0 collective-permute-done.refs_1_
  11.0 3.0 %collective-permute-start.5 = (bf16[272,128]{1,0:T(8,128)(2,1)S(1)}, bf16[272,128]{1,0:T(8,128)(2,1)S(1)}, u32[]{:S(2)}, u32[]{:S(2)}) collective-permute-start(bf16[272,128]{1,0:T(8,128)(2,1)S(1)} %get-tuple-element.29), channel_id=1, source_target_pairs={{0,12},{1,13},{2,14},{3,15},{4,8},{5,9},{6,10},{7,11},{8,4},{9,5},... | collective-permute-start | bytes 208904 | tf_op jit(solution)/shard_map/ppermute | solution.py:40
  14.0 0.0 collective-permute-done.1.refs_2_
  14.0 0.5 %collective-permute-start.6 = (bf16[272,128]{1,0:T(8,128)(2,1)S(1)}, bf16[272,128]{1,0:T(8,128)(2,1)S(1)}, u32[]{:S(2)}, u32[]{:S(2)}) collective-permute-start(bf16[272,128]{1,0:T(8,128)(2,1)S(1)} %get-tuple-element.30), channel_id=1, source_target_pairs={{0,28},{1,29},{2,30},{3,31},{4,24},{5,25},{6,26},{7,27},{8,20},{9,... | collective-permute-start | bytes 208904 | tf_op jit(solution)/shard_map/ppermute | solution.py:40
  14.4 0.9 %collective-permute-done.2.refs_3_ = bf16[272,128]{1,0:T(8,128)(2,1)S(1)} collective-permute-done((bf16[272,128]{1,0:T(8,128)(2,1)S(1)}, bf16[272,128]{1,0:T(8,128)(2,1)S(1)}, u32[]{:S(2)}, u32[]{:S(2)}) %collective-permute-start.2) | collective-permute-done | bytes 69664 | tf_op jit(solution)/shard_map/ppermute | solution.py:40
  15.3 0.0 collective-permute-done.3.refs_4_
  15.3 3.2 %collective-permute-done.4.refs_5_ = bf16[272,128]{1,0:T(8,128)(2,1)S(1)} collective-permute-done((bf16[272,128]{1,0:T(8,128)(2,1)S(1)}, bf16[272,128]{1,0:T(8,128)(2,1)S(1)}, u32[]{:S(2)}, u32[]{:S(2)}) %collective-permute-start.4) | collective-permute-done | bytes 69664 | tf_op jit(solution)/shard_map/ppermute | solution.py:40
  18.5 0.0 collective-permute-done.5.refs_6_
  18.5 0.0 copy-start
  18.5 0.0 copy-start.1
  18.5 1.1 %shard_map.56.refs_8_ = bf16[8,16,128,128]{3,2,1,0:T(8,128)(2,1)S(1)} custom-call(bf16[272,128]{1,0:T(8,128)(2,1)S(1)} %get-tuple-element.23.refs_0_, bf16[272,128]{1,0:T(8,128)(2,1)S(1)} %collective-permute-done.refs_1_, bf16[272,128]{1,0:T(8,128)(2,1)S(1)} %collective-permute-done.1.refs_2_, bf16[272,128]{1,0:T(8,128)(2,1)S(1)} %collective-permute-done.2.refs_3_, ...), custom_call_target="tpu_custom_call" | custom-call | bytes 8388608 | tf_op jit(solution)/shard_map/pallas_call | solution.py:214
  19.6 1.4 %collective-permute-done.6.refs_7_ = bf16[272,128]{1,0:T(8,128)(2,1)S(1)} collective-permute-done((bf16[272,128]{1,0:T(8,128)(2,1)S(1)}, bf16[272,128]{1,0:T(8,128)(2,1)S(1)}, u32[]{:S(2)}, u32[]{:S(2)}) %collective-permute-start.6) | collective-permute-done | bytes 69664 | tf_op jit(solution)/shard_map/ppermute | solution.py:40
  21.0 1.9 %shard_map.57 = (bf16[256,128]{1,0:T(8,128)(2,1)S(1)}, bf16[256,128]{1,0:T(8,128)(2,1)S(1)}, bf16[256,128]{1,0:T(8,128)(2,1)S(1)}, bf16[256,128]{1,0:T(8,128)(2,...) custom-call(bf16[272,128]{1,0:T(8,128)(2,1)S(1)} %get-tuple-element., ...), custom_call_target="tpu_custom_call", output_to_operand_aliasing={{8}: (8, {})} | custom-call | tf_op jit(solution)/shard_map/pallas_call | solution.py:223
  22.9 0.5 %collective-permute-start.8 = (bf16[256,128]{1,0:T(8,128)(2,1)S(1)}, bf16[256,128]{1,0:T(8,128)(2,1)S(1)}, u32[]{:S(2)}, u32[]{:S(2)}) collective-permute-start(bf16[256,128]{1,0:T(8,128)(2,1)S(1)} %get-tuple-element.33), channel_id=1, source_target_pairs={{0,16},{1,17},{2,18},{3,19},{4,20},{5,21},{6,22},{7,23},{8,24},{9,... | collective-permute-start | bytes 196616 | tf_op jit(solution)/shard_map/ppermute | solution.py:40
  23.4 0.5 %collective-permute-start.9 = (bf16[256,128]{1,0:T(8,128)(2,1)S(1)}, bf16[256,128]{1,0:T(8,128)(2,1)S(1)}, u32[]{:S(2)}, u32[]{:S(2)}) collective-permute-start(bf16[256,128]{1,0:T(8,128)(2,1)S(1)} %get-tuple-element.34), channel_id=1, source_target_pairs={{0,4},{1,5},{2,6},{3,7},{4,0},{5,1},{6,2},{7,3},{8,12},{9,13},{10,... | collective-permute-start | bytes 196616 | tf_op jit(solution)/shard_map/ppermute | solution.py:40
  23.9 3.5 %collective-permute-start.10 = (bf16[256,128]{1,0:T(8,128)(2,1)S(1)}, bf16[256,128]{1,0:T(8,128)(2,1)S(1)}, u32[]{:S(2)}, u32[]{:S(2)}) collective-permute-start(bf16[256,128]{1,0:T(8,128)(2,1)S(1)} %get-tuple-element.35), channel_id=1, source_target_pairs={{0,20},{1,21},{2,22},{3,23},{4,16},{5,17},{6,18},{7,19},{8,28},{9,... | collective-permute-start | bytes 196616 | tf_op jit(solution)/shard_map/ppermute | solution.py:40
  27.4 0.0 collective-permute-start.11
  27.4 1.9 %collective-permute-start.12 = (bf16[256,128]{1,0:T(8,128)(2,1)S(1)}, bf16[256,128]{1,0:T(8,128)(2,1)S(1)}, u32[]{:S(2)}, u32[]{:S(2)}) collective-permute-start(bf16[256,128]{1,0:T(8,128)(2,1)S(1)} %get-tuple-element.37), channel_id=1, source_target_pairs={{0,24},{1,25},{2,26},{3,27},{4,28},{5,29},{6,30},{7,31},{8,16},{9,... | collective-permute-start | bytes 196616 | tf_op jit(solution)/shard_map/ppermute | solution.py:40
  29.3 0.0 collective-permute-done.8.refs_1_
  29.3 0.3 collective-permute-start.13
  29.5 0.0 collective-permute-done.9.refs_2_
  29.5 3.7 %collective-permute-start.7 = (bf16[256,128]{1,0:T(8,128)(2,1)S(1)}, bf16[256,128]{1,0:T(8,128)(2,1)S(1)}, u32[]{:S(2)}, u32[]{:S(2)}) collective-permute-start(bf16[256,128]{1,0:T(8,128)(2,1)S(1)} %get-tuple-element.31), channel_id=1, source_target_pairs={{0,28},{1,29},{2,30},{3,31},{4,24},{5,25},{6,26},{7,27},{8,20},{9,... | collective-permute-start | bytes 196616 | tf_op jit(solution)/shard_map/ppermute | solution.py:40
  33.3 0.0 collective-permute-done.10.refs_3_
  33.3 0.0 collective-permute-done.11.refs_4_
  33.3 0.2 collective-permute-done.12.refs_5_
  33.5 1.4 %collective-permute-done.13.refs_6_ = bf16[256,128]{1,0:T(8,128)(2,1)S(1)} collective-permute-done((bf16[256,128]{1,0:T(8,128)(2,1)S(1)}, bf16[256,128]{1,0:T(8,128)(2,1)S(1)}, u32[]{:S(2)}, u32[]{:S(2)}) %collective-permute-start.13) | collective-permute-done | bytes 65568 | tf_op jit(solution)/shard_map/ppermute | solution.py:40
  34.9 0.0 copy-done
  34.9 0.0 copy-done.1
  34.9 1.0 %shard_map.58.refs_1_ = bf16[128,2048]{1,0:T(8,128)(2,1)} custom-call(bf16[128,2048]{1,0:T(8,128)(2,1)S(1)} %copy-done, f32[1,2048]{1,0:T(1,128)S(1)} %bitcast.1, bf16[128,2048]{1,0:T(8,128)(2,1)S(1)} %get-tuple-element.22.mixed_ref, bf16[256,128]{1,0:T(8,128)(2,1)S(1)} %get-tuple-element.32.refs_0_, bf16[256,128]{1,0:T(8,128)(2,1)S(1)} %collective-permute-done.8.refs_1_, ...), custom_call_target="tpu_custom_call" | custom-call | tf_op jit(solution)/shard_map/pallas_call | solution.py:244
  36.0 0.6 %collective-permute-done.7.refs_0_ = bf16[256,128]{1,0:T(8,128)(2,1)S(1)} collective-permute-done((bf16[256,128]{1,0:T(8,128)(2,1)S(1)}, bf16[256,128]{1,0:T(8,128)(2,1)S(1)}, u32[]{:S(2)}, u32[]{:S(2)}) %collective-permute-start.7) | collective-permute-done | bytes 65568 | tf_op jit(solution)/shard_map/ppermute | solution.py:40
  36.5 0.7 %shard_map.59 = bf16[128,2048]{1,0:T(8,128)(2,1)} custom-call(bf16[128,2048]{1,0:T(8,128)(2,1)S(1)} %copy-done, f32[1,2048]{1,0:T(1,128)S(1)} %bitcast.2, bf16[128,2048]{1,0:T(8,128)(2,1)S(1)} %get-tuple-element.22.mixed_ref, bf16[256,128]{1,0:T(8,128)(2,1)S(1)} %collective-permute-done.7.refs_0_, ...), custom_call_target="tpu_custom_call", output_to_operand_aliasing={{}: (4, {})} | custom-call | tf_op jit(solution)/shard_map/pallas_call | solution.py:244
Async XLA Ops:
  1.5 9.5 %collective-permute-start = (bf16[272,128]{1,0:T(8,128)(2,1)S(1)}, bf16[272,128]{1,0:T(8,128)(2,1)S(1)}, u32[]{:S(2)}, u32[]{:S(2)}) collective-permute-start(bf16[272,128]{1,0:T(8,128)(2,1)S(1)} %get-tuple-element.24), channel_id=1, source_target_pairs={{0,24},{1,25},{2,26},{3,27},{4,28},{5,29},{6,30},{7,31},{8,16},{9,... | collective-permute-start | bytes 208904 | tf_op jit(solution)/shard_map/ppermute | solution.py:40
  6.6 7.3 %collective-permute-start.1 = (bf16[272,128]{1,0:T(8,128)(2,1)S(1)}, bf16[272,128]{1,0:T(8,128)(2,1)S(1)}, u32[]{:S(2)}, u32[]{:S(2)}) collective-permute-start(bf16[272,128]{1,0:T(8,128)(2,1)S(1)} %get-tuple-element.25), channel_id=1, source_target_pairs={{0,8},{1,9},{2,10},{3,11},{4,12},{5,13},{6,14},{7,15},{8,0},{9,1},... | collective-permute-start | bytes 208904 | tf_op jit(solution)/shard_map/ppermute | solution.py:40
  6.6 8.7 %collective-permute-start.2 = (bf16[272,128]{1,0:T(8,128)(2,1)S(1)}, bf16[272,128]{1,0:T(8,128)(2,1)S(1)}, u32[]{:S(2)}, u32[]{:S(2)}) collective-permute-start(bf16[272,128]{1,0:T(8,128)(2,1)S(1)} %get-tuple-element.26), channel_id=1, source_target_pairs={{0,16},{1,17},{2,18},{3,19},{4,20},{5,21},{6,22},{7,23},{8,24},{9,... | collective-permute-start | bytes 208904 | tf_op jit(solution)/shard_map/ppermute | solution.py:40
  7.3 8.1 %collective-permute-start.3 = (bf16[272,128]{1,0:T(8,128)(2,1)S(1)}, bf16[272,128]{1,0:T(8,128)(2,1)S(1)}, u32[]{:S(2)}, u32[]{:S(2)}) collective-permute-start(bf16[272,128]{1,0:T(8,128)(2,1)S(1)} %get-tuple-element.27), channel_id=1, source_target_pairs={{0,4},{1,5},{2,6},{3,7},{4,0},{5,1},{6,2},{7,3},{8,12},{9,13},{10,... | collective-permute-start | bytes 208904 | tf_op jit(solution)/shard_map/ppermute | solution.py:40
  8.9 9.6 %collective-permute-start.4 = (bf16[272,128]{1,0:T(8,128)(2,1)S(1)}, bf16[272,128]{1,0:T(8,128)(2,1)S(1)}, u32[]{:S(2)}, u32[]{:S(2)}) collective-permute-start(bf16[272,128]{1,0:T(8,128)(2,1)S(1)} %get-tuple-element.28), channel_id=1, source_target_pairs={{0,20},{1,21},{2,22},{3,23},{4,16},{5,17},{6,18},{7,19},{8,28},{9,... | collective-permute-start | bytes 208904 | tf_op jit(solution)/shard_map/ppermute | solution.py:40
  11.0 7.5 %collective-permute-start.5 = (bf16[272,128]{1,0:T(8,128)(2,1)S(1)}, bf16[272,128]{1,0:T(8,128)(2,1)S(1)}, u32[]{:S(2)}, u32[]{:S(2)}) collective-permute-start(bf16[272,128]{1,0:T(8,128)(2,1)S(1)} %get-tuple-element.29), channel_id=1, source_target_pairs={{0,12},{1,13},{2,14},{3,15},{4,8},{5,9},{6,10},{7,11},{8,4},{9,5},... | collective-permute-start | bytes 208904 | tf_op jit(solution)/shard_map/ppermute | solution.py:40
  14.0 7.0 %collective-permute-start.6 = (bf16[272,128]{1,0:T(8,128)(2,1)S(1)}, bf16[272,128]{1,0:T(8,128)(2,1)S(1)}, u32[]{:S(2)}, u32[]{:S(2)}) collective-permute-start(bf16[272,128]{1,0:T(8,128)(2,1)S(1)} %get-tuple-element.30), channel_id=1, source_target_pairs={{0,28},{1,29},{2,30},{3,31},{4,24},{5,25},{6,26},{7,27},{8,20},{9,... | collective-permute-start | bytes 208904 | tf_op jit(solution)/shard_map/ppermute | solution.py:40
  18.5 16.4 %copy-start = (bf16[128,2048]{1,0:T(8,128)(2,1)S(1)}, bf16[128,2048]{1,0:T(8,128)(2,1)}, u32[]{:S(2)}) copy-start(bf16[128,2048]{1,0:T(8,128)(2,1)} %query_ref.3) | copy-start | bytes 1572868
  18.5 16.4 %copy-start.1 = (f32[2048]{0:T(1024)S(1)}, f32[2048]{0:T(1024)}, u32[]{:S(2)}) copy-start(f32[2048]{0:T(1024)} %param.9) | copy-start | bytes 24580
  22.9 6.3 %collective-permute-start.8 = (bf16[256,128]{1,0:T(8,128)(2,1)S(1)}, bf16[256,128]{1,0:T(8,128)(2,1)S(1)}, u32[]{:S(2)}, u32[]{:S(2)}) collective-permute-start(bf16[256,128]{1,0:T(8,128)(2,1)S(1)} %get-tuple-element.33), channel_id=1, source_target_pairs={{0,16},{1,17},{2,18},{3,19},{4,20},{5,21},{6,22},{7,23},{8,24},{9,... | collective-permute-start | bytes 196616 | tf_op jit(solution)/shard_map/ppermute | solution.py:40
  23.4 6.1 %collective-permute-start.9 = (bf16[256,128]{1,0:T(8,128)(2,1)S(1)}, bf16[256,128]{1,0:T(8,128)(2,1)S(1)}, u32[]{:S(2)}, u32[]{:S(2)}) collective-permute-start(bf16[256,128]{1,0:T(8,128)(2,1)S(1)} %get-tuple-element.34), channel_id=1, source_target_pairs={{0,4},{1,5},{2,6},{3,7},{4,0},{5,1},{6,2},{7,3},{8,12},{9,13},{10,... | collective-permute-start | bytes 196616 | tf_op jit(solution)/shard_map/ppermute | solution.py:40
  23.9 9.3 %collective-permute-start.10 = (bf16[256,128]{1,0:T(8,128)(2,1)S(1)}, bf16[256,128]{1,0:T(8,128)(2,1)S(1)}, u32[]{:S(2)}, u32[]{:S(2)}) collective-permute-start(bf16[256,128]{1,0:T(8,128)(2,1)S(1)} %get-tuple-element.35), channel_id=1, source_target_pairs={{0,20},{1,21},{2,22},{3,23},{4,16},{5,17},{6,18},{7,19},{8,28},{9,... | collective-permute-start | bytes 196616 | tf_op jit(solution)/shard_map/ppermute | solution.py:40
  27.4 5.9 %collective-permute-start.11 = (bf16[256,128]{1,0:T(8,128)(2,1)S(1)}, bf16[256,128]{1,0:T(8,128)(2,1)S(1)}, u32[]{:S(2)}, u32[]{:S(2)}) collective-permute-start(bf16[256,128]{1,0:T(8,128)(2,1)S(1)} %get-tuple-element.36), channel_id=1, source_target_pairs={{0,8},{1,9},{2,10},{3,11},{4,12},{5,13},{6,14},{7,15},{8,0},{9,1},... | collective-permute-start | bytes 196616 | tf_op jit(solution)/shard_map/ppermute | solution.py:40
  27.4 6.1 %collective-permute-start.12 = (bf16[256,128]{1,0:T(8,128)(2,1)S(1)}, bf16[256,128]{1,0:T(8,128)(2,1)S(1)}, u32[]{:S(2)}, u32[]{:S(2)}) collective-permute-start(bf16[256,128]{1,0:T(8,128)(2,1)S(1)} %get-tuple-element.37), channel_id=1, source_target_pairs={{0,24},{1,25},{2,26},{3,27},{4,28},{5,29},{6,30},{7,31},{8,16},{9,... | collective-permute-start | bytes 196616 | tf_op jit(solution)/shard_map/ppermute | solution.py:40
  29.3 5.7 %collective-permute-start.13 = (bf16[256,128]{1,0:T(8,128)(2,1)S(1)}, bf16[256,128]{1,0:T(8,128)(2,1)S(1)}, u32[]{:S(2)}, u32[]{:S(2)}) collective-permute-start(bf16[256,128]{1,0:T(8,128)(2,1)S(1)} %get-tuple-element.38), channel_id=1, source_target_pairs={{0,12},{1,13},{2,14},{3,15},{4,8},{5,9},{6,10},{7,11},{8,4},{9,5},... | collective-permute-start | bytes 196616 | tf_op jit(solution)/shard_map/ppermute | solution.py:40
  29.5 7.0 %collective-permute-start.7 = (bf16[256,128]{1,0:T(8,128)(2,1)S(1)}, bf16[256,128]{1,0:T(8,128)(2,1)S(1)}, u32[]{:S(2)}, u32[]{:S(2)}) collective-permute-start(bf16[256,128]{1,0:T(8,128)(2,1)S(1)} %get-tuple-element.31), channel_id=1, source_target_pairs={{0,28},{1,29},{2,30},{3,31},{4,24},{5,25},{6,26},{7,27},{8,20},{9,... | collective-permute-start | bytes 196616 | tf_op jit(solution)/shard_map/ppermute | solution.py:40

commit v6 on v5

v6 whole, which is shorter than its diff:
```python
import functools

import jax
import jax.numpy as jnp
from jax import lax
from jax.experimental import pallas as pl
from jax.experimental.pallas import tpu as pltpu
from jax.sharding import PartitionSpec as P

GROUP = 16
BLOCK = 128
LAGS = 8
LANES = 128
TILE = 16
SIDE = LANES // GROUP
GATHER = ((6, 2, 4, 3, 5, 1, 7), (6, 2, 4, 3, 5, 1, 7))
RETURN = ((4, 1, 5, 2, 6, 3, 7), (4, 1, 5, 2, 6, 3, 7))
CHUNKS = 2
EARLY = 7
AHEAD = 2
FIRST = 7
SMALL = pltpu.CompilerParams(vmem_limit_bytes=16 * 1024 * 1024)


def place():
    return lax.axis_index("ctx") % LAGS


def partners(orders):
    core = lax.axis_index("ch") % 2
    return [place()] + [place() ^ jnp.where(core == 0, first, second) for first, second in zip(*orders)]


def exchange(blocks, orders):
    size = lax.axis_size("ch")
    devices = range(lax.axis_size("ctx") * size)
    got = [blocks[0]]
    for block, steps in zip(blocks[1:], zip(*orders)):
        pairs = [(one, (one // size ^ steps[one % size % 2]) * size + one % size) for one in devices]
        got.append(lax.ppermute(block, ("ctx", "ch"), pairs))
    return got


def mix_kernel(key_hbm, value_hbm, taps_hbm, *refs):
    sent_refs, (mixed_ref, key_ref, value_ref, taps_ref, turned_ref, arrived) = refs[:LAGS], refs[LAGS:]
    halves = sent_refs[0].shape[0] // BLOCK
    width = halves * LANES
    taps_copy = pltpu.make_async_copy(taps_hbm, taps_ref, arrived.at[4])
    taps_copy.start()
    copies = []
    for index, first in enumerate((place() & 4 ^ 4, place() & 4)):
        columns = pl.ds(pl.multiple_of(first * width, width), 4 * width)
        pair = [
            pltpu.make_async_copy(key_hbm.at[:, columns], key_ref.at[:, columns], arrived.at[2 * index]),
            pltpu.make_async_copy(value_hbm.at[:, columns], value_ref.at[:, columns], arrived.at[2 * index + 1]),
        ]
        for copy in pair:
            copy.start()
        copies.append(pair)
    taps_copy.wait()
    turned_ref[...] = taps_ref[...].T
    parts = list(zip(partners(GATHER), sent_refs))
    for partner, sent_ref in parts:
        first = pl.multiple_of(partner * TILE, TILE)
        sent_ref[width : width + TILE, :] = turned_ref[pl.ds(first, TILE), :]
    steps = (0,) + GATHER[0]
    for pair, here in zip(copies, (True, False)):
        for copy in pair:
            copy.wait()
        for step, (partner, sent_ref) in zip(steps, parts):
            if (step >= 4) != here:
                continue
            for half in range(halves):
                columns = pl.ds(pl.multiple_of((partner * halves + half) * LANES, LANES), LANES)
                mixed = (
                    key_ref[:, columns].astype(jnp.float32) * value_ref[:, columns].astype(jnp.float32)
                ).astype(jnp.bfloat16)
                mixed_ref[:, columns] = mixed
                sent_ref[half * BLOCK : (half + 1) * BLOCK, :] = mixed.T


def circulant(row):
    return pltpu.roll(jnp.broadcast_to(row, (BLOCK, LANES)), 0, 1, stride=1, stride_axis=0).astype(jnp.bfloat16)


def early_kernel(*refs):
    *got_refs, circulants, blocks, taps = refs
    width = blocks.shape[1]
    for index, (partner, got_ref) in enumerate(zip(partners(GATHER), got_refs)):
        taps[index] = got_ref[width : width + TILE, :].astype(jnp.float32)
        blocks[partner] = got_ref[0:width, :]

    @pl.loop(0, TILE, unroll=8)
    def _(group):
        for index, partner in enumerate(partners(GATHER)[:EARLY]):
            circulants[partner, group] = circulant(taps[index, pl.ds(group, 1), :])


def conv_kernel(sources, *refs):
    late_ref, *earlier_refs = refs[: 1 + (sources - 1) * LAGS]
    *conv_refs, circulants, blocks, taps, results, earlier = refs[1 + (sources - 1) * LAGS + 2 :]
    width = blocks.shape[1]
    late = partners(GATHER)[EARLY]
    taps[...] = late_ref[width : width + TILE, :].astype(jnp.float32)
    blocks[late] = late_ref[0:width, :]
    for partner, earlier_ref in zip(partners(GATHER), earlier_refs):
        earlier[partner] = earlier_ref[0:width, :]

    def add_late(group):
        circulants[late, group] = circulant(taps[group : group + 1, :])

    for group in range(AHEAD):
        add_late(group)
    causal = lax.broadcasted_iota(jnp.int32, (BLOCK, LANES), 1).astype(jnp.int16) >= lax.broadcasted_iota(
        jnp.int32, (BLOCK, LANES), 0
    ).astype(jnp.int16)
    for group in range(TILE):
        if group + AHEAD < TILE:
            add_late(group + AHEAD)
        rows = slice(group * GROUP, (group + 1) * GROUP)
        before = jnp.zeros((BLOCK, LANES), jnp.bfloat16)
        filters, signals = [], []
        for lag in range(LAGS):
            turned = circulants[lag, group]
            filters.append(jnp.where(causal, turned, before))
            before = turned
            signal = [blocks[block, rows, :] for block in range(LAGS - lag)]
            if sources > 1:
                signal = [earlier[block, rows, :] for block in range(LAGS - lag, LAGS)] + signal
            elif lag:
                signal = [jnp.zeros((lag * GROUP, LANES), jnp.bfloat16)] + signal
            signals.append(jnp.concatenate(signal, axis=0))
        total = jnp.dot(
            jnp.concatenate(signals, axis=1),
            jnp.concatenate(filters, axis=0),
            preferred_element_type=jnp.float32,
        )
        results[group] = total.astype(jnp.bfloat16)
    for partner, conv_ref in zip(partners(RETURN), conv_refs):
        rows = pl.ds(pl.multiple_of(partner * GROUP, GROUP), GROUP)
        for group in range(TILE):
            conv_ref[group * GROUP : (group + 1) * GROUP, :] = results[group, rows, :]


def gate_kernel(rounds, query_ref, skip_ref, mixed_ref, *refs):
    conv_refs, (gated_hbm, gated_ref, left) = refs[: rounds.stop - rounds.start], refs[-3:]
    halves = conv_refs[0].shape[0] // BLOCK
    width = halves * LANES
    copies = []
    for index, partner in enumerate(partners(RETURN)[rounds]):
        for half in range(halves):
            columns = pl.ds(pl.multiple_of((partner * halves + half) * LANES, LANES), LANES)
            rows = slice(half * BLOCK, (half + 1) * BLOCK)
            mixed = mixed_ref[:, columns].astype(jnp.float32)
            conv = conv_refs[index][rows, :].T.astype(jnp.float32)
            summed = conv + skip_ref[:, columns] * mixed
            gated_ref[:, columns] = (query_ref[:, columns].astype(jnp.float32) * summed).astype(jnp.bfloat16)
        columns = pl.ds(pl.multiple_of(partner * width, width), width)
        copy = pltpu.make_async_copy(gated_ref.at[:, columns], gated_hbm.at[:, columns], left.at[index])
        copy.start()
        copies.append(copy)
    for copy in copies:
        copy.wait()


def per_device(query, key, value, filter_taps, skip):
    rows, channels = query.shape
    halves = channels // LAGS // LANES
    count = lax.axis_size("ctx")
    if count > LAGS:
        all_taps = lax.all_gather(filter_taps, "ctx", axis=0, tiled=True)
        first_tap = lax.axis_index("ctx") % LAGS * BLOCK
        filter_taps = lax.dynamic_slice_in_dim(all_taps, first_tap, BLOCK, axis=0)
    in_hbm = [pltpu.with_memory_space_constraint(array, pltpu.HBM) for array in (key, value, filter_taps)]
    whole = pl.BlockSpec(memory_space=pltpu.VMEM)
    *sent, mixed = pl.pallas_call(
        mix_kernel,
        out_shape=[jax.ShapeDtypeStruct((halves * BLOCK + TILE, LANES), jnp.bfloat16)] * LAGS
        + [jax.ShapeDtypeStruct(key.shape, jnp.bfloat16)],
        in_specs=[pl.BlockSpec(memory_space=pl.ANY)] * 3,
        out_specs=[whole] * (LAGS + 1),
        scratch_shapes=[
            pltpu.VMEM(key.shape, key.dtype),
            pltpu.VMEM(value.shape, value.dtype),
            pltpu.VMEM(filter_taps.shape, filter_taps.dtype),
            pltpu.VMEM((LANES, BLOCK), jnp.bfloat16),
            pltpu.SemaphoreType.DMA((5,)),
        ],
        compiler_params=SMALL,
    )(*in_hbm)
    got = exchange(sent, GATHER)
    sources = 1
    if count > LAGS:
        sources = 2
        onward = [(source, source + LAGS) for source in range(count - LAGS)]
        got = got + [lax.ppermute(block, "ctx", onward) for block in got]
    prepared = [
        jax.ShapeDtypeStruct((LAGS, TILE, BLOCK, LANES), jnp.bfloat16),
        jax.ShapeDtypeStruct((LAGS, halves * BLOCK, LANES), jnp.bfloat16),
    ]
    early = pl.pallas_call(
        early_kernel,
        out_shape=prepared,
        in_specs=[whole] * EARLY,
        out_specs=[whole] * 2,
        scratch_shapes=[pltpu.VMEM((EARLY, TILE, LANES), jnp.float32)],
        cost_estimate=pl.CostEstimate(flops=0, bytes_accessed=8 * 1024 * 1024, transcendentals=0),
        compiler_params=SMALL,
    )(*got[:EARLY])
    late = got[EARLY:]
    *conv, _, _ = pl.pallas_call(
        lambda *refs: conv_kernel(sources, *refs),
        out_shape=[jax.ShapeDtypeStruct((halves * BLOCK, LANES), jnp.bfloat16)] * LAGS + prepared,
        in_specs=[whole] * (len(late) + 2),
        out_specs=[whole] * (LAGS + 2),
        scratch_shapes=[
            pltpu.VMEM((TILE, LANES), jnp.float32),
            pltpu.VMEM((TILE, BLOCK, LANES), jnp.bfloat16),
            pltpu.VMEM((LAGS, halves * BLOCK, LANES), jnp.bfloat16),
        ],
        input_output_aliases={len(late): LAGS, len(late) + 1: LAGS + 1},
        compiler_params=SMALL,
    )(*late, *early)
    back = exchange(conv, RETURN)
    gated = None
    for rounds in (slice(0, FIRST), slice(FIRST, LAGS)):
        size = rounds.stop - rounds.start
        inputs = [query, skip.reshape(1, channels), mixed, *back[rounds]]
        specs = [whole] * len(inputs)
        if gated is not None:
            inputs.append(gated)
            specs.append(pl.BlockSpec(memory_space=pl.ANY))
        gated = pl.pallas_call(
            functools.partial(gate_kernel, rounds),
            out_shape=jax.ShapeDtypeStruct((rows, channels), jnp.bfloat16),
            in_specs=specs,
            out_specs=pl.BlockSpec(memory_space=pl.ANY),
            scratch_shapes=[pltpu.VMEM((rows, channels), jnp.bfloat16), pltpu.SemaphoreType.DMA((size,))],
            input_output_aliases={} if gated is None else {len(inputs) - 1: 0},
            compiler_params=SMALL,
        )(*inputs)
    return gated


def solution(mesh):
    placed = (P("ctx", "ch"), P("ctx", "ch"), P("ctx", "ch"), P("ctx", "ch"), P("ch"))
    return jax.shard_map(
        per_device, mesh=mesh, in_specs=placed, out_specs=P("ctx", "ch"), check_vma=False
    )
```

time: 37.4 us -> 37 us (0.989)
  waiting for transfers between devices: 7.71 us -> 7.19 us
  starting transfers between devices: 23.2 us -> 23.7 us
  Pallas kernels: 6.31 us -> 5.92 us
    ppermute x14, starting transfers between devices: 23.2 us -> 23.7 us  [exchange(): got.append(lax.ppermute(block, ('ctx', 'ch'), pairs))]
    ppermute x14, waiting for transfers between devices: 7.71 us -> 7.19 us  [exchange(): got.append(lax.ppermute(block, ('ctx', 'ch'), pairs))]
    pallas_call x1, Pallas kernels: 1.95 us -> 1.51 us  [per_device(): pl.pallas_call(lambda *refs: conv_kernel(sources, *refs), out_shape=[jax....]
where the time goes in v6:
time: 37 us; the launch traced here: 36.9 us
  starting transfers between devices  23.7 us (64%)
  waiting for transfers between devices  7.19 us (19%)
  Pallas kernels  5.92 us (16%)
    ppermute x14, starting transfers between devices, exchange(): got.append(lax.ppermute(block, ('ctx', 'ch'), pairs))  23.7 us
    ppermute x14, waiting for transfers between devices, exchange(): got.append(lax.ppermute(block, ('ctx', 'ch'), pairs))  7.19 us
    pallas_call x2, Pallas kernels, per_device(): pl.pallas_call(functools.partial(gate_kernel, rounds), out_shape=jax.Shap...  1.73 us
    pallas_call x1, Pallas kernels, per_device(): pl.pallas_call(mix_kernel, out_shape=[jax.ShapeDtypeStruct((halves * BLOC...  1.55 us
    pallas_call x1, Pallas kernels, per_device(): pl.pallas_call(lambda *refs: conv_kernel(sources, *refs), out_shape=[jax....  1.51 us
    pallas_call x1, Pallas kernels, per_device(): pl.pallas_call(early_kernel, out_shape=prepared, in_specs=[whole] * EARLY...  1.14 us
  transfers between devices with their start and end apart: 14, of which 6 were waited for; matrix products, arithmetic and copies ran while one was open for 0% of the time, Pallas kernels for 6%

profile of v6, /device:TPU:0, one launch (start us, length us, event | category | flops | bytes accessed | tf_op | source)
XLA Modules:
  0.0 36.9 jit_solution(4089686934620351554)
XLA Ops:
  0.0 0.0 copy-start
  0.0 0.0 copy-start.1
  0.0 1.5 %shard_map.55 = (bf16[272,128]{1,0:T(8,128)(2,1)S(1)}, bf16[272,128]{1,0:T(8,128)(2,1)S(1)}, bf16[272,128]{1,0:T(8,128)(2,1)S(1)}, bf16[272,128]{1,0:T(8,128)(2,...) custom-call(bf16[128,2048]{1,0:T(8,128)(2,1)} %key_hbm.1, ...), custom_call_target="tpu_custom_call" | custom-call | tf_op jit(solution)/shard_map/pallas_call | solution.py:176
  1.6 5.1 %collective-permute-start.1 = (bf16[272,128]{1,0:T(8,128)(2,1)S(1)}, bf16[272,128]{1,0:T(8,128)(2,1)S(1)}, u32[]{:S(2)}, u32[]{:S(2)}) collective-permute-start(bf16[272,128]{1,0:T(8,128)(2,1)S(1)} %get-tuple-element.27), channel_id=1, source_target_pairs={{0,24},{1,25},{2,26},{3,27},{4,28},{5,29},{6,30},{7,31},{8,16},{9,... | collective-permute-start | bytes 208904 | tf_op jit(solution)/shard_map/ppermute | solution.py:40
  6.7 0.0 collective-permute-start.2
  6.7 0.6 %collective-permute-start.3 = (bf16[272,128]{1,0:T(8,128)(2,1)S(1)}, bf16[272,128]{1,0:T(8,128)(2,1)S(1)}, u32[]{:S(2)}, u32[]{:S(2)}) collective-permute-start(bf16[272,128]{1,0:T(8,128)(2,1)S(1)} %get-tuple-element.29), channel_id=1, source_target_pairs={{0,16},{1,17},{2,18},{3,19},{4,20},{5,21},{6,22},{7,23},{8,24},{9,... | collective-permute-start | bytes 208904 | tf_op jit(solution)/shard_map/ppermute | solution.py:40
  7.3 2.3 %collective-permute-start.4 = (bf16[272,128]{1,0:T(8,128)(2,1)S(1)}, bf16[272,128]{1,0:T(8,128)(2,1)S(1)}, u32[]{:S(2)}, u32[]{:S(2)}) collective-permute-start(bf16[272,128]{1,0:T(8,128)(2,1)S(1)} %get-tuple-element.30), channel_id=1, source_target_pairs={{0,12},{1,13},{2,14},{3,15},{4,8},{5,9},{6,10},{7,11},{8,4},{9,5},... | collective-permute-start | bytes 208904 | tf_op jit(solution)/shard_map/ppermute | solution.py:40
  9.6 2.9 %collective-permute-start.5 = (bf16[272,128]{1,0:T(8,128)(2,1)S(1)}, bf16[272,128]{1,0:T(8,128)(2,1)S(1)}, u32[]{:S(2)}, u32[]{:S(2)}) collective-permute-start(bf16[272,128]{1,0:T(8,128)(2,1)S(1)} %get-tuple-element.31), channel_id=1, source_target_pairs={{0,20},{1,21},{2,22},{3,23},{4,16},{5,17},{6,18},{7,19},{8,28},{9,... | collective-permute-start | bytes 208904 | tf_op jit(solution)/shard_map/ppermute | solution.py:40
  12.5 0.0 collective-permute-done.1.refs_1_
  12.5 1.5 %collective-permute-start.6 = (bf16[272,128]{1,0:T(8,128)(2,1)S(1)}, bf16[272,128]{1,0:T(8,128)(2,1)S(1)}, u32[]{:S(2)}, u32[]{:S(2)}) collective-permute-start(bf16[272,128]{1,0:T(8,128)(2,1)S(1)} %get-tuple-element.32), channel_id=1, source_target_pairs={{0,4},{1,5},{2,6},{3,7},{4,0},{5,1},{6,2},{7,3},{8,12},{9,13},{10,... | collective-permute-start | bytes 208904 | tf_op jit(solution)/shard_map/ppermute | solution.py:40
  14.0 0.0 collective-permute-done.2.refs_2_
  14.0 1.0 %collective-permute-start = (bf16[272,128]{1,0:T(8,128)(2,1)S(1)}, bf16[272,128]{1,0:T(8,128)(2,1)S(1)}, u32[]{:S(2)}, u32[]{:S(2)}) collective-permute-start(bf16[272,128]{1,0:T(8,128)(2,1)S(1)} %get-tuple-element.25), channel_id=1, source_target_pairs={{0,28},{1,29},{2,30},{3,31},{4,24},{5,25},{6,26},{7,27},{8,20},{9,... | collective-permute-start | bytes 208904 | tf_op jit(solution)/shard_map/ppermute | solution.py:40
  15.0 0.0 collective-permute-done.3.refs_3_
  15.0 0.0 collective-permute-done.4.refs_4_
  15.0 2.4 %collective-permute-done.5.refs_5_ = bf16[272,128]{1,0:T(8,128)(2,1)S(1)} collective-permute-done((bf16[272,128]{1,0:T(8,128)(2,1)S(1)}, bf16[272,128]{1,0:T(8,128)(2,1)S(1)}, u32[]{:S(2)}, u32[]{:S(2)}) %collective-permute-start.5) | collective-permute-done | bytes 69664 | tf_op jit(solution)/shard_map/ppermute | solution.py:40
  17.4 0.2 collective-permute-done.6.refs_6_
  17.5 1.1 %shard_map.56 = (bf16[8,16,128,128]{3,2,1,0:T(8,128)(2,1)S(1)}, bf16[8,256,128]{2,1,0:T(8,128)(2,1)S(1)}) custom-call(bf16[272,128]{1,0:T(8,128)(2,1)S(1)} %get-tuple-element.26.refs_0_, bf16[272,128]{1,0:T(8,128)(2,1)S(1)} %collective-permute-done.1.refs_1_, bf16[272,128]{1,0:T(8,128)(2,1)S(1)} %collective-permute-done.2.refs_2_, ...), custom_call_target="tpu_custom_call" | custom-call | bytes 8388608 | tf_op jit(solution)/shard_map/pallas_call | solution.py:201
  18.7 2.4 %collective-permute-done.refs_0_ = bf16[272,128]{1,0:T(8,128)(2,1)S(1)} collective-permute-done((bf16[272,128]{1,0:T(8,128)(2,1)S(1)}, bf16[272,128]{1,0:T(8,128)(2,1)S(1)}, u32[]{:S(2)}, u32[]{:S(2)}) %collective-permute-start) | collective-permute-done | bytes 69664 | tf_op jit(solution)/shard_map/ppermute | solution.py:40
  21.0 1.5 %shard_map.57 = (bf16[256,128]{1,0:T(8,128)(2,1)S(1)}, bf16[256,128]{1,0:T(8,128)(2,1)S(1)}, bf16[256,128]{1,0:T(8,128)(2,1)S(1)}, bf16[256,128]{1,0:T(8,128)(2,...) custom-call(bf16[272,128]{1,0:T(8,128)(2,1)S(1)} %collective-permute, ...), custom_call_target="tpu_custom_call", output_to_operand_aliasing={{8}: (1, {}), {9}: (2, {})} | custom-call | tf_op jit(solution)/shard_map/pallas_call | solution.py:211
  22.5 0.5 %collective-permute-start.8 = (bf16[256,128]{1,0:T(8,128)(2,1)S(1)}, bf16[256,128]{1,0:T(8,128)(2,1)S(1)}, u32[]{:S(2)}, u32[]{:S(2)}) collective-permute-start(bf16[256,128]{1,0:T(8,128)(2,1)S(1)} %get-tuple-element.37), channel_id=1, source_target_pairs={{0,16},{1,17},{2,18},{3,19},{4,20},{5,21},{6,22},{7,23},{8,24},{9,... | collective-permute-start | bytes 196616 | tf_op jit(solution)/shard_map/ppermute | solution.py:40
  23.0 0.5 %collective-permute-start.9 = (bf16[256,128]{1,0:T(8,128)(2,1)S(1)}, bf16[256,128]{1,0:T(8,128)(2,1)S(1)}, u32[]{:S(2)}, u32[]{:S(2)}) collective-permute-start(bf16[256,128]{1,0:T(8,128)(2,1)S(1)} %get-tuple-element.38), channel_id=1, source_target_pairs={{0,4},{1,5},{2,6},{3,7},{4,0},{5,1},{6,2},{7,3},{8,12},{9,13},{10,... | collective-permute-start | bytes 196616 | tf_op jit(solution)/shard_map/ppermute | solution.py:40
  23.5 3.5 %collective-permute-start.10 = (bf16[256,128]{1,0:T(8,128)(2,1)S(1)}, bf16[256,128]{1,0:T(8,128)(2,1)S(1)}, u32[]{:S(2)}, u32[]{:S(2)}) collective-permute-start(bf16[256,128]{1,0:T(8,128)(2,1)S(1)} %get-tuple-element.39), channel_id=1, source_target_pairs={{0,20},{1,21},{2,22},{3,23},{4,16},{5,17},{6,18},{7,19},{8,28},{9,... | collective-permute-start | bytes 196616 | tf_op jit(solution)/shard_map/ppermute | solution.py:40
  27.0 0.0 collective-permute-start.11
  27.0 1.9 %collective-permute-start.12 = (bf16[256,128]{1,0:T(8,128)(2,1)S(1)}, bf16[256,128]{1,0:T(8,128)(2,1)S(1)}, u32[]{:S(2)}, u32[]{:S(2)}) collective-permute-start(bf16[256,128]{1,0:T(8,128)(2,1)S(1)} %get-tuple-element.41), channel_id=1, source_target_pairs={{0,24},{1,25},{2,26},{3,27},{4,28},{5,29},{6,30},{7,31},{8,16},{9,... | collective-permute-start | bytes 196616 | tf_op jit(solution)/shard_map/ppermute | solution.py:40
  28.9 0.0 collective-permute-done.8.refs_1_
  28.9 0.4 collective-permute-start.13
  29.2 0.0 collective-permute-done.9.refs_2_
  29.2 3.6 %collective-permute-start.7 = (bf16[256,128]{1,0:T(8,128)(2,1)S(1)}, bf16[256,128]{1,0:T(8,128)(2,1)S(1)}, u32[]{:S(2)}, u32[]{:S(2)}) collective-permute-start(bf16[256,128]{1,0:T(8,128)(2,1)S(1)} %get-tuple-element.35), channel_id=1, source_target_pairs={{0,28},{1,29},{2,30},{3,31},{4,24},{5,25},{6,26},{7,27},{8,20},{9,... | collective-permute-start | bytes 196616 | tf_op jit(solution)/shard_map/ppermute | solution.py:40
  32.9 0.0 collective-permute-done.10.refs_3_
  32.9 0.0 collective-permute-done.11.refs_4_
  32.9 0.4 %collective-permute-done.12.refs_5_ = bf16[256,128]{1,0:T(8,128)(2,1)S(1)} collective-permute-done((bf16[256,128]{1,0:T(8,128)(2,1)S(1)}, bf16[256,128]{1,0:T(8,128)(2,1)S(1)}, u32[]{:S(2)}, u32[]{:S(2)}) %collective-permute-start.12) | collective-permute-done | bytes 65568 | tf_op jit(solution)/shard_map/ppermute | solution.py:40
  33.3 0.8 %collective-permute-done.13.refs_6_ = bf16[256,128]{1,0:T(8,128)(2,1)S(1)} collective-permute-done((bf16[256,128]{1,0:T(8,128)(2,1)S(1)}, bf16[256,128]{1,0:T(8,128)(2,1)S(1)}, u32[]{:S(2)}, u32[]{:S(2)}) %collective-permute-start.13) | collective-permute-done | bytes 65568 | tf_op jit(solution)/shard_map/ppermute | solution.py:40
  34.0 0.0 copy-done
  34.0 0.0 copy-done.1
  34.0 1.0 %shard_map.58.refs_1_ = bf16[128,2048]{1,0:T(8,128)(2,1)} custom-call(bf16[128,2048]{1,0:T(8,128)(2,1)S(1)} %copy-done, f32[1,2048]{1,0:T(1,128)S(1)} %bitcast.1, bf16[128,2048]{1,0:T(8,128)(2,1)S(1)} %get-tuple-element.24.mixed_ref, bf16[256,128]{1,0:T(8,128)(2,1)S(1)} %get-tuple-element.36.refs_0_, bf16[256,128]{1,0:T(8,128)(2,1)S(1)} %collective-permute-done.8.refs_1_, ...), custom_call_target="tpu_custom_call" | custom-call | tf_op jit(solution)/shard_map/pallas_call | solution.py:233
  35.1 1.1 %collective-permute-done.7.refs_0_ = bf16[256,128]{1,0:T(8,128)(2,1)S(1)} collective-permute-done((bf16[256,128]{1,0:T(8,128)(2,1)S(1)}, bf16[256,128]{1,0:T(8,128)(2,1)S(1)}, u32[]{:S(2)}, u32[]{:S(2)}) %collective-permute-start.7) | collective-permute-done | bytes 65568 | tf_op jit(solution)/shard_map/ppermute | solution.py:40
  36.2 0.7 %shard_map.59 = bf16[128,2048]{1,0:T(8,128)(2,1)} custom-call(bf16[128,2048]{1,0:T(8,128)(2,1)S(1)} %copy-done, f32[1,2048]{1,0:T(1,128)S(1)} %bitcast.2, bf16[128,2048]{1,0:T(8,128)(2,1)S(1)} %get-tuple-element.24.mixed_ref, bf16[256,128]{1,0:T(8,128)(2,1)S(1)} %collective-permute-done.7.refs_0_, ...), custom_call_target="tpu_custom_call", output_to_operand_aliasing={{}: (4, {})} | custom-call | tf_op jit(solution)/shard_map/pallas_call | solution.py:233
Async XLA Ops:
  0.0 34.0 %copy-start = (bf16[128,2048]{1,0:T(8,128)(2,1)S(1)}, bf16[128,2048]{1,0:T(8,128)(2,1)}, u32[]{:S(2)}) copy-start(bf16[128,2048]{1,0:T(8,128)(2,1)} %query_ref.3) | copy-start | bytes 1572868
  0.0 34.0 %copy-start.1 = (f32[2048]{0:T(1024)S(1)}, f32[2048]{0:T(1024)}, u32[]{:S(2)}) copy-start(f32[2048]{0:T(1024)} %param.9) | copy-start | bytes 24580
  1.6 11.0 %collective-permute-start.1 = (bf16[272,128]{1,0:T(8,128)(2,1)S(1)}, bf16[272,128]{1,0:T(8,128)(2,1)S(1)}, u32[]{:S(2)}, u32[]{:S(2)}) collective-permute-start(bf16[272,128]{1,0:T(8,128)(2,1)S(1)} %get-tuple-element.27), channel_id=1, source_target_pairs={{0,24},{1,25},{2,26},{3,27},{4,28},{5,29},{6,30},{7,31},{8,16},{9,... | collective-permute-start | bytes 208904 | tf_op jit(solution)/shard_map/ppermute | solution.py:40
  6.7 7.3 %collective-permute-start.2 = (bf16[272,128]{1,0:T(8,128)(2,1)S(1)}, bf16[272,128]{1,0:T(8,128)(2,1)S(1)}, u32[]{:S(2)}, u32[]{:S(2)}) collective-permute-start(bf16[272,128]{1,0:T(8,128)(2,1)S(1)} %get-tuple-element.28), channel_id=1, source_target_pairs={{0,8},{1,9},{2,10},{3,11},{4,12},{5,13},{6,14},{7,15},{8,0},{9,1},... | collective-permute-start | bytes 208904 | tf_op jit(solution)/shard_map/ppermute | solution.py:40
  6.7 8.3 %collective-permute-start.3 = (bf16[272,128]{1,0:T(8,128)(2,1)S(1)}, bf16[272,128]{1,0:T(8,128)(2,1)S(1)}, u32[]{:S(2)}, u32[]{:S(2)}) collective-permute-start(bf16[272,128]{1,0:T(8,128)(2,1)S(1)} %get-tuple-element.29), channel_id=1, source_target_pairs={{0,16},{1,17},{2,18},{3,19},{4,20},{5,21},{6,22},{7,23},{8,24},{9,... | collective-permute-start | bytes 208904 | tf_op jit(solution)/shard_map/ppermute | solution.py:40
  7.3 7.7 %collective-permute-start.4 = (bf16[272,128]{1,0:T(8,128)(2,1)S(1)}, bf16[272,128]{1,0:T(8,128)(2,1)S(1)}, u32[]{:S(2)}, u32[]{:S(2)}) collective-permute-start(bf16[272,128]{1,0:T(8,128)(2,1)S(1)} %get-tuple-element.30), channel_id=1, source_target_pairs={{0,12},{1,13},{2,14},{3,15},{4,8},{5,9},{6,10},{7,11},{8,4},{9,5},... | collective-permute-start | bytes 208904 | tf_op jit(solution)/shard_map/ppermute | solution.py:40
  9.6 7.7 %collective-permute-start.5 = (bf16[272,128]{1,0:T(8,128)(2,1)S(1)}, bf16[272,128]{1,0:T(8,128)(2,1)S(1)}, u32[]{:S(2)}, u32[]{:S(2)}) collective-permute-start(bf16[272,128]{1,0:T(8,128)(2,1)S(1)} %get-tuple-element.31), channel_id=1, source_target_pairs={{0,20},{1,21},{2,22},{3,23},{4,16},{5,17},{6,18},{7,19},{8,28},{9,... | collective-permute-start | bytes 208904 | tf_op jit(solution)/shard_map/ppermute | solution.py:40
  12.5 5.0 %collective-permute-start.6 = (bf16[272,128]{1,0:T(8,128)(2,1)S(1)}, bf16[272,128]{1,0:T(8,128)(2,1)S(1)}, u32[]{:S(2)}, u32[]{:S(2)}) collective-permute-start(bf16[272,128]{1,0:T(8,128)(2,1)S(1)} %get-tuple-element.32), channel_id=1, source_target_pairs={{0,4},{1,5},{2,6},{3,7},{4,0},{5,1},{6,2},{7,3},{8,12},{9,13},{10,... | collective-permute-start | bytes 208904 | tf_op jit(solution)/shard_map/ppermute | solution.py:40
  14.0 7.0 %collective-permute-start = (bf16[272,128]{1,0:T(8,128)(2,1)S(1)}, bf16[272,128]{1,0:T(8,128)(2,1)S(1)}, u32[]{:S(2)}, u32[]{:S(2)}) collective-permute-start(bf16[272,128]{1,0:T(8,128)(2,1)S(1)} %get-tuple-element.25), channel_id=1, source_target_pairs={{0,28},{1,29},{2,30},{3,31},{4,24},{5,25},{6,26},{7,27},{8,20},{9,... | collective-permute-start | bytes 208904 | tf_op jit(solution)/shard_map/ppermute | solution.py:40
  22.5 6.3 %collective-permute-start.8 = (bf16[256,128]{1,0:T(8,128)(2,1)S(1)}, bf16[256,128]{1,0:T(8,128)(2,1)S(1)}, u32[]{:S(2)}, u32[]{:S(2)}) collective-permute-start(bf16[256,128]{1,0:T(8,128)(2,1)S(1)} %get-tuple-element.37), channel_id=1, source_target_pairs={{0,16},{1,17},{2,18},{3,19},{4,20},{5,21},{6,22},{7,23},{8,24},{9,... | collective-permute-start | bytes 196616 | tf_op jit(solution)/shard_map/ppermute | solution.py:40
  23.0 6.2 %collective-permute-start.9 = (bf16[256,128]{1,0:T(8,128)(2,1)S(1)}, bf16[256,128]{1,0:T(8,128)(2,1)S(1)}, u32[]{:S(2)}, u32[]{:S(2)}) collective-permute-start(bf16[256,128]{1,0:T(8,128)(2,1)S(1)} %get-tuple-element.38), channel_id=1, source_target_pairs={{0,4},{1,5},{2,6},{3,7},{4,0},{5,1},{6,2},{7,3},{8,12},{9,13},{10,... | collective-permute-start | bytes 196616 | tf_op jit(solution)/shard_map/ppermute | solution.py:40
  23.5 9.3 %collective-permute-start.10 = (bf16[256,128]{1,0:T(8,128)(2,1)S(1)}, bf16[256,128]{1,0:T(8,128)(2,1)S(1)}, u32[]{:S(2)}, u32[]{:S(2)}) collective-permute-start(bf16[256,128]{1,0:T(8,128)(2,1)S(1)} %get-tuple-element.39), channel_id=1, source_target_pairs={{0,20},{1,21},{2,22},{3,23},{4,16},{5,17},{6,18},{7,19},{8,28},{9,... | collective-permute-start | bytes 196616 | tf_op jit(solution)/shard_map/ppermute | solution.py:40
  27.0 5.9 %collective-permute-start.11 = (bf16[256,128]{1,0:T(8,128)(2,1)S(1)}, bf16[256,128]{1,0:T(8,128)(2,1)S(1)}, u32[]{:S(2)}, u32[]{:S(2)}) collective-permute-start(bf16[256,128]{1,0:T(8,128)(2,1)S(1)} %get-tuple-element.40), channel_id=1, source_target_pairs={{0,8},{1,9},{2,10},{3,11},{4,12},{5,13},{6,14},{7,15},{8,0},{9,1},... | collective-permute-start | bytes 196616 | tf_op jit(solution)/shard_map/ppermute | solution.py:40
  27.0 6.3 %collective-permute-start.12 = (bf16[256,128]{1,0:T(8,128)(2,1)S(1)}, bf16[256,128]{1,0:T(8,128)(2,1)S(1)}, u32[]{:S(2)}, u32[]{:S(2)}) collective-permute-start(bf16[256,128]{1,0:T(8,128)(2,1)S(1)} %get-tuple-element.41), channel_id=1, source_target_pairs={{0,24},{1,25},{2,26},{3,27},{4,28},{5,29},{6,30},{7,31},{8,16},{9,... | collective-permute-start | bytes 196616 | tf_op jit(solution)/shard_map/ppermute | solution.py:40
  28.9 5.2 %collective-permute-start.13 = (bf16[256,128]{1,0:T(8,128)(2,1)S(1)}, bf16[256,128]{1,0:T(8,128)(2,1)S(1)}, u32[]{:S(2)}, u32[]{:S(2)}) collective-permute-start(bf16[256,128]{1,0:T(8,128)(2,1)S(1)} %get-tuple-element.42), channel_id=1, source_target_pairs={{0,12},{1,13},{2,14},{3,15},{4,8},{5,9},{6,10},{7,11},{8,4},{9,5},... | collective-permute-start | bytes 196616 | tf_op jit(solution)/shard_map/ppermute | solution.py:40
  29.2 7.0 %collective-permute-start.7 = (bf16[256,128]{1,0:T(8,128)(2,1)S(1)}, bf16[256,128]{1,0:T(8,128)(2,1)S(1)}, u32[]{:S(2)}, u32[]{:S(2)}) collective-permute-start(bf16[256,128]{1,0:T(8,128)(2,1)S(1)} %get-tuple-element.35), channel_id=1, source_target_pairs={{0,28},{1,29},{2,30},{3,31},{4,24},{5,25},{6,26},{7,27},{8,20},{9,... | collective-permute-start | bytes 196616 | tf_op jit(solution)/shard_map/ppermute | solution.py:40

commit v7 on v6

--- a/solution.py
+++ b/solution.py
@@ -13,11 +13,12 @@
 LANES = 128
 TILE = 16
 SIDE = LANES // GROUP
-GATHER = ((6, 2, 4, 3, 5, 1, 7), (6, 2, 4, 3, 5, 1, 7))
+GATHER = ((6, 1, 4, 2, 5, 3, 7), (6, 1, 4, 2, 5, 3, 7))
 RETURN = ((4, 1, 5, 2, 6, 3, 7), (4, 1, 5, 2, 6, 3, 7))
 CHUNKS = 2
 EARLY = 7
 AHEAD = 2
+UNROLL = 8
 FIRST = 7
 SMALL = pltpu.CompilerParams(vmem_limit_bytes=16 * 1024 * 1024)
 
@@ -41,8 +42,15 @@
     return got
 
 
+def later_lanes():
+    lane = lax.broadcasted_iota(jnp.int32, (BLOCK, LANES), 1)
+    row = lax.broadcasted_iota(jnp.int32, (BLOCK, LANES), 0)
+    return lane.astype(jnp.int16) >= row.astype(jnp.int16)
+
+
 def mix_kernel(key_hbm, value_hbm, taps_hbm, *refs):
-    sent_refs, (mixed_ref, key_ref, value_ref, taps_ref, turned_ref, arrived) = refs[:LAGS], refs[LAGS:]
+    sent_refs, refs = refs[:LAGS], refs[LAGS:]
+    mixed_ref, home_ref, key_ref, value_ref, taps_ref, turned_ref, home_taps, arrived = refs
     halves = sent_refs[0].shape[0] // BLOCK
     width = halves * LANES
     taps_copy = pltpu.make_async_copy(taps_hbm, taps_ref, arrived.at[4])
@@ -78,6 +86,30 @@
                 mixed_ref[:, columns] = mixed
                 sent_ref[half * BLOCK : (half + 1) * BLOCK, :] = mixed.T
 
+    @pl.when(lax.axis_index("ctx") == 0)
+    def _():
+        home_taps[...] = turned_ref[...].astype(jnp.float32)
+        causal = later_lanes()
+        for partner, sent_ref in parts:
+
+            @pl.loop(0, TILE // 2, unroll=UNROLL)
+            def _(pair):
+                first = partner * TILE + 2 * pair
+                rows = [circulant(home_taps[pl.ds(first + index, 1), :]) for index in range(2)]
+                filters = [jnp.where(causal, row, jnp.zeros_like(row)) for row in rows]
+                both = sent_ref[pl.ds(pl.multiple_of(2 * pair * GROUP, 2 * GROUP), 2 * GROUP), :]
+                nothing = jnp.zeros((GROUP, LANES), jnp.bfloat16)
+                signal = jnp.concatenate(
+                    [
+                        jnp.concatenate([both[0:GROUP], nothing], axis=0),
+                        jnp.concatenate([nothing, both[GROUP : 2 * GROUP]], axis=0),
+                    ],
+                    axis=1,
+                )
+                total = jnp.dot(signal, jnp.concatenate(filters, axis=0), preferred_element_type=jnp.float32)
+                there = pl.ds(pl.multiple_of(first * GROUP, 2 * GROUP), 2 * GROUP)
+                home_ref[there, :] = total.astype(jnp.bfloat16)
+
 
 def circulant(row):
     return pltpu.roll(jnp.broadcast_to(row, (BLOCK, LANES)), 0, 1, stride=1, stride_axis=0).astype(jnp.bfloat16)
@@ -111,9 +143,7 @@
 
     for group in range(AHEAD):
         add_late(group)
-    causal = lax.broadcasted_iota(jnp.int32, (BLOCK, LANES), 1).astype(jnp.int16) >= lax.broadcasted_iota(
-        jnp.int32, (BLOCK, LANES), 0
-    ).astype(jnp.int16)
+    causal = later_lanes()
     for group in range(TILE):
         if group + AHEAD < TILE:
             add_late(group + AHEAD)
@@ -142,25 +172,39 @@
             conv_ref[group * GROUP : (group + 1) * GROUP, :] = results[group, rows, :]
 
 
-def gate_kernel(rounds, query_ref, skip_ref, mixed_ref, *refs):
-    conv_refs, (gated_hbm, gated_ref, left) = refs[: rounds.stop - rounds.start], refs[-3:]
-    halves = conv_refs[0].shape[0] // BLOCK
-    width = halves * LANES
+def gate_parts(numbers, convs, query_ref, skip_ref, mixed_ref, gated_hbm, gated_ref, left):
     copies = []
-    for index, partner in enumerate(partners(RETURN)[rounds]):
+    for index, (number, conv_ref) in enumerate(zip(numbers, convs)):
+        halves = conv_ref.shape[0] // BLOCK
         for half in range(halves):
-            columns = pl.ds(pl.multiple_of((partner * halves + half) * LANES, LANES), LANES)
-            rows = slice(half * BLOCK, (half + 1) * BLOCK)
+            columns = pl.ds(pl.multiple_of((number * halves + half) * LANES, LANES), LANES)
             mixed = mixed_ref[:, columns].astype(jnp.float32)
-            conv = conv_refs[index][rows, :].T.astype(jnp.float32)
+            conv = conv_ref[half * BLOCK : (half + 1) * BLOCK, :].T.astype(jnp.float32)
             summed = conv + skip_ref[:, columns] * mixed
             gated_ref[:, columns] = (query_ref[:, columns].astype(jnp.float32) * summed).astype(jnp.bfloat16)
-        columns = pl.ds(pl.multiple_of(partner * width, width), width)
+        columns = pl.ds(pl.multiple_of(number * halves * LANES, halves * LANES), halves * LANES)
         copy = pltpu.make_async_copy(gated_ref.at[:, columns], gated_hbm.at[:, columns], left.at[index])
         copy.start()
         copies.append(copy)
     for copy in copies:
         copy.wait()
+
+
+def gate_kernel(rounds, query_ref, skip_ref, mixed_ref, home_ref, *refs):
+    conv_refs, (gated_hbm, gated_ref, left) = refs[: rounds.stop - rounds.start], refs[-3:]
+    common = (query_ref, skip_ref, mixed_ref, gated_hbm, gated_ref, left)
+    at_home = lax.axis_index("ctx") == 0
+
+    @pl.when(jnp.logical_not(at_home))
+    def _():
+        gate_parts(partners(RETURN)[rounds], conv_refs, *common)
+
+    if rounds.start == 0:
+
+        @pl.when(at_home)
+        def _():
+            width = home_ref.shape[0] // LAGS
+            gate_parts(range(LAGS), [home_ref.at[part * width : (part + 1) * width] for part in range(LAGS)], *common)
 
 
 def per_device(query, key, value, filter_taps, skip):
@@ -173,17 +217,18 @@
         filter_taps = lax.dynamic_slice_in_dim(all_taps, first_tap, BLOCK, axis=0)
     in_hbm = [pltpu.with_memory_space_constraint(array, pltpu.HBM) for array in (key, value, filter_taps)]
     whole = pl.BlockSpec(memory_space=pltpu.VMEM)
-    *sent, mixed = pl.pallas_call(
+    *sent, mixed, home = pl.pallas_call(
         mix_kernel,
         out_shape=[jax.ShapeDtypeStruct((halves * BLOCK + TILE, LANES), jnp.bfloat16)] * LAGS
-        + [jax.ShapeDtypeStruct(key.shape, jnp.bfloat16)],
+        + [jax.ShapeDtypeStruct(key.shape, jnp.bfloat16), jax.ShapeDtypeStruct((channels, rows), jnp.bfloat16)],
         in_specs=[pl.BlockSpec(memory_space=pl.ANY)] * 3,
-        out_specs=[whole] * (LAGS + 1),
+        out_specs=[whole] * (LAGS + 2),
         scratch_shapes=[
             pltpu.VMEM(key.shape, key.dtype),
             pltpu.VMEM(value.shape, value.dtype),
             pltpu.VMEM(filter_taps.shape, filter_taps.dtype),
             pltpu.VMEM((LANES, BLOCK), jnp.bfloat16),
+            pltpu.VMEM((LANES, BLOCK), jnp.float32),
             pltpu.SemaphoreType.DMA((5,)),
         ],
         compiler_params=SMALL,
@@ -224,8 +269,7 @@
     back = exchange(conv, RETURN)
     gated = None
     for rounds in (slice(0, FIRST), slice(FIRST, LAGS)):
-        size = rounds.stop - rounds.start
-        inputs = [query, skip.reshape(1, channels), mixed, *back[rounds]]
+        inputs = [query, skip.reshape(1, channels), mixed, home, *back[rounds]]
         specs = [whole] * len(inputs)
         if gated is not None:
             inputs.append(gated)
@@ -235,7 +279,7 @@
             out_shape=jax.ShapeDtypeStruct((rows, channels), jnp.bfloat16),
             in_specs=specs,
             out_specs=pl.BlockSpec(memory_space=pl.ANY),
-            scratch_shapes=[pltpu.VMEM((rows, channels), jnp.bfloat16), pltpu.SemaphoreType.DMA((size,))],
+            scratch_shapes=[pltpu.VMEM((rows, channels), jnp.bfloat16), pltpu.SemaphoreType.DMA((LAGS,))],
             input_output_aliases={} if gated is None else {len(inputs) - 1: 0},
             compiler_params=SMALL,
         )(*inputs)

time: 37 us -> 36.4 us (0.984)
  starting transfers between devices: 23.7 us -> 21.5 us
  waiting for transfers between devices: 7.19 us -> 8.14 us
  Pallas kernels: 5.92 us -> 6.54 us
    ppermute x14, starting transfers between devices: 23.7 us -> 21.5 us  [exchange(): got.append(lax.ppermute(block, ('ctx', 'ch'), pairs))]
    pallas_call x1, Pallas kernels: 1.55 us -> 2.84 us  [per_device(): pl.pallas_call(mix_kernel, out_shape=[jax.ShapeDtypeStruct((halves * BLOC...]
    ppermute x14, waiting for transfers between devices: 7.19 us -> 8.14 us  [exchange(): got.append(lax.ppermute(block, ('ctx', 'ch'), pairs))]
    pallas_call x2, Pallas kernels: 1.73 us -> 1.05 us  [per_device(): pl.pallas_call(functools.partial(gate_kernel, rounds), out_shape=jax.Shap...]
  transfers between devices with their start and end apart: 14 -> 14, of which waited for: 6 -> 7; matrix products, arithmetic and copies ran while one was open for 0% -> 0% of each run, Pallas kernels for 6% -> 6%
where the time goes in v7:
time: 36.4 us; the launch traced here: 36.3 us
  starting transfers between devices  21.5 us (59%)
  waiting for transfers between devices  8.14 us (22%)
  Pallas kernels  6.54 us (18%)
    ppermute x14, starting transfers between devices, exchange(): got.append(lax.ppermute(block, ('ctx', 'ch'), pairs))  21.5 us
    ppermute x14, waiting for transfers between devices, exchange(): got.append(lax.ppermute(block, ('ctx', 'ch'), pairs))  8.14 us
    pallas_call x1, Pallas kernels, per_device(): pl.pallas_call(mix_kernel, out_shape=[jax.ShapeDtypeStruct((halves * BLOC...  2.84 us
    pallas_call x1, Pallas kernels, per_device(): pl.pallas_call(lambda *refs: conv_kernel(sources, *refs), out_shape=[jax....  1.51 us
    pallas_call x1, Pallas kernels, per_device(): pl.pallas_call(early_kernel, out_shape=prepared, in_specs=[whole] * EARLY...  1.14 us
    pallas_call x2, Pallas kernels, per_device(): pl.pallas_call(functools.partial(gate_kernel, rounds), out_shape=jax.Shap...  1.05 us
  transfers between devices with their start and end apart: 14, of which 7 were waited for; matrix products, arithmetic and copies ran while one was open for 0% of the time, Pallas kernels for 6%

profile of v7, /device:TPU:0, one launch (start us, length us, event | category | flops | bytes accessed | tf_op | source)
XLA Modules:
  0.0 36.3 jit_solution(7007098619714362970)
XLA Ops:
  0.0 0.0 copy-start
  0.0 0.0 copy-start.1
  0.0 2.8 %shard_map.55 = (bf16[272,128]{1,0:T(8,128)(2,1)S(1)}, bf16[272,128]{1,0:T(8,128)(2,1)S(1)}, bf16[272,128]{1,0:T(8,128)(2,1)S(1)}, bf16[272,128]{1,0:T(8,128)(2,...) custom-call(bf16[128,2048]{1,0:T(8,128)(2,1)} %key_hbm.1, ...), custom_call_target="tpu_custom_call" | custom-call | tf_op jit(solution)/shard_map/pallas_call | solution.py:220
  2.9 3.8 %collective-permute-start.1 = (bf16[272,128]{1,0:T(8,128)(2,1)S(1)}, bf16[272,128]{1,0:T(8,128)(2,1)S(1)}, u32[]{:S(2)}, u32[]{:S(2)}) collective-permute-start(bf16[272,128]{1,0:T(8,128)(2,1)S(1)} %get-tuple-element.29), channel_id=1, source_target_pairs={{0,24},{1,25},{2,26},{3,27},{4,28},{5,29},{6,30},{7,31},{8,16},{9,... | collective-permute-start | bytes 208904 | tf_op jit(solution)/shard_map/ppermute | solution.py:41
  6.7 1.5 %collective-permute-start.2 = (bf16[272,128]{1,0:T(8,128)(2,1)S(1)}, bf16[272,128]{1,0:T(8,128)(2,1)S(1)}, u32[]{:S(2)}, u32[]{:S(2)}) collective-permute-start(bf16[272,128]{1,0:T(8,128)(2,1)S(1)} %get-tuple-element.30), channel_id=1, source_target_pairs={{0,4},{1,5},{2,6},{3,7},{4,0},{5,1},{6,2},{7,3},{8,12},{9,13},{10,... | collective-permute-start | bytes 208904 | tf_op jit(solution)/shard_map/ppermute | solution.py:41
  8.2 0.0 collective-permute-start.3
  8.2 0.8 %collective-permute-start.4 = (bf16[272,128]{1,0:T(8,128)(2,1)S(1)}, bf16[272,128]{1,0:T(8,128)(2,1)S(1)}, u32[]{:S(2)}, u32[]{:S(2)}) collective-permute-start(bf16[272,128]{1,0:T(8,128)(2,1)S(1)} %get-tuple-element.32), channel_id=1, source_target_pairs={{0,8},{1,9},{2,10},{3,11},{4,12},{5,13},{6,14},{7,15},{8,0},{9,1},... | collective-permute-start | bytes 208904 | tf_op jit(solution)/shard_map/ppermute | solution.py:41
  9.0 2.1 %collective-permute-start.5 = (bf16[272,128]{1,0:T(8,128)(2,1)S(1)}, bf16[272,128]{1,0:T(8,128)(2,1)S(1)}, u32[]{:S(2)}, u32[]{:S(2)}) collective-permute-start(bf16[272,128]{1,0:T(8,128)(2,1)S(1)} %get-tuple-element.33), channel_id=1, source_target_pairs={{0,20},{1,21},{2,22},{3,23},{4,16},{5,17},{6,18},{7,19},{8,28},{9,... | collective-permute-start | bytes 208904 | tf_op jit(solution)/shard_map/ppermute | solution.py:41
  11.1 0.0 collective-permute-done.1.refs_1_
  11.1 3.0 %collective-permute-start.6 = (bf16[272,128]{1,0:T(8,128)(2,1)S(1)}, bf16[272,128]{1,0:T(8,128)(2,1)S(1)}, u32[]{:S(2)}, u32[]{:S(2)}) collective-permute-start(bf16[272,128]{1,0:T(8,128)(2,1)S(1)} %get-tuple-element.34), channel_id=1, source_target_pairs={{0,12},{1,13},{2,14},{3,15},{4,8},{5,9},{6,10},{7,11},{8,4},{9,5},... | collective-permute-start | bytes 208904 | tf_op jit(solution)/shard_map/ppermute | solution.py:41
  14.0 0.0 collective-permute-done.2.refs_2_
  14.0 0.5 %collective-permute-start = (bf16[272,128]{1,0:T(8,128)(2,1)S(1)}, bf16[272,128]{1,0:T(8,128)(2,1)S(1)}, u32[]{:S(2)}, u32[]{:S(2)}) collective-permute-start(bf16[272,128]{1,0:T(8,128)(2,1)S(1)} %get-tuple-element.27), channel_id=1, source_target_pairs={{0,28},{1,29},{2,30},{3,31},{4,24},{5,25},{6,26},{7,27},{8,20},{9,... | collective-permute-start | bytes 208904 | tf_op jit(solution)/shard_map/ppermute | solution.py:41
  14.5 0.3 collective-permute-done.3.refs_3_
  14.8 0.0 collective-permute-done.4.refs_4_
  14.8 2.1 %collective-permute-done.5.refs_5_ = bf16[272,128]{1,0:T(8,128)(2,1)S(1)} collective-permute-done((bf16[272,128]{1,0:T(8,128)(2,1)S(1)}, bf16[272,128]{1,0:T(8,128)(2,1)S(1)}, u32[]{:S(2)}, u32[]{:S(2)}) %collective-permute-start.5) | collective-permute-done | bytes 69664 | tf_op jit(solution)/shard_map/ppermute | solution.py:41
  16.9 0.0 collective-permute-done.6.refs_6_
  16.9 1.1 %shard_map.56 = (bf16[8,16,128,128]{3,2,1,0:T(8,128)(2,1)S(1)}, bf16[8,256,128]{2,1,0:T(8,128)(2,1)S(1)}) custom-call(bf16[272,128]{1,0:T(8,128)(2,1)S(1)} %get-tuple-element.28.refs_0_, bf16[272,128]{1,0:T(8,128)(2,1)S(1)} %collective-permute-done.1.refs_1_, bf16[272,128]{1,0:T(8,128)(2,1)S(1)} %collective-permute-done.2.refs_2_, ...), custom_call_target="tpu_custom_call" | custom-call | bytes 8388608 | tf_op jit(solution)/shard_map/pallas_call | solution.py:246
  18.0 3.0 %collective-permute-done.refs_0_ = bf16[272,128]{1,0:T(8,128)(2,1)S(1)} collective-permute-done((bf16[272,128]{1,0:T(8,128)(2,1)S(1)}, bf16[272,128]{1,0:T(8,128)(2,1)S(1)}, u32[]{:S(2)}, u32[]{:S(2)}) %collective-permute-start) | collective-permute-done | bytes 69664 | tf_op jit(solution)/shard_map/ppermute | solution.py:41
  21.0 1.5 %shard_map.57 = (bf16[256,128]{1,0:T(8,128)(2,1)S(1)}, bf16[256,128]{1,0:T(8,128)(2,1)S(1)}, bf16[256,128]{1,0:T(8,128)(2,1)S(1)}, bf16[256,128]{1,0:T(8,128)(2,...) custom-call(bf16[272,128]{1,0:T(8,128)(2,1)S(1)} %collective-permute, ...), custom_call_target="tpu_custom_call", output_to_operand_aliasing={{8}: (1, {}), {9}: (2, {})} | custom-call | tf_op jit(solution)/shard_map/pallas_call | solution.py:256
  22.6 0.4 %collective-permute-start.8 = (bf16[256,128]{1,0:T(8,128)(2,1)S(1)}, bf16[256,128]{1,0:T(8,128)(2,1)S(1)}, u32[]{:S(2)}, u32[]{:S(2)}) collective-permute-start(bf16[256,128]{1,0:T(8,128)(2,1)S(1)} %get-tuple-element.39), channel_id=1, source_target_pairs={{0,16},{1,17},{2,18},{3,19},{4,20},{5,21},{6,22},{7,23},{8,24},{9,... | collective-permute-start | bytes 196616 | tf_op jit(solution)/shard_map/ppermute | solution.py:41
  22.9 0.6 %collective-permute-start.9 = (bf16[256,128]{1,0:T(8,128)(2,1)S(1)}, bf16[256,128]{1,0:T(8,128)(2,1)S(1)}, u32[]{:S(2)}, u32[]{:S(2)}) collective-permute-start(bf16[256,128]{1,0:T(8,128)(2,1)S(1)} %get-tuple-element.40), channel_id=1, source_target_pairs={{0,4},{1,5},{2,6},{3,7},{4,0},{5,1},{6,2},{7,3},{8,12},{9,13},{10,... | collective-permute-start | bytes 196616 | tf_op jit(solution)/shard_map/ppermute | solution.py:41
  23.5 3.5 %collective-permute-start.10 = (bf16[256,128]{1,0:T(8,128)(2,1)S(1)}, bf16[256,128]{1,0:T(8,128)(2,1)S(1)}, u32[]{:S(2)}, u32[]{:S(2)}) collective-permute-start(bf16[256,128]{1,0:T(8,128)(2,1)S(1)} %get-tuple-element.41), channel_id=1, source_target_pairs={{0,20},{1,21},{2,22},{3,23},{4,16},{5,17},{6,18},{7,19},{8,28},{9,... | collective-permute-start | bytes 196616 | tf_op jit(solution)/shard_map/ppermute | solution.py:41
  27.0 0.0 collective-permute-start.11
  27.0 1.8 %collective-permute-start.12 = (bf16[256,128]{1,0:T(8,128)(2,1)S(1)}, bf16[256,128]{1,0:T(8,128)(2,1)S(1)}, u32[]{:S(2)}, u32[]{:S(2)}) collective-permute-start(bf16[256,128]{1,0:T(8,128)(2,1)S(1)} %get-tuple-element.43), channel_id=1, source_target_pairs={{0,24},{1,25},{2,26},{3,27},{4,28},{5,29},{6,30},{7,31},{8,16},{9,... | collective-permute-start | bytes 196616 | tf_op jit(solution)/shard_map/ppermute | solution.py:41
  28.8 0.4 %collective-permute-done.8.refs_1_ = bf16[256,128]{1,0:T(8,128)(2,1)S(1)} collective-permute-done((bf16[256,128]{1,0:T(8,128)(2,1)S(1)}, bf16[256,128]{1,0:T(8,128)(2,1)S(1)}, u32[]{:S(2)}, u32[]{:S(2)}) %collective-permute-start.8) | collective-permute-done | bytes 65568 | tf_op jit(solution)/shard_map/ppermute | solution.py:41
  29.2 0.0 collective-permute-start.13
  29.2 0.0 collective-permute-done.9.refs_2_
  29.2 3.7 %collective-permute-start.7 = (bf16[256,128]{1,0:T(8,128)(2,1)S(1)}, bf16[256,128]{1,0:T(8,128)(2,1)S(1)}, u32[]{:S(2)}, u32[]{:S(2)}) collective-permute-start(bf16[256,128]{1,0:T(8,128)(2,1)S(1)} %get-tuple-element.37), channel_id=1, source_target_pairs={{0,28},{1,29},{2,30},{3,31},{4,24},{5,25},{6,26},{7,27},{8,20},{9,... | collective-permute-start | bytes 196616 | tf_op jit(solution)/shard_map/ppermute | solution.py:41
  32.9 0.3 collective-permute-done.10.refs_3_
  33.1 0.0 collective-permute-done.11.refs_4_
  33.1 0.0 collective-permute-done.12.refs_5_
  33.2 1.2 %collective-permute-done.13.refs_6_ = bf16[256,128]{1,0:T(8,128)(2,1)S(1)} collective-permute-done((bf16[256,128]{1,0:T(8,128)(2,1)S(1)}, bf16[256,128]{1,0:T(8,128)(2,1)S(1)}, u32[]{:S(2)}, u32[]{:S(2)}) %collective-permute-start.13) | collective-permute-done | bytes 65568 | tf_op jit(solution)/shard_map/ppermute | solution.py:41
  34.4 0.0 copy-done
  34.4 0.0 copy-done.1
  34.4 1.0 %shard_map.58.refs_1_ = bf16[128,2048]{1,0:T(8,128)(2,1)} custom-call(bf16[128,2048]{1,0:T(8,128)(2,1)S(1)} %copy-done, f32[1,2048]{1,0:T(1,128)S(1)} %bitcast.1, bf16[128,2048]{1,0:T(8,128)(2,1)S(1)} %get-tuple-element.25.mixed_ref, bf16[2048,128]{1,0:T(8,128)(2,1)S(1)} %get-tuple-element.26.home_ref, bf16[256,128]{1,0:T(8,128)(2,1)S(1)} %get-tuple-element.38.refs_0_, ...), custom_call_target="tpu_custom_call" | custom-call | tf_op jit(solution)/shard_map/pallas_call | solution.py:277
  35.4 0.9 %collective-permute-done.7.refs_0_ = bf16[256,128]{1,0:T(8,128)(2,1)S(1)} collective-permute-done((bf16[256,128]{1,0:T(8,128)(2,1)S(1)}, bf16[256,128]{1,0:T(8,128)(2,1)S(1)}, u32[]{:S(2)}, u32[]{:S(2)}) %collective-permute-start.7) | collective-permute-done | bytes 65568 | tf_op jit(solution)/shard_map/ppermute | solution.py:41
  36.2 0.1 shard_map.59
Async XLA Ops:
  0.0 34.4 %copy-start = (bf16[128,2048]{1,0:T(8,128)(2,1)S(1)}, bf16[128,2048]{1,0:T(8,128)(2,1)}, u32[]{:S(2)}) copy-start(bf16[128,2048]{1,0:T(8,128)(2,1)} %query_ref.3) | copy-start | bytes 1572868
  0.0 34.4 %copy-start.1 = (f32[2048]{0:T(1024)S(1)}, f32[2048]{0:T(1024)}, u32[]{:S(2)}) copy-start(f32[2048]{0:T(1024)} %param.9) | copy-start | bytes 24580
  2.9 8.2 %collective-permute-start.1 = (bf16[272,128]{1,0:T(8,128)(2,1)S(1)}, bf16[272,128]{1,0:T(8,128)(2,1)S(1)}, u32[]{:S(2)}, u32[]{:S(2)}) collective-permute-start(bf16[272,128]{1,0:T(8,128)(2,1)S(1)} %get-tuple-element.29), channel_id=1, source_target_pairs={{0,24},{1,25},{2,26},{3,27},{4,28},{5,29},{6,30},{7,31},{8,16},{9,... | collective-permute-start | bytes 208904 | tf_op jit(solution)/shard_map/ppermute | solution.py:41
  6.7 7.3 %collective-permute-start.2 = (bf16[272,128]{1,0:T(8,128)(2,1)S(1)}, bf16[272,128]{1,0:T(8,128)(2,1)S(1)}, u32[]{:S(2)}, u32[]{:S(2)}) collective-permute-start(bf16[272,128]{1,0:T(8,128)(2,1)S(1)} %get-tuple-element.30), channel_id=1, source_target_pairs={{0,4},{1,5},{2,6},{3,7},{4,0},{5,1},{6,2},{7,3},{8,12},{9,13},{10,... | collective-permute-start | bytes 208904 | tf_op jit(solution)/shard_map/ppermute | solution.py:41
  8.2 6.6 %collective-permute-start.3 = (bf16[272,128]{1,0:T(8,128)(2,1)S(1)}, bf16[272,128]{1,0:T(8,128)(2,1)S(1)}, u32[]{:S(2)}, u32[]{:S(2)}) collective-permute-start(bf16[272,128]{1,0:T(8,128)(2,1)S(1)} %get-tuple-element.31), channel_id=1, source_target_pairs={{0,16},{1,17},{2,18},{3,19},{4,20},{5,21},{6,22},{7,23},{8,24},{9,... | collective-permute-start | bytes 208904 | tf_op jit(solution)/shard_map/ppermute | solution.py:41
  8.2 6.6 %collective-permute-start.4 = (bf16[272,128]{1,0:T(8,128)(2,1)S(1)}, bf16[272,128]{1,0:T(8,128)(2,1)S(1)}, u32[]{:S(2)}, u32[]{:S(2)}) collective-permute-start(bf16[272,128]{1,0:T(8,128)(2,1)S(1)} %get-tuple-element.32), channel_id=1, source_target_pairs={{0,8},{1,9},{2,10},{3,11},{4,12},{5,13},{6,14},{7,15},{8,0},{9,1},... | collective-permute-start | bytes 208904 | tf_op jit(solution)/shard_map/ppermute | solution.py:41
  9.0 7.9 %collective-permute-start.5 = (bf16[272,128]{1,0:T(8,128)(2,1)S(1)}, bf16[272,128]{1,0:T(8,128)(2,1)S(1)}, u32[]{:S(2)}, u32[]{:S(2)}) collective-permute-start(bf16[272,128]{1,0:T(8,128)(2,1)S(1)} %get-tuple-element.33), channel_id=1, source_target_pairs={{0,20},{1,21},{2,22},{3,23},{4,16},{5,17},{6,18},{7,19},{8,28},{9,... | collective-permute-start | bytes 208904 | tf_op jit(solution)/shard_map/ppermute | solution.py:41
  11.1 5.8 %collective-permute-start.6 = (bf16[272,128]{1,0:T(8,128)(2,1)S(1)}, bf16[272,128]{1,0:T(8,128)(2,1)S(1)}, u32[]{:S(2)}, u32[]{:S(2)}) collective-permute-start(bf16[272,128]{1,0:T(8,128)(2,1)S(1)} %get-tuple-element.34), channel_id=1, source_target_pairs={{0,12},{1,13},{2,14},{3,15},{4,8},{5,9},{6,10},{7,11},{8,4},{9,5},... | collective-permute-start | bytes 208904 | tf_op jit(solution)/shard_map/ppermute | solution.py:41
  14.0 7.0 %collective-permute-start = (bf16[272,128]{1,0:T(8,128)(2,1)S(1)}, bf16[272,128]{1,0:T(8,128)(2,1)S(1)}, u32[]{:S(2)}, u32[]{:S(2)}) collective-permute-start(bf16[272,128]{1,0:T(8,128)(2,1)S(1)} %get-tuple-element.27), channel_id=1, source_target_pairs={{0,28},{1,29},{2,30},{3,31},{4,24},{5,25},{6,26},{7,27},{8,20},{9,... | collective-permute-start | bytes 208904 | tf_op jit(solution)/shard_map/ppermute | solution.py:41
  22.6 6.6 %collective-permute-start.8 = (bf16[256,128]{1,0:T(8,128)(2,1)S(1)}, bf16[256,128]{1,0:T(8,128)(2,1)S(1)}, u32[]{:S(2)}, u32[]{:S(2)}) collective-permute-start(bf16[256,128]{1,0:T(8,128)(2,1)S(1)} %get-tuple-element.39), channel_id=1, source_target_pairs={{0,16},{1,17},{2,18},{3,19},{4,20},{5,21},{6,22},{7,23},{8,24},{9,... | collective-permute-start | bytes 196616 | tf_op jit(solution)/shard_map/ppermute | solution.py:41
  22.9 6.3 %collective-permute-start.9 = (bf16[256,128]{1,0:T(8,128)(2,1)S(1)}, bf16[256,128]{1,0:T(8,128)(2,1)S(1)}, u32[]{:S(2)}, u32[]{:S(2)}) collective-permute-start(bf16[256,128]{1,0:T(8,128)(2,1)S(1)} %get-tuple-element.40), channel_id=1, source_target_pairs={{0,4},{1,5},{2,6},{3,7},{4,0},{5,1},{6,2},{7,3},{8,12},{9,13},{10,... | collective-permute-start | bytes 196616 | tf_op jit(solution)/shard_map/ppermute | solution.py:41
  23.5 9.6 %collective-permute-start.10 = (bf16[256,128]{1,0:T(8,128)(2,1)S(1)}, bf16[256,128]{1,0:T(8,128)(2,1)S(1)}, u32[]{:S(2)}, u32[]{:S(2)}) collective-permute-start(bf16[256,128]{1,0:T(8,128)(2,1)S(1)} %get-tuple-element.41), channel_id=1, source_target_pairs={{0,20},{1,21},{2,22},{3,23},{4,16},{5,17},{6,18},{7,19},{8,28},{9,... | collective-permute-start | bytes 196616 | tf_op jit(solution)/shard_map/ppermute | solution.py:41
  27.0 6.1 %collective-permute-start.11 = (bf16[256,128]{1,0:T(8,128)(2,1)S(1)}, bf16[256,128]{1,0:T(8,128)(2,1)S(1)}, u32[]{:S(2)}, u32[]{:S(2)}) collective-permute-start(bf16[256,128]{1,0:T(8,128)(2,1)S(1)} %get-tuple-element.42), channel_id=1, source_target_pairs={{0,8},{1,9},{2,10},{3,11},{4,12},{5,13},{6,14},{7,15},{8,0},{9,1},... | collective-permute-start | bytes 196616 | tf_op jit(solution)/shard_map/ppermute | solution.py:41
  27.0 6.2 %collective-permute-start.12 = (bf16[256,128]{1,0:T(8,128)(2,1)S(1)}, bf16[256,128]{1,0:T(8,128)(2,1)S(1)}, u32[]{:S(2)}, u32[]{:S(2)}) collective-permute-start(bf16[256,128]{1,0:T(8,128)(2,1)S(1)} %get-tuple-element.43), channel_id=1, source_target_pairs={{0,24},{1,25},{2,26},{3,27},{4,28},{5,29},{6,30},{7,31},{8,16},{9,... | collective-permute-start | bytes 196616 | tf_op jit(solution)/shard_map/ppermute | solution.py:41
  29.2 5.2 %collective-permute-start.13 = (bf16[256,128]{1,0:T(8,128)(2,1)S(1)}, bf16[256,128]{1,0:T(8,128)(2,1)S(1)}, u32[]{:S(2)}, u32[]{:S(2)}) collective-permute-start(bf16[256,128]{1,0:T(8,128)(2,1)S(1)} %get-tuple-element.44), channel_id=1, source_target_pairs={{0,12},{1,13},{2,14},{3,15},{4,8},{5,9},{6,10},{7,11},{8,4},{9,5},... | collective-permute-start | bytes 196616 | tf_op jit(solution)/shard_map/ppermute | solution.py:41
  29.2 7.0 %collective-permute-start.7 = (bf16[256,128]{1,0:T(8,128)(2,1)S(1)}, bf16[256,128]{1,0:T(8,128)(2,1)S(1)}, u32[]{:S(2)}, u32[]{:S(2)}) collective-permute-start(bf16[256,128]{1,0:T(8,128)(2,1)S(1)} %get-tuple-element.37), channel_id=1, source_target_pairs={{0,28},{1,29},{2,30},{3,31},{4,24},{5,25},{6,26},{7,27},{8,20},{9,... | collective-permute-start | bytes 196616 | tf_op jit(solution)/shard_map/ppermute | solution.py:41

commit v8 on v7

--- a/solution.py
+++ b/solution.py
@@ -17,7 +17,7 @@
 RETURN = ((4, 1, 5, 2, 6, 3, 7), (4, 1, 5, 2, 6, 3, 7))
 CHUNKS = 2
 EARLY = 7
-AHEAD = 2
+AHEAD = 4
 UNROLL = 8
 FIRST = 7
 SMALL = pltpu.CompilerParams(vmem_limit_bytes=16 * 1024 * 1024)
@@ -160,11 +160,16 @@
             elif lag:
                 signal = [jnp.zeros((lag * GROUP, LANES), jnp.bfloat16)] + signal
             signals.append(jnp.concatenate(signal, axis=0))
-        total = jnp.dot(
-            jnp.concatenate(signals, axis=1),
-            jnp.concatenate(filters, axis=0),
-            preferred_element_type=jnp.float32,
-        )
+        total = None
+        for lag in range(0, LAGS, 2):
+            skipped = lag * GROUP if sources == 1 else 0
+            signal = jnp.concatenate([one[skipped:] for one in signals[lag : lag + 2]], axis=1)
+            part = jnp.dot(signal, jnp.concatenate(filters[lag : lag + 2], axis=0), preferred_element_type=jnp.float32)
+            if skipped:
+                part = jnp.concatenate([total[:skipped], total[skipped:] + part], axis=0)
+            elif lag:
+                part = total + part
+            total = part
         results[group] = total.astype(jnp.bfloat16)
     for partner, conv_ref in zip(partners(RETURN), conv_refs):
         rows = pl.ds(pl.multiple_of(partner * GROUP, GROUP), GROUP)

time: 36.4 us -> 36.1 us (level)
  no operation moved by 1% of the time
where the time goes in v8:
time: 36.1 us; the launch traced here: 35.9 us
  starting transfers between devices  21.5 us (60%)
  waiting for transfers between devices  8.14 us (23%)
  Pallas kernels  6.2 us (17%)
    ppermute x14, starting transfers between devices, exchange(): got.append(lax.ppermute(block, ('ctx', 'ch'), pairs))  21.5 us
    ppermute x14, waiting for transfers between devices, exchange(): got.append(lax.ppermute(block, ('ctx', 'ch'), pairs))  8.14 us
    pallas_call x1, Pallas kernels, per_device(): pl.pallas_call(mix_kernel, out_shape=[jax.ShapeDtypeStruct((halves * BLOC...  2.84 us
    pallas_call x1, Pallas kernels, per_device(): pl.pallas_call(lambda *refs: conv_kernel(sources, *refs), out_shape=[jax....  1.17 us
    pallas_call x1, Pallas kernels, per_device(): pl.pallas_call(early_kernel, out_shape=prepared, in_specs=[whole] * EARLY...  1.14 us
    pallas_call x2, Pallas kernels, per_device(): pl.pallas_call(functools.partial(gate_kernel, rounds), out_shape=jax.Shap...  1.05 us
  transfers between devices with their start and end apart: 14, of which 7 were waited for; matrix products, arithmetic and copies ran while one was open for 0% of the time, Pallas kernels for 6%

profile of v8, /device:TPU:0, one launch (start us, length us, event | category | flops | bytes accessed | tf_op | source)
XLA Modules:
  0.0 35.9 jit_solution(16176829412305198795)
XLA Ops:
  0.0 0.0 copy-start
  0.0 0.0 copy-start.1
  0.0 2.8 %shard_map.55 = (bf16[272,128]{1,0:T(8,128)(2,1)S(1)}, bf16[272,128]{1,0:T(8,128)(2,1)S(1)}, bf16[272,128]{1,0:T(8,128)(2,1)S(1)}, bf16[272,128]{1,0:T(8,128)(2,...) custom-call(bf16[128,2048]{1,0:T(8,128)(2,1)} %key_hbm.1, ...), custom_call_target="tpu_custom_call" | custom-call | tf_op jit(solution)/shard_map/pallas_call | solution.py:225
  2.9 3.8 %collective-permute-start.1 = (bf16[272,128]{1,0:T(8,128)(2,1)S(1)}, bf16[272,128]{1,0:T(8,128)(2,1)S(1)}, u32[]{:S(2)}, u32[]{:S(2)}) collective-permute-start(bf16[272,128]{1,0:T(8,128)(2,1)S(1)} %get-tuple-element.29), channel_id=1, source_target_pairs={{0,24},{1,25},{2,26},{3,27},{4,28},{5,29},{6,30},{7,31},{8,16},{9,... | collective-permute-start | bytes 208904 | tf_op jit(solution)/shard_map/ppermute | solution.py:41
  6.7 1.5 %collective-permute-start.2 = (bf16[272,128]{1,0:T(8,128)(2,1)S(1)}, bf16[272,128]{1,0:T(8,128)(2,1)S(1)}, u32[]{:S(2)}, u32[]{:S(2)}) collective-permute-start(bf16[272,128]{1,0:T(8,128)(2,1)S(1)} %get-tuple-element.30), channel_id=1, source_target_pairs={{0,4},{1,5},{2,6},{3,7},{4,0},{5,1},{6,2},{7,3},{8,12},{9,13},{10,... | collective-permute-start | bytes 208904 | tf_op jit(solution)/shard_map/ppermute | solution.py:41
  8.2 0.0 collective-permute-start.3
  8.2 0.8 %collective-permute-start.4 = (bf16[272,128]{1,0:T(8,128)(2,1)S(1)}, bf16[272,128]{1,0:T(8,128)(2,1)S(1)}, u32[]{:S(2)}, u32[]{:S(2)}) collective-permute-start(bf16[272,128]{1,0:T(8,128)(2,1)S(1)} %get-tuple-element.32), channel_id=1, source_target_pairs={{0,8},{1,9},{2,10},{3,11},{4,12},{5,13},{6,14},{7,15},{8,0},{9,1},... | collective-permute-start | bytes 208904 | tf_op jit(solution)/shard_map/ppermute | solution.py:41
  9.0 2.1 %collective-permute-start.5 = (bf16[272,128]{1,0:T(8,128)(2,1)S(1)}, bf16[272,128]{1,0:T(8,128)(2,1)S(1)}, u32[]{:S(2)}, u32[]{:S(2)}) collective-permute-start(bf16[272,128]{1,0:T(8,128)(2,1)S(1)} %get-tuple-element.33), channel_id=1, source_target_pairs={{0,20},{1,21},{2,22},{3,23},{4,16},{5,17},{6,18},{7,19},{8,28},{9,... | collective-permute-start | bytes 208904 | tf_op jit(solution)/shard_map/ppermute | solution.py:41
  11.1 0.0 collective-permute-done.1.refs_1_
  11.1 3.0 %collective-permute-start.6 = (bf16[272,128]{1,0:T(8,128)(2,1)S(1)}, bf16[272,128]{1,0:T(8,128)(2,1)S(1)}, u32[]{:S(2)}, u32[]{:S(2)}) collective-permute-start(bf16[272,128]{1,0:T(8,128)(2,1)S(1)} %get-tuple-element.34), channel_id=1, source_target_pairs={{0,12},{1,13},{2,14},{3,15},{4,8},{5,9},{6,10},{7,11},{8,4},{9,5},... | collective-permute-start | bytes 208904 | tf_op jit(solution)/shard_map/ppermute | solution.py:41
  14.0 0.0 collective-permute-done.2.refs_2_
  14.0 0.5 %collective-permute-start = (bf16[272,128]{1,0:T(8,128)(2,1)S(1)}, bf16[272,128]{1,0:T(8,128)(2,1)S(1)}, u32[]{:S(2)}, u32[]{:S(2)}) collective-permute-start(bf16[272,128]{1,0:T(8,128)(2,1)S(1)} %get-tuple-element.27), channel_id=1, source_target_pairs={{0,28},{1,29},{2,30},{3,31},{4,24},{5,25},{6,26},{7,27},{8,20},{9,... | collective-permute-start | bytes 208904 | tf_op jit(solution)/shard_map/ppermute | solution.py:41
  14.5 0.3 collective-permute-done.3.refs_3_
  14.8 0.0 collective-permute-done.4.refs_4_
  14.8 2.1 %collective-permute-done.5.refs_5_ = bf16[272,128]{1,0:T(8,128)(2,1)S(1)} collective-permute-done((bf16[272,128]{1,0:T(8,128)(2,1)S(1)}, bf16[272,128]{1,0:T(8,128)(2,1)S(1)}, u32[]{:S(2)}, u32[]{:S(2)}) %collective-permute-start.5) | collective-permute-done | bytes 69664 | tf_op jit(solution)/shard_map/ppermute | solution.py:41
  16.9 0.0 collective-permute-done.6.refs_6_
  16.9 1.1 %shard_map.56 = (bf16[8,16,128,128]{3,2,1,0:T(8,128)(2,1)S(1)}, bf16[8,256,128]{2,1,0:T(8,128)(2,1)S(1)}) custom-call(bf16[272,128]{1,0:T(8,128)(2,1)S(1)} %get-tuple-element.28.refs_0_, bf16[272,128]{1,0:T(8,128)(2,1)S(1)} %collective-permute-done.1.refs_1_, bf16[272,128]{1,0:T(8,128)(2,1)S(1)} %collective-permute-done.2.refs_2_, ...), custom_call_target="tpu_custom_call" | custom-call | bytes 8388608 | tf_op jit(solution)/shard_map/pallas_call | solution.py:251
  18.0 3.0 %collective-permute-done.refs_0_ = bf16[272,128]{1,0:T(8,128)(2,1)S(1)} collective-permute-done((bf16[272,128]{1,0:T(8,128)(2,1)S(1)}, bf16[272,128]{1,0:T(8,128)(2,1)S(1)}, u32[]{:S(2)}, u32[]{:S(2)}) %collective-permute-start) | collective-permute-done | bytes 69664 | tf_op jit(solution)/shard_map/ppermute | solution.py:41
  21.0 1.2 %shard_map.57 = (bf16[256,128]{1,0:T(8,128)(2,1)S(1)}, bf16[256,128]{1,0:T(8,128)(2,1)S(1)}, bf16[256,128]{1,0:T(8,128)(2,1)S(1)}, bf16[256,128]{1,0:T(8,128)(2,...) custom-call(bf16[272,128]{1,0:T(8,128)(2,1)S(1)} %collective-permute, ...), custom_call_target="tpu_custom_call", output_to_operand_aliasing={{8}: (1, {}), {9}: (2, {})} | custom-call | tf_op jit(solution)/shard_map/pallas_call | solution.py:261
  22.2 0.4 %collective-permute-start.8 = (bf16[256,128]{1,0:T(8,128)(2,1)S(1)}, bf16[256,128]{1,0:T(8,128)(2,1)S(1)}, u32[]{:S(2)}, u32[]{:S(2)}) collective-permute-start(bf16[256,128]{1,0:T(8,128)(2,1)S(1)} %get-tuple-element.39), channel_id=1, source_target_pairs={{0,16},{1,17},{2,18},{3,19},{4,20},{5,21},{6,22},{7,23},{8,24},{9,... | collective-permute-start | bytes 196616 | tf_op jit(solution)/shard_map/ppermute | solution.py:41
  22.6 0.6 %collective-permute-start.9 = (bf16[256,128]{1,0:T(8,128)(2,1)S(1)}, bf16[256,128]{1,0:T(8,128)(2,1)S(1)}, u32[]{:S(2)}, u32[]{:S(2)}) collective-permute-start(bf16[256,128]{1,0:T(8,128)(2,1)S(1)} %get-tuple-element.40), channel_id=1, source_target_pairs={{0,4},{1,5},{2,6},{3,7},{4,0},{5,1},{6,2},{7,3},{8,12},{9,13},{10,... | collective-permute-start | bytes 196616 | tf_op jit(solution)/shard_map/ppermute | solution.py:41
  23.2 3.5 %collective-permute-start.10 = (bf16[256,128]{1,0:T(8,128)(2,1)S(1)}, bf16[256,128]{1,0:T(8,128)(2,1)S(1)}, u32[]{:S(2)}, u32[]{:S(2)}) collective-permute-start(bf16[256,128]{1,0:T(8,128)(2,1)S(1)} %get-tuple-element.41), channel_id=1, source_target_pairs={{0,20},{1,21},{2,22},{3,23},{4,16},{5,17},{6,18},{7,19},{8,28},{9,... | collective-permute-start | bytes 196616 | tf_op jit(solution)/shard_map/ppermute | solution.py:41
  26.7 0.0 collective-permute-start.11
  26.7 1.8 %collective-permute-start.12 = (bf16[256,128]{1,0:T(8,128)(2,1)S(1)}, bf16[256,128]{1,0:T(8,128)(2,1)S(1)}, u32[]{:S(2)}, u32[]{:S(2)}) collective-permute-start(bf16[256,128]{1,0:T(8,128)(2,1)S(1)} %get-tuple-element.43), channel_id=1, source_target_pairs={{0,24},{1,25},{2,26},{3,27},{4,28},{5,29},{6,30},{7,31},{8,16},{9,... | collective-permute-start | bytes 196616 | tf_op jit(solution)/shard_map/ppermute | solution.py:41
  28.5 0.4 %collective-permute-done.8.refs_1_ = bf16[256,128]{1,0:T(8,128)(2,1)S(1)} collective-permute-done((bf16[256,128]{1,0:T(8,128)(2,1)S(1)}, bf16[256,128]{1,0:T(8,128)(2,1)S(1)}, u32[]{:S(2)}, u32[]{:S(2)}) %collective-permute-start.8) | collective-permute-done | bytes 65568 | tf_op jit(solution)/shard_map/ppermute | solution.py:41
  28.9 0.0 collective-permute-start.13
  28.9 0.0 collective-permute-done.9.refs_2_
  28.9 3.7 %collective-permute-start.7 = (bf16[256,128]{1,0:T(8,128)(2,1)S(1)}, bf16[256,128]{1,0:T(8,128)(2,1)S(1)}, u32[]{:S(2)}, u32[]{:S(2)}) collective-permute-start(bf16[256,128]{1,0:T(8,128)(2,1)S(1)} %get-tuple-element.37), channel_id=1, source_target_pairs={{0,28},{1,29},{2,30},{3,31},{4,24},{5,25},{6,26},{7,27},{8,20},{9,... | collective-permute-start | bytes 196616 | tf_op jit(solution)/shard_map/ppermute | solution.py:41
  32.5 0.3 collective-permute-done.10.refs_3_
  32.8 0.0 collective-permute-done.11.refs_4_
  32.8 0.0 collective-permute-done.12.refs_5_
  32.8 1.2 %collective-permute-done.13.refs_6_ = bf16[256,128]{1,0:T(8,128)(2,1)S(1)} collective-permute-done((bf16[256,128]{1,0:T(8,128)(2,1)S(1)}, bf16[256,128]{1,0:T(8,128)(2,1)S(1)}, u32[]{:S(2)}, u32[]{:S(2)}) %collective-permute-start.13) | collective-permute-done | bytes 65568 | tf_op jit(solution)/shard_map/ppermute | solution.py:41
  34.0 0.0 copy-done
  34.0 0.0 copy-done.1
  34.0 1.0 %shard_map.58.refs_1_ = bf16[128,2048]{1,0:T(8,128)(2,1)} custom-call(bf16[128,2048]{1,0:T(8,128)(2,1)S(1)} %copy-done, f32[1,2048]{1,0:T(1,128)S(1)} %bitcast.1, bf16[128,2048]{1,0:T(8,128)(2,1)S(1)} %get-tuple-element.25.mixed_ref, bf16[2048,128]{1,0:T(8,128)(2,1)S(1)} %get-tuple-element.26.home_ref, bf16[256,128]{1,0:T(8,128)(2,1)S(1)} %get-tuple-element.38.refs_0_, ...), custom_call_target="tpu_custom_call" | custom-call | tf_op jit(solution)/shard_map/pallas_call | solution.py:282
  35.0 0.8 %collective-permute-done.7.refs_0_ = bf16[256,128]{1,0:T(8,128)(2,1)S(1)} collective-permute-done((bf16[256,128]{1,0:T(8,128)(2,1)S(1)}, bf16[256,128]{1,0:T(8,128)(2,1)S(1)}, u32[]{:S(2)}, u32[]{:S(2)}) %collective-permute-start.7) | collective-permute-done | bytes 65568 | tf_op jit(solution)/shard_map/ppermute | solution.py:41
  35.9 0.1 shard_map.59
Async XLA Ops:
  0.0 34.0 %copy-start = (bf16[128,2048]{1,0:T(8,128)(2,1)S(1)}, bf16[128,2048]{1,0:T(8,128)(2,1)}, u32[]{:S(2)}) copy-start(bf16[128,2048]{1,0:T(8,128)(2,1)} %query_ref.3) | copy-start | bytes 1572868
  0.0 34.0 %copy-start.1 = (f32[2048]{0:T(1024)S(1)}, f32[2048]{0:T(1024)}, u32[]{:S(2)}) copy-start(f32[2048]{0:T(1024)} %param.9) | copy-start | bytes 24580
  2.9 8.2 %collective-permute-start.1 = (bf16[272,128]{1,0:T(8,128)(2,1)S(1)}, bf16[272,128]{1,0:T(8,128)(2,1)S(1)}, u32[]{:S(2)}, u32[]{:S(2)}) collective-permute-start(bf16[272,128]{1,0:T(8,128)(2,1)S(1)} %get-tuple-element.29), channel_id=1, source_target_pairs={{0,24},{1,25},{2,26},{3,27},{4,28},{5,29},{6,30},{7,31},{8,16},{9,... | collective-permute-start | bytes 208904 | tf_op jit(solution)/shard_map/ppermute | solution.py:41
  6.7 7.3 %collective-permute-start.2 = (bf16[272,128]{1,0:T(8,128)(2,1)S(1)}, bf16[272,128]{1,0:T(8,128)(2,1)S(1)}, u32[]{:S(2)}, u32[]{:S(2)}) collective-permute-start(bf16[272,128]{1,0:T(8,128)(2,1)S(1)} %get-tuple-element.30), channel_id=1, source_target_pairs={{0,4},{1,5},{2,6},{3,7},{4,0},{5,1},{6,2},{7,3},{8,12},{9,13},{10,... | collective-permute-start | bytes 208904 | tf_op jit(solution)/shard_map/ppermute | solution.py:41
  8.2 6.6 %collective-permute-start.3 = (bf16[272,128]{1,0:T(8,128)(2,1)S(1)}, bf16[272,128]{1,0:T(8,128)(2,1)S(1)}, u32[]{:S(2)}, u32[]{:S(2)}) collective-permute-start(bf16[272,128]{1,0:T(8,128)(2,1)S(1)} %get-tuple-element.31), channel_id=1, source_target_pairs={{0,16},{1,17},{2,18},{3,19},{4,20},{5,21},{6,22},{7,23},{8,24},{9,... | collective-permute-start | bytes 208904 | tf_op jit(solution)/shard_map/ppermute | solution.py:41
  8.2 6.6 %collective-permute-start.4 = (bf16[272,128]{1,0:T(8,128)(2,1)S(1)}, bf16[272,128]{1,0:T(8,128)(2,1)S(1)}, u32[]{:S(2)}, u32[]{:S(2)}) collective-permute-start(bf16[272,128]{1,0:T(8,128)(2,1)S(1)} %get-tuple-element.32), channel_id=1, source_target_pairs={{0,8},{1,9},{2,10},{3,11},{4,12},{5,13},{6,14},{7,15},{8,0},{9,1},... | collective-permute-start | bytes 208904 | tf_op jit(solution)/shard_map/ppermute | solution.py:41
  9.0 7.9 %collective-permute-start.5 = (bf16[272,128]{1,0:T(8,128)(2,1)S(1)}, bf16[272,128]{1,0:T(8,128)(2,1)S(1)}, u32[]{:S(2)}, u32[]{:S(2)}) collective-permute-start(bf16[272,128]{1,0:T(8,128)(2,1)S(1)} %get-tuple-element.33), channel_id=1, source_target_pairs={{0,20},{1,21},{2,22},{3,23},{4,16},{5,17},{6,18},{7,19},{8,28},{9,... | collective-permute-start | bytes 208904 | tf_op jit(solution)/shard_map/ppermute | solution.py:41
  11.1 5.8 %collective-permute-start.6 = (bf16[272,128]{1,0:T(8,128)(2,1)S(1)}, bf16[272,128]{1,0:T(8,128)(2,1)S(1)}, u32[]{:S(2)}, u32[]{:S(2)}) collective-permute-start(bf16[272,128]{1,0:T(8,128)(2,1)S(1)} %get-tuple-element.34), channel_id=1, source_target_pairs={{0,12},{1,13},{2,14},{3,15},{4,8},{5,9},{6,10},{7,11},{8,4},{9,5},... | collective-permute-start | bytes 208904 | tf_op jit(solution)/shard_map/ppermute | solution.py:41
  14.0 7.0 %collective-permute-start = (bf16[272,128]{1,0:T(8,128)(2,1)S(1)}, bf16[272,128]{1,0:T(8,128)(2,1)S(1)}, u32[]{:S(2)}, u32[]{:S(2)}) collective-permute-start(bf16[272,128]{1,0:T(8,128)(2,1)S(1)} %get-tuple-element.27), channel_id=1, source_target_pairs={{0,28},{1,29},{2,30},{3,31},{4,24},{5,25},{6,26},{7,27},{8,20},{9,... | collective-permute-start | bytes 208904 | tf_op jit(solution)/shard_map/ppermute | solution.py:41
  22.2 6.6 %collective-permute-start.8 = (bf16[256,128]{1,0:T(8,128)(2,1)S(1)}, bf16[256,128]{1,0:T(8,128)(2,1)S(1)}, u32[]{:S(2)}, u32[]{:S(2)}) collective-permute-start(bf16[256,128]{1,0:T(8,128)(2,1)S(1)} %get-tuple-element.39), channel_id=1, source_target_pairs={{0,16},{1,17},{2,18},{3,19},{4,20},{5,21},{6,22},{7,23},{8,24},{9,... | collective-permute-start | bytes 196616 | tf_op jit(solution)/shard_map/ppermute | solution.py:41
  22.6 6.3 %collective-permute-start.9 = (bf16[256,128]{1,0:T(8,128)(2,1)S(1)}, bf16[256,128]{1,0:T(8,128)(2,1)S(1)}, u32[]{:S(2)}, u32[]{:S(2)}) collective-permute-start(bf16[256,128]{1,0:T(8,128)(2,1)S(1)} %get-tuple-element.40), channel_id=1, source_target_pairs={{0,4},{1,5},{2,6},{3,7},{4,0},{5,1},{6,2},{7,3},{8,12},{9,13},{10,... | collective-permute-start | bytes 196616 | tf_op jit(solution)/shard_map/ppermute | solution.py:41
  23.2 9.6 %collective-permute-start.10 = (bf16[256,128]{1,0:T(8,128)(2,1)S(1)}, bf16[256,128]{1,0:T(8,128)(2,1)S(1)}, u32[]{:S(2)}, u32[]{:S(2)}) collective-permute-start(bf16[256,128]{1,0:T(8,128)(2,1)S(1)} %get-tuple-element.41), channel_id=1, source_target_pairs={{0,20},{1,21},{2,22},{3,23},{4,16},{5,17},{6,18},{7,19},{8,28},{9,... | collective-permute-start | bytes 196616 | tf_op jit(solution)/shard_map/ppermute | solution.py:41
  26.7 6.1 %collective-permute-start.11 = (bf16[256,128]{1,0:T(8,128)(2,1)S(1)}, bf16[256,128]{1,0:T(8,128)(2,1)S(1)}, u32[]{:S(2)}, u32[]{:S(2)}) collective-permute-start(bf16[256,128]{1,0:T(8,128)(2,1)S(1)} %get-tuple-element.42), channel_id=1, source_target_pairs={{0,8},{1,9},{2,10},{3,11},{4,12},{5,13},{6,14},{7,15},{8,0},{9,1},... | collective-permute-start | bytes 196616 | tf_op jit(solution)/shard_map/ppermute | solution.py:41
  26.7 6.2 %collective-permute-start.12 = (bf16[256,128]{1,0:T(8,128)(2,1)S(1)}, bf16[256,128]{1,0:T(8,128)(2,1)S(1)}, u32[]{:S(2)}, u32[]{:S(2)}) collective-permute-start(bf16[256,128]{1,0:T(8,128)(2,1)S(1)} %get-tuple-element.43), channel_id=1, source_target_pairs={{0,24},{1,25},{2,26},{3,27},{4,28},{5,29},{6,30},{7,31},{8,16},{9,... | collective-permute-start | bytes 196616 | tf_op jit(solution)/shard_map/ppermute | solution.py:41
  28.9 5.2 %collective-permute-start.13 = (bf16[256,128]{1,0:T(8,128)(2,1)S(1)}, bf16[256,128]{1,0:T(8,128)(2,1)S(1)}, u32[]{:S(2)}, u32[]{:S(2)}) collective-permute-start(bf16[256,128]{1,0:T(8,128)(2,1)S(1)} %get-tuple-element.44), channel_id=1, source_target_pairs={{0,12},{1,13},{2,14},{3,15},{4,8},{5,9},{6,10},{7,11},{8,4},{9,5},... | collective-permute-start | bytes 196616 | tf_op jit(solution)/shard_map/ppermute | solution.py:41
  28.9 7.0 %collective-permute-start.7 = (bf16[256,128]{1,0:T(8,128)(2,1)S(1)}, bf16[256,128]{1,0:T(8,128)(2,1)S(1)}, u32[]{:S(2)}, u32[]{:S(2)}) collective-permute-start(bf16[256,128]{1,0:T(8,128)(2,1)S(1)} %get-tuple-element.37), channel_id=1, source_target_pairs={{0,28},{1,29},{2,30},{3,31},{4,24},{5,25},{6,26},{7,27},{8,20},{9,... | collective-permute-start | bytes 196616 | tf_op jit(solution)/shard_map/ppermute | solution.py:41

commit v9 on v8

--- a/solution.py
+++ b/solution.py
@@ -14,7 +14,7 @@
 TILE = 16
 SIDE = LANES // GROUP
 GATHER = ((6, 1, 4, 2, 5, 3, 7), (6, 1, 4, 2, 5, 3, 7))
-RETURN = ((4, 1, 5, 2, 6, 3, 7), (4, 1, 5, 2, 6, 3, 7))
+RETURN = ((4, 1, 7, 2, 6, 3, 5), (4, 1, 7, 2, 6, 3, 5))
 CHUNKS = 2
 EARLY = 7
 AHEAD = 4

time: 36.1 us -> 35.8 us (level)
  starting transfers between devices: 21.5 us -> 20.7 us
  waiting for transfers between devices: 8.14 us -> 8.63 us
    ppermute x14, starting transfers between devices: 21.5 us -> 20.7 us  [exchange(): got.append(lax.ppermute(block, ('ctx', 'ch'), pairs))]
    ppermute x14, waiting for transfers between devices: 8.14 us -> 8.63 us  [exchange(): got.append(lax.ppermute(block, ('ctx', 'ch'), pairs))]
  transfers between devices with their start and end apart: 14 -> 14, of which waited for: 7 -> 6; matrix products, arithmetic and copies ran while one was open for 0% -> 0% of each run, Pallas kernels for 6% -> 6%
where the time goes in v9:
time: 35.8 us; the launch traced here: 35.6 us
  starting transfers between devices  20.7 us (58%)
  waiting for transfers between devices  8.63 us (24%)
  Pallas kernels  6.22 us (17%)
    ppermute x14, starting transfers between devices, exchange(): got.append(lax.ppermute(block, ('ctx', 'ch'), pairs))  20.7 us
    ppermute x14, waiting for transfers between devices, exchange(): got.append(lax.ppermute(block, ('ctx', 'ch'), pairs))  8.63 us
    pallas_call x1, Pallas kernels, per_device(): pl.pallas_call(mix_kernel, out_shape=[jax.ShapeDtypeStruct((halves * BLOC...  2.84 us
    pallas_call x1, Pallas kernels, per_device(): pl.pallas_call(lambda *refs: conv_kernel(sources, *refs), out_shape=[jax....  1.17 us
    pallas_call x1, Pallas kernels, per_device(): pl.pallas_call(early_kernel, out_shape=prepared, in_specs=[whole] * EARLY...  1.14 us
    pallas_call x2, Pallas kernels, per_device(): pl.pallas_call(functools.partial(gate_kernel, rounds), out_shape=jax.Shap...  1.07 us
  transfers between devices with their start and end apart: 14, of which 6 were waited for; matrix products, arithmetic and copies ran while one was open for 0% of the time, Pallas kernels for 6%

profile of v9, /device:TPU:0, one launch (start us, length us, event | category | flops | bytes accessed | tf_op | source)
XLA Modules:
  0.0 35.6 jit_solution(5670865747164007822)
XLA Ops:
  0.0 0.0 copy-start
  0.0 0.0 copy-start.1
  0.0 2.8 %shard_map.55 = (bf16[272,128]{1,0:T(8,128)(2,1)S(1)}, bf16[272,128]{1,0:T(8,128)(2,1)S(1)}, bf16[272,128]{1,0:T(8,128)(2,1)S(1)}, bf16[272,128]{1,0:T(8,128)(2,...) custom-call(bf16[128,2048]{1,0:T(8,128)(2,1)} %key_hbm.1, ...), custom_call_target="tpu_custom_call" | custom-call | tf_op jit(solution)/shard_map/pallas_call | solution.py:225
  2.9 3.8 %collective-permute-start.1 = (bf16[272,128]{1,0:T(8,128)(2,1)S(1)}, bf16[272,128]{1,0:T(8,128)(2,1)S(1)}, u32[]{:S(2)}, u32[]{:S(2)}) collective-permute-start(bf16[272,128]{1,0:T(8,128)(2,1)S(1)} %get-tuple-element.29), channel_id=1, source_target_pairs={{0,24},{1,25},{2,26},{3,27},{4,28},{5,29},{6,30},{7,31},{8,16},{9,... | collective-permute-start | bytes 208904 | tf_op jit(solution)/shard_map/ppermute | solution.py:41
  6.7 1.5 %collective-permute-start.2 = (bf16[272,128]{1,0:T(8,128)(2,1)S(1)}, bf16[272,128]{1,0:T(8,128)(2,1)S(1)}, u32[]{:S(2)}, u32[]{:S(2)}) collective-permute-start(bf16[272,128]{1,0:T(8,128)(2,1)S(1)} %get-tuple-element.30), channel_id=1, source_target_pairs={{0,4},{1,5},{2,6},{3,7},{4,0},{5,1},{6,2},{7,3},{8,12},{9,13},{10,... | collective-permute-start | bytes 208904 | tf_op jit(solution)/shard_map/ppermute | solution.py:41
  8.2 0.0 collective-permute-start.3
  8.2 0.8 %collective-permute-start.4 = (bf16[272,128]{1,0:T(8,128)(2,1)S(1)}, bf16[272,128]{1,0:T(8,128)(2,1)S(1)}, u32[]{:S(2)}, u32[]{:S(2)}) collective-permute-start(bf16[272,128]{1,0:T(8,128)(2,1)S(1)} %get-tuple-element.32), channel_id=1, source_target_pairs={{0,8},{1,9},{2,10},{3,11},{4,12},{5,13},{6,14},{7,15},{8,0},{9,1},... | collective-permute-start | bytes 208904 | tf_op jit(solution)/shard_map/ppermute | solution.py:41
  9.0 2.1 %collective-permute-start.5 = (bf16[272,128]{1,0:T(8,128)(2,1)S(1)}, bf16[272,128]{1,0:T(8,128)(2,1)S(1)}, u32[]{:S(2)}, u32[]{:S(2)}) collective-permute-start(bf16[272,128]{1,0:T(8,128)(2,1)S(1)} %get-tuple-element.33), channel_id=1, source_target_pairs={{0,20},{1,21},{2,22},{3,23},{4,16},{5,17},{6,18},{7,19},{8,28},{9,... | collective-permute-start | bytes 208904 | tf_op jit(solution)/shard_map/ppermute | solution.py:41
  11.1 0.0 collective-permute-done.1.refs_1_
  11.1 3.0 %collective-permute-start.6 = (bf16[272,128]{1,0:T(8,128)(2,1)S(1)}, bf16[272,128]{1,0:T(8,128)(2,1)S(1)}, u32[]{:S(2)}, u32[]{:S(2)}) collective-permute-start(bf16[272,128]{1,0:T(8,128)(2,1)S(1)} %get-tuple-element.34), channel_id=1, source_target_pairs={{0,12},{1,13},{2,14},{3,15},{4,8},{5,9},{6,10},{7,11},{8,4},{9,5},... | collective-permute-start | bytes 208904 | tf_op jit(solution)/shard_map/ppermute | solution.py:41
  14.0 0.0 collective-permute-done.2.refs_2_
  14.0 0.5 %collective-permute-start = (bf16[272,128]{1,0:T(8,128)(2,1)S(1)}, bf16[272,128]{1,0:T(8,128)(2,1)S(1)}, u32[]{:S(2)}, u32[]{:S(2)}) collective-permute-start(bf16[272,128]{1,0:T(8,128)(2,1)S(1)} %get-tuple-element.27), channel_id=1, source_target_pairs={{0,28},{1,29},{2,30},{3,31},{4,24},{5,25},{6,26},{7,27},{8,20},{9,... | collective-permute-start | bytes 208904 | tf_op jit(solution)/shard_map/ppermute | solution.py:41
  14.5 0.3 collective-permute-done.3.refs_3_
  14.8 0.0 collective-permute-done.4.refs_4_
  14.8 2.1 %collective-permute-done.5.refs_5_ = bf16[272,128]{1,0:T(8,128)(2,1)S(1)} collective-permute-done((bf16[272,128]{1,0:T(8,128)(2,1)S(1)}, bf16[272,128]{1,0:T(8,128)(2,1)S(1)}, u32[]{:S(2)}, u32[]{:S(2)}) %collective-permute-start.5) | collective-permute-done | bytes 69664 | tf_op jit(solution)/shard_map/ppermute | solution.py:41
  16.9 0.0 collective-permute-done.6.refs_6_
  16.9 1.1 %shard_map.56 = (bf16[8,16,128,128]{3,2,1,0:T(8,128)(2,1)S(1)}, bf16[8,256,128]{2,1,0:T(8,128)(2,1)S(1)}) custom-call(bf16[272,128]{1,0:T(8,128)(2,1)S(1)} %get-tuple-element.28.refs_0_, bf16[272,128]{1,0:T(8,128)(2,1)S(1)} %collective-permute-done.1.refs_1_, bf16[272,128]{1,0:T(8,128)(2,1)S(1)} %collective-permute-done.2.refs_2_, ...), custom_call_target="tpu_custom_call" | custom-call | bytes 8388608 | tf_op jit(solution)/shard_map/pallas_call | solution.py:251
  18.0 3.0 %collective-permute-done.refs_0_ = bf16[272,128]{1,0:T(8,128)(2,1)S(1)} collective-permute-done((bf16[272,128]{1,0:T(8,128)(2,1)S(1)}, bf16[272,128]{1,0:T(8,128)(2,1)S(1)}, u32[]{:S(2)}, u32[]{:S(2)}) %collective-permute-start) | collective-permute-done | bytes 69664 | tf_op jit(solution)/shard_map/ppermute | solution.py:41
  21.0 1.2 %shard_map.57 = (bf16[256,128]{1,0:T(8,128)(2,1)S(1)}, bf16[256,128]{1,0:T(8,128)(2,1)S(1)}, bf16[256,128]{1,0:T(8,128)(2,1)S(1)}, bf16[256,128]{1,0:T(8,128)(2,...) custom-call(bf16[272,128]{1,0:T(8,128)(2,1)S(1)} %collective-permute, ...), custom_call_target="tpu_custom_call", output_to_operand_aliasing={{8}: (1, {}), {9}: (2, {})} | custom-call | tf_op jit(solution)/shard_map/pallas_call | solution.py:261
  22.2 0.4 %collective-permute-start.8 = (bf16[256,128]{1,0:T(8,128)(2,1)S(1)}, bf16[256,128]{1,0:T(8,128)(2,1)S(1)}, u32[]{:S(2)}, u32[]{:S(2)}) collective-permute-start(bf16[256,128]{1,0:T(8,128)(2,1)S(1)} %get-tuple-element.39), channel_id=1, source_target_pairs={{0,16},{1,17},{2,18},{3,19},{4,20},{5,21},{6,22},{7,23},{8,24},{9,... | collective-permute-start | bytes 196616 | tf_op jit(solution)/shard_map/ppermute | solution.py:41
  22.6 0.6 %collective-permute-start.9 = (bf16[256,128]{1,0:T(8,128)(2,1)S(1)}, bf16[256,128]{1,0:T(8,128)(2,1)S(1)}, u32[]{:S(2)}, u32[]{:S(2)}) collective-permute-start(bf16[256,128]{1,0:T(8,128)(2,1)S(1)} %get-tuple-element.40), channel_id=1, source_target_pairs={{0,4},{1,5},{2,6},{3,7},{4,0},{5,1},{6,2},{7,3},{8,12},{9,13},{10,... | collective-permute-start | bytes 196616 | tf_op jit(solution)/shard_map/ppermute | solution.py:41
  23.2 1.7 %collective-permute-start.10 = (bf16[256,128]{1,0:T(8,128)(2,1)S(1)}, bf16[256,128]{1,0:T(8,128)(2,1)S(1)}, u32[]{:S(2)}, u32[]{:S(2)}) collective-permute-start(bf16[256,128]{1,0:T(8,128)(2,1)S(1)} %get-tuple-element.41), channel_id=1, source_target_pairs={{0,28},{1,29},{2,30},{3,31},{4,24},{5,25},{6,26},{7,27},{8,20},{9,... | collective-permute-start | bytes 196616 | tf_op jit(solution)/shard_map/ppermute | solution.py:41
  24.8 2.4 %collective-permute-start.11 = (bf16[256,128]{1,0:T(8,128)(2,1)S(1)}, bf16[256,128]{1,0:T(8,128)(2,1)S(1)}, u32[]{:S(2)}, u32[]{:S(2)}) collective-permute-start(bf16[256,128]{1,0:T(8,128)(2,1)S(1)} %get-tuple-element.42), channel_id=1, source_target_pairs={{0,8},{1,9},{2,10},{3,11},{4,12},{5,13},{6,14},{7,15},{8,0},{9,1},... | collective-permute-start | bytes 196616 | tf_op jit(solution)/shard_map/ppermute | solution.py:41
  27.2 0.9 %collective-permute-start.12 = (bf16[256,128]{1,0:T(8,128)(2,1)S(1)}, bf16[256,128]{1,0:T(8,128)(2,1)S(1)}, u32[]{:S(2)}, u32[]{:S(2)}) collective-permute-start(bf16[256,128]{1,0:T(8,128)(2,1)S(1)} %get-tuple-element.43), channel_id=1, source_target_pairs={{0,24},{1,25},{2,26},{3,27},{4,28},{5,29},{6,30},{7,31},{8,16},{9,... | collective-permute-start | bytes 196616 | tf_op jit(solution)/shard_map/ppermute | solution.py:41
  28.1 1.3 %collective-permute-done.8.refs_1_ = bf16[256,128]{1,0:T(8,128)(2,1)S(1)} collective-permute-done((bf16[256,128]{1,0:T(8,128)(2,1)S(1)}, bf16[256,128]{1,0:T(8,128)(2,1)S(1)}, u32[]{:S(2)}, u32[]{:S(2)}) %collective-permute-start.8) | collective-permute-done | bytes 65568 | tf_op jit(solution)/shard_map/ppermute | solution.py:41
  29.3 0.0 collective-permute-start.13
  29.4 0.0 collective-permute-done.9.refs_2_
  29.4 3.2 %collective-permute-start.7 = (bf16[256,128]{1,0:T(8,128)(2,1)S(1)}, bf16[256,128]{1,0:T(8,128)(2,1)S(1)}, u32[]{:S(2)}, u32[]{:S(2)}) collective-permute-start(bf16[256,128]{1,0:T(8,128)(2,1)S(1)} %get-tuple-element.37), channel_id=1, source_target_pairs={{0,20},{1,21},{2,22},{3,23},{4,16},{5,17},{6,18},{7,19},{8,28},{9,... | collective-permute-start | bytes 196616 | tf_op jit(solution)/shard_map/ppermute | solution.py:41
  32.5 0.0 collective-permute-done.10.refs_3_
  32.5 0.0 collective-permute-done.11.refs_4_
  32.5 0.9 %collective-permute-done.12.refs_5_ = bf16[256,128]{1,0:T(8,128)(2,1)S(1)} collective-permute-done((bf16[256,128]{1,0:T(8,128)(2,1)S(1)}, bf16[256,128]{1,0:T(8,128)(2,1)S(1)}, u32[]{:S(2)}, u32[]{:S(2)}) %collective-permute-start.12) | collective-permute-done | bytes 65568 | tf_op jit(solution)/shard_map/ppermute | solution.py:41
  33.5 1.1 %collective-permute-done.13.refs_6_ = bf16[256,128]{1,0:T(8,128)(2,1)S(1)} collective-permute-done((bf16[256,128]{1,0:T(8,128)(2,1)S(1)}, bf16[256,128]{1,0:T(8,128)(2,1)S(1)}, u32[]{:S(2)}, u32[]{:S(2)}) %collective-permute-start.13) | collective-permute-done | bytes 65568 | tf_op jit(solution)/shard_map/ppermute | solution.py:41
  34.5 0.0 copy-done
  34.5 0.0 copy-done.1
  34.5 1.0 %shard_map.58.refs_1_ = bf16[128,2048]{1,0:T(8,128)(2,1)} custom-call(bf16[128,2048]{1,0:T(8,128)(2,1)S(1)} %copy-done, f32[1,2048]{1,0:T(1,128)S(1)} %bitcast.1, bf16[128,2048]{1,0:T(8,128)(2,1)S(1)} %get-tuple-element.25.mixed_ref, bf16[2048,128]{1,0:T(8,128)(2,1)S(1)} %get-tuple-element.26.home_ref, bf16[256,128]{1,0:T(8,128)(2,1)S(1)} %get-tuple-element.38.refs_0_, ...), custom_call_target="tpu_custom_call" | custom-call | tf_op jit(solution)/shard_map/pallas_call | solution.py:282
  35.5 0.0 collective-permute-done.7.refs_0_
  35.5 0.1 shard_map.59
Async XLA Ops:
  0.0 34.5 %copy-start = (bf16[128,2048]{1,0:T(8,128)(2,1)S(1)}, bf16[128,2048]{1,0:T(8,128)(2,1)}, u32[]{:S(2)}) copy-start(bf16[128,2048]{1,0:T(8,128)(2,1)} %query_ref.3) | copy-start | bytes 1572868
  0.0 34.5 %copy-start.1 = (f32[2048]{0:T(1024)S(1)}, f32[2048]{0:T(1024)}, u32[]{:S(2)}) copy-start(f32[2048]{0:T(1024)} %param.9) | copy-start | bytes 24580
  2.9 8.2 %collective-permute-start.1 = (bf16[272,128]{1,0:T(8,128)(2,1)S(1)}, bf16[272,128]{1,0:T(8,128)(2,1)S(1)}, u32[]{:S(2)}, u32[]{:S(2)}) collective-permute-start(bf16[272,128]{1,0:T(8,128)(2,1)S(1)} %get-tuple-element.29), channel_id=1, source_target_pairs={{0,24},{1,25},{2,26},{3,27},{4,28},{5,29},{6,30},{7,31},{8,16},{9,... | collective-permute-start | bytes 208904 | tf_op jit(solution)/shard_map/ppermute | solution.py:41
  6.7 7.3 %collective-permute-start.2 = (bf16[272,128]{1,0:T(8,128)(2,1)S(1)}, bf16[272,128]{1,0:T(8,128)(2,1)S(1)}, u32[]{:S(2)}, u32[]{:S(2)}) collective-permute-start(bf16[272,128]{1,0:T(8,128)(2,1)S(1)} %get-tuple-element.30), channel_id=1, source_target_pairs={{0,4},{1,5},{2,6},{3,7},{4,0},{5,1},{6,2},{7,3},{8,12},{9,13},{10,... | collective-permute-start | bytes 208904 | tf_op jit(solution)/shard_map/ppermute | solution.py:41
  8.2 6.6 %collective-permute-start.3 = (bf16[272,128]{1,0:T(8,128)(2,1)S(1)}, bf16[272,128]{1,0:T(8,128)(2,1)S(1)}, u32[]{:S(2)}, u32[]{:S(2)}) collective-permute-start(bf16[272,128]{1,0:T(8,128)(2,1)S(1)} %get-tuple-element.31), channel_id=1, source_target_pairs={{0,16},{1,17},{2,18},{3,19},{4,20},{5,21},{6,22},{7,23},{8,24},{9,... | collective-permute-start | bytes 208904 | tf_op jit(solution)/shard_map/ppermute | solution.py:41
  8.2 6.6 %collective-permute-start.4 = (bf16[272,128]{1,0:T(8,128)(2,1)S(1)}, bf16[272,128]{1,0:T(8,128)(2,1)S(1)}, u32[]{:S(2)}, u32[]{:S(2)}) collective-permute-start(bf16[272,128]{1,0:T(8,128)(2,1)S(1)} %get-tuple-element.32), channel_id=1, source_target_pairs={{0,8},{1,9},{2,10},{3,11},{4,12},{5,13},{6,14},{7,15},{8,0},{9,1},... | collective-permute-start | bytes 208904 | tf_op jit(solution)/shard_map/ppermute | solution.py:41
  9.0 7.9 %collective-permute-start.5 = (bf16[272,128]{1,0:T(8,128)(2,1)S(1)}, bf16[272,128]{1,0:T(8,128)(2,1)S(1)}, u32[]{:S(2)}, u32[]{:S(2)}) collective-permute-start(bf16[272,128]{1,0:T(8,128)(2,1)S(1)} %get-tuple-element.33), channel_id=1, source_target_pairs={{0,20},{1,21},{2,22},{3,23},{4,16},{5,17},{6,18},{7,19},{8,28},{9,... | collective-permute-start | bytes 208904 | tf_op jit(solution)/shard_map/ppermute | solution.py:41
  11.1 5.8 %collective-permute-start.6 = (bf16[272,128]{1,0:T(8,128)(2,1)S(1)}, bf16[272,128]{1,0:T(8,128)(2,1)S(1)}, u32[]{:S(2)}, u32[]{:S(2)}) collective-permute-start(bf16[272,128]{1,0:T(8,128)(2,1)S(1)} %get-tuple-element.34), channel_id=1, source_target_pairs={{0,12},{1,13},{2,14},{3,15},{4,8},{5,9},{6,10},{7,11},{8,4},{9,5},... | collective-permute-start | bytes 208904 | tf_op jit(solution)/shard_map/ppermute | solution.py:41
  14.0 7.0 %collective-permute-start = (bf16[272,128]{1,0:T(8,128)(2,1)S(1)}, bf16[272,128]{1,0:T(8,128)(2,1)S(1)}, u32[]{:S(2)}, u32[]{:S(2)}) collective-permute-start(bf16[272,128]{1,0:T(8,128)(2,1)S(1)} %get-tuple-element.27), channel_id=1, source_target_pairs={{0,28},{1,29},{2,30},{3,31},{4,24},{5,25},{6,26},{7,27},{8,20},{9,... | collective-permute-start | bytes 208904 | tf_op jit(solution)/shard_map/ppermute | solution.py:41
  22.2 7.1 %collective-permute-start.8 = (bf16[256,128]{1,0:T(8,128)(2,1)S(1)}, bf16[256,128]{1,0:T(8,128)(2,1)S(1)}, u32[]{:S(2)}, u32[]{:S(2)}) collective-permute-start(bf16[256,128]{1,0:T(8,128)(2,1)S(1)} %get-tuple-element.39), channel_id=1, source_target_pairs={{0,16},{1,17},{2,18},{3,19},{4,20},{5,21},{6,22},{7,23},{8,24},{9,... | collective-permute-start | bytes 196616 | tf_op jit(solution)/shard_map/ppermute | solution.py:41
  22.6 6.8 %collective-permute-start.9 = (bf16[256,128]{1,0:T(8,128)(2,1)S(1)}, bf16[256,128]{1,0:T(8,128)(2,1)S(1)}, u32[]{:S(2)}, u32[]{:S(2)}) collective-permute-start(bf16[256,128]{1,0:T(8,128)(2,1)S(1)} %get-tuple-element.40), channel_id=1, source_target_pairs={{0,4},{1,5},{2,6},{3,7},{4,0},{5,1},{6,2},{7,3},{8,12},{9,13},{10,... | collective-permute-start | bytes 196616 | tf_op jit(solution)/shard_map/ppermute | solution.py:41
  23.2 9.4 %collective-permute-start.10 = (bf16[256,128]{1,0:T(8,128)(2,1)S(1)}, bf16[256,128]{1,0:T(8,128)(2,1)S(1)}, u32[]{:S(2)}, u32[]{:S(2)}) collective-permute-start(bf16[256,128]{1,0:T(8,128)(2,1)S(1)} %get-tuple-element.41), channel_id=1, source_target_pairs={{0,28},{1,29},{2,30},{3,31},{4,24},{5,25},{6,26},{7,27},{8,20},{9,... | collective-permute-start | bytes 196616 | tf_op jit(solution)/shard_map/ppermute | solution.py:41
  24.8 7.7 %collective-permute-start.11 = (bf16[256,128]{1,0:T(8,128)(2,1)S(1)}, bf16[256,128]{1,0:T(8,128)(2,1)S(1)}, u32[]{:S(2)}, u32[]{:S(2)}) collective-permute-start(bf16[256,128]{1,0:T(8,128)(2,1)S(1)} %get-tuple-element.42), channel_id=1, source_target_pairs={{0,8},{1,9},{2,10},{3,11},{4,12},{5,13},{6,14},{7,15},{8,0},{9,1},... | collective-permute-start | bytes 196616 | tf_op jit(solution)/shard_map/ppermute | solution.py:41
  27.2 6.2 %collective-permute-start.12 = (bf16[256,128]{1,0:T(8,128)(2,1)S(1)}, bf16[256,128]{1,0:T(8,128)(2,1)S(1)}, u32[]{:S(2)}, u32[]{:S(2)}) collective-permute-start(bf16[256,128]{1,0:T(8,128)(2,1)S(1)} %get-tuple-element.43), channel_id=1, source_target_pairs={{0,24},{1,25},{2,26},{3,27},{4,28},{5,29},{6,30},{7,31},{8,16},{9,... | collective-permute-start | bytes 196616 | tf_op jit(solution)/shard_map/ppermute | solution.py:41
  29.3 5.2 %collective-permute-start.13 = (bf16[256,128]{1,0:T(8,128)(2,1)S(1)}, bf16[256,128]{1,0:T(8,128)(2,1)S(1)}, u32[]{:S(2)}, u32[]{:S(2)}) collective-permute-start(bf16[256,128]{1,0:T(8,128)(2,1)S(1)} %get-tuple-element.44), channel_id=1, source_target_pairs={{0,12},{1,13},{2,14},{3,15},{4,8},{5,9},{6,10},{7,11},{8,4},{9,5},... | collective-permute-start | bytes 196616 | tf_op jit(solution)/shard_map/ppermute | solution.py:41
  29.4 6.2 %collective-permute-start.7 = (bf16[256,128]{1,0:T(8,128)(2,1)S(1)}, bf16[256,128]{1,0:T(8,128)(2,1)S(1)}, u32[]{:S(2)}, u32[]{:S(2)}) collective-permute-start(bf16[256,128]{1,0:T(8,128)(2,1)S(1)} %get-tuple-element.37), channel_id=1, source_target_pairs={{0,20},{1,21},{2,22},{3,23},{4,16},{5,17},{6,18},{7,19},{8,28},{9,... | collective-permute-start | bytes 196616 | tf_op jit(solution)/shard_map/ppermute | solution.py:41

commit v10 on v9

--- a/solution.py
+++ b/solution.py
@@ -17,7 +17,6 @@
 RETURN = ((4, 1, 7, 2, 6, 3, 5), (4, 1, 7, 2, 6, 3, 5))
 CHUNKS = 2
 EARLY = 7
-AHEAD = 4
 UNROLL = 8
 FIRST = 7
 SMALL = pltpu.CompilerParams(vmem_limit_bytes=16 * 1024 * 1024)
@@ -130,28 +129,23 @@
 
 def conv_kernel(sources, *refs):
     late_ref, *earlier_refs = refs[: 1 + (sources - 1) * LAGS]
-    *conv_refs, circulants, blocks, taps, results, earlier = refs[1 + (sources - 1) * LAGS + 2 :]
+    circulants, early_blocks, *conv_refs, taps, results, blocks, earlier = refs[1 + (sources - 1) * LAGS :]
     width = blocks.shape[1]
     late = partners(GATHER)[EARLY]
     taps[...] = late_ref[width : width + TILE, :].astype(jnp.float32)
+    blocks[...] = early_blocks[...]
     blocks[late] = late_ref[0:width, :]
     for partner, earlier_ref in zip(partners(GATHER), earlier_refs):
         earlier[partner] = earlier_ref[0:width, :]
 
-    def add_late(group):
-        circulants[late, group] = circulant(taps[group : group + 1, :])
-
-    for group in range(AHEAD):
-        add_late(group)
     causal = later_lanes()
     for group in range(TILE):
-        if group + AHEAD < TILE:
-            add_late(group + AHEAD)
+        newest = circulant(taps[group : group + 1, :])
         rows = slice(group * GROUP, (group + 1) * GROUP)
         before = jnp.zeros((BLOCK, LANES), jnp.bfloat16)
         filters, signals = [], []
         for lag in range(LAGS):
-            turned = circulants[lag, group]
+            turned = jnp.where(lag == late, newest, circulants[lag, group])
             filters.append(jnp.where(causal, turned, before))
             before = turned
             signal = [blocks[block, rows, :] for block in range(LAGS - lag)]
@@ -258,17 +252,17 @@
         compiler_params=SMALL,
     )(*got[:EARLY])
     late = got[EARLY:]
-    *conv, _, _ = pl.pallas_call(
+    conv = pl.pallas_call(
         lambda *refs: conv_kernel(sources, *refs),
-        out_shape=[jax.ShapeDtypeStruct((halves * BLOCK, LANES), jnp.bfloat16)] * LAGS + prepared,
+        out_shape=[jax.ShapeDtypeStruct((halves * BLOCK, LANES), jnp.bfloat16)] * LAGS,
         in_specs=[whole] * (len(late) + 2),
-        out_specs=[whole] * (LAGS + 2),
+        out_specs=[whole] * LAGS,
         scratch_shapes=[
             pltpu.VMEM((TILE, LANES), jnp.float32),
             pltpu.VMEM((TILE, BLOCK, LANES), jnp.bfloat16),
             pltpu.VMEM((LAGS, halves * BLOCK, LANES), jnp.bfloat16),
+            pltpu.VMEM((LAGS, halves * BLOCK, LANES), jnp.bfloat16),
         ],
-        input_output_aliases={len(late): LAGS, len(late) + 1: LAGS + 1},
         compiler_params=SMALL,
     )(*late, *early)
     back = exchange(conv, RETURN)

time: 35.8 us -> 35.7 us (level)
  no operation moved by 1% of the time
where the time goes in v10:
time: 35.7 us; the launch traced here: 35.5 us
  starting transfers between devices  20.7 us (58%)
  waiting for transfers between devices  8.63 us (24%)
  Pallas kernels  6.14 us (17%)
    ppermute x14, starting transfers between devices, exchange(): got.append(lax.ppermute(block, ('ctx', 'ch'), pairs))  20.7 us
    ppermute x14, waiting for transfers between devices, exchange(): got.append(lax.ppermute(block, ('ctx', 'ch'), pairs))  8.63 us
    pallas_call x1, Pallas kernels, per_device(): pl.pallas_call(mix_kernel, out_shape=[jax.ShapeDtypeStruct((halves * BLOC...  2.84 us
    pallas_call x1, Pallas kernels, per_device(): pl.pallas_call(early_kernel, out_shape=prepared, in_specs=[whole] * EARLY...  1.14 us
    pallas_call x1, Pallas kernels, per_device(): pl.pallas_call(lambda *refs: conv_kernel(sources, *refs), out_shape=[jax....  1.08 us
    pallas_call x2, Pallas kernels, per_device(): pl.pallas_call(functools.partial(gate_kernel, rounds), out_shape=jax.Shap...  1.07 us
  transfers between devices with their start and end apart: 14, of which 6 were waited for; matrix products, arithmetic and copies ran while one was open for 0% of the time, Pallas kernels for 6%

profile of v10, /device:TPU:0, one launch (start us, length us, event | category | flops | bytes accessed | tf_op | source)
XLA Modules:
  0.0 35.5 jit_solution(4042459279665920705)
XLA Ops:
  0.0 0.0 copy-start
  0.0 0.0 copy-start.1
  0.0 2.8 %shard_map.55 = (bf16[272,128]{1,0:T(8,128)(2,1)S(1)}, bf16[272,128]{1,0:T(8,128)(2,1)S(1)}, bf16[272,128]{1,0:T(8,128)(2,1)S(1)}, bf16[272,128]{1,0:T(8,128)(2,...) custom-call(bf16[128,2048]{1,0:T(8,128)(2,1)} %key_hbm.1, ...), custom_call_target="tpu_custom_call" | custom-call | tf_op jit(solution)/shard_map/pallas_call | solution.py:219
  2.9 3.8 %collective-permute-start.1 = (bf16[272,128]{1,0:T(8,128)(2,1)S(1)}, bf16[272,128]{1,0:T(8,128)(2,1)S(1)}, u32[]{:S(2)}, u32[]{:S(2)}) collective-permute-start(bf16[272,128]{1,0:T(8,128)(2,1)S(1)} %get-tuple-element.29), channel_id=1, source_target_pairs={{0,24},{1,25},{2,26},{3,27},{4,28},{5,29},{6,30},{7,31},{8,16},{9,... | collective-permute-start | bytes 208904 | tf_op jit(solution)/shard_map/ppermute | solution.py:40
  6.7 1.5 %collective-permute-start.2 = (bf16[272,128]{1,0:T(8,128)(2,1)S(1)}, bf16[272,128]{1,0:T(8,128)(2,1)S(1)}, u32[]{:S(2)}, u32[]{:S(2)}) collective-permute-start(bf16[272,128]{1,0:T(8,128)(2,1)S(1)} %get-tuple-element.30), channel_id=1, source_target_pairs={{0,4},{1,5},{2,6},{3,7},{4,0},{5,1},{6,2},{7,3},{8,12},{9,13},{10,... | collective-permute-start | bytes 208904 | tf_op jit(solution)/shard_map/ppermute | solution.py:40
  8.2 0.0 collective-permute-start.3
  8.2 0.8 %collective-permute-start.4 = (bf16[272,128]{1,0:T(8,128)(2,1)S(1)}, bf16[272,128]{1,0:T(8,128)(2,1)S(1)}, u32[]{:S(2)}, u32[]{:S(2)}) collective-permute-start(bf16[272,128]{1,0:T(8,128)(2,1)S(1)} %get-tuple-element.32), channel_id=1, source_target_pairs={{0,8},{1,9},{2,10},{3,11},{4,12},{5,13},{6,14},{7,15},{8,0},{9,1},... | collective-permute-start | bytes 208904 | tf_op jit(solution)/shard_map/ppermute | solution.py:40
  9.0 2.1 %collective-permute-start.5 = (bf16[272,128]{1,0:T(8,128)(2,1)S(1)}, bf16[272,128]{1,0:T(8,128)(2,1)S(1)}, u32[]{:S(2)}, u32[]{:S(2)}) collective-permute-start(bf16[272,128]{1,0:T(8,128)(2,1)S(1)} %get-tuple-element.33), channel_id=1, source_target_pairs={{0,20},{1,21},{2,22},{3,23},{4,16},{5,17},{6,18},{7,19},{8,28},{9,... | collective-permute-start | bytes 208904 | tf_op jit(solution)/shard_map/ppermute | solution.py:40
  11.1 0.0 collective-permute-done.1.refs_1_
  11.1 3.0 %collective-permute-start.6 = (bf16[272,128]{1,0:T(8,128)(2,1)S(1)}, bf16[272,128]{1,0:T(8,128)(2,1)S(1)}, u32[]{:S(2)}, u32[]{:S(2)}) collective-permute-start(bf16[272,128]{1,0:T(8,128)(2,1)S(1)} %get-tuple-element.34), channel_id=1, source_target_pairs={{0,12},{1,13},{2,14},{3,15},{4,8},{5,9},{6,10},{7,11},{8,4},{9,5},... | collective-permute-start | bytes 208904 | tf_op jit(solution)/shard_map/ppermute | solution.py:40
  14.0 0.0 collective-permute-done.2.refs_2_
  14.0 0.5 %collective-permute-start = (bf16[272,128]{1,0:T(8,128)(2,1)S(1)}, bf16[272,128]{1,0:T(8,128)(2,1)S(1)}, u32[]{:S(2)}, u32[]{:S(2)}) collective-permute-start(bf16[272,128]{1,0:T(8,128)(2,1)S(1)} %get-tuple-element.27), channel_id=1, source_target_pairs={{0,28},{1,29},{2,30},{3,31},{4,24},{5,25},{6,26},{7,27},{8,20},{9,... | collective-permute-start | bytes 208904 | tf_op jit(solution)/shard_map/ppermute | solution.py:40
  14.5 0.3 collective-permute-done.3.refs_3_
  14.8 0.0 collective-permute-done.4.refs_4_
  14.8 2.1 %collective-permute-done.5.refs_5_ = bf16[272,128]{1,0:T(8,128)(2,1)S(1)} collective-permute-done((bf16[272,128]{1,0:T(8,128)(2,1)S(1)}, bf16[272,128]{1,0:T(8,128)(2,1)S(1)}, u32[]{:S(2)}, u32[]{:S(2)}) %collective-permute-start.5) | collective-permute-done | bytes 69664 | tf_op jit(solution)/shard_map/ppermute | solution.py:40
  16.9 0.0 collective-permute-done.6.refs_6_
  16.9 1.1 %shard_map.56 = (bf16[8,16,128,128]{3,2,1,0:T(8,128)(2,1)S(1)}, bf16[8,256,128]{2,1,0:T(8,128)(2,1)S(1)}) custom-call(bf16[272,128]{1,0:T(8,128)(2,1)S(1)} %get-tuple-element.28.refs_0_, bf16[272,128]{1,0:T(8,128)(2,1)S(1)} %collective-permute-done.1.refs_1_, bf16[272,128]{1,0:T(8,128)(2,1)S(1)} %collective-permute-done.2.refs_2_, ...), custom_call_target="tpu_custom_call" | custom-call | bytes 8388608 | tf_op jit(solution)/shard_map/pallas_call | solution.py:245
  18.0 3.0 %collective-permute-done.refs_0_ = bf16[272,128]{1,0:T(8,128)(2,1)S(1)} collective-permute-done((bf16[272,128]{1,0:T(8,128)(2,1)S(1)}, bf16[272,128]{1,0:T(8,128)(2,1)S(1)}, u32[]{:S(2)}, u32[]{:S(2)}) %collective-permute-start) | collective-permute-done | bytes 69664 | tf_op jit(solution)/shard_map/ppermute | solution.py:40
  21.0 1.1 %shard_map.57 = (bf16[256,128]{1,0:T(8,128)(2,1)S(1)}, bf16[256,128]{1,0:T(8,128)(2,1)S(1)}, bf16[256,128]{1,0:T(8,128)(2,1)S(1)}, bf16[256,128]{1,0:T(8,128)(2,...) custom-call(bf16[272,128]{1,0:T(8,128)(2,1)S(1)} %collective-permute, ...), custom_call_target="tpu_custom_call" | custom-call | tf_op jit(solution)/shard_map/pallas_call | solution.py:255
  22.1 0.4 %collective-permute-start.8 = (bf16[256,128]{1,0:T(8,128)(2,1)S(1)}, bf16[256,128]{1,0:T(8,128)(2,1)S(1)}, u32[]{:S(2)}, u32[]{:S(2)}) collective-permute-start(bf16[256,128]{1,0:T(8,128)(2,1)S(1)} %get-tuple-element.39), channel_id=1, source_target_pairs={{0,16},{1,17},{2,18},{3,19},{4,20},{5,21},{6,22},{7,23},{8,24},{9,... | collective-permute-start | bytes 196616 | tf_op jit(solution)/shard_map/ppermute | solution.py:40
  22.5 0.6 %collective-permute-start.9 = (bf16[256,128]{1,0:T(8,128)(2,1)S(1)}, bf16[256,128]{1,0:T(8,128)(2,1)S(1)}, u32[]{:S(2)}, u32[]{:S(2)}) collective-permute-start(bf16[256,128]{1,0:T(8,128)(2,1)S(1)} %get-tuple-element.40), channel_id=1, source_target_pairs={{0,4},{1,5},{2,6},{3,7},{4,0},{5,1},{6,2},{7,3},{8,12},{9,13},{10,... | collective-permute-start | bytes 196616 | tf_op jit(solution)/shard_map/ppermute | solution.py:40
  23.1 1.7 %collective-permute-start.10 = (bf16[256,128]{1,0:T(8,128)(2,1)S(1)}, bf16[256,128]{1,0:T(8,128)(2,1)S(1)}, u32[]{:S(2)}, u32[]{:S(2)}) collective-permute-start(bf16[256,128]{1,0:T(8,128)(2,1)S(1)} %get-tuple-element.41), channel_id=1, source_target_pairs={{0,28},{1,29},{2,30},{3,31},{4,24},{5,25},{6,26},{7,27},{8,20},{9,... | collective-permute-start | bytes 196616 | tf_op jit(solution)/shard_map/ppermute | solution.py:40
  24.7 2.4 %collective-permute-start.11 = (bf16[256,128]{1,0:T(8,128)(2,1)S(1)}, bf16[256,128]{1,0:T(8,128)(2,1)S(1)}, u32[]{:S(2)}, u32[]{:S(2)}) collective-permute-start(bf16[256,128]{1,0:T(8,128)(2,1)S(1)} %get-tuple-element.42), channel_id=1, source_target_pairs={{0,8},{1,9},{2,10},{3,11},{4,12},{5,13},{6,14},{7,15},{8,0},{9,1},... | collective-permute-start | bytes 196616 | tf_op jit(solution)/shard_map/ppermute | solution.py:40
  27.1 0.8 %collective-permute-start.12 = (bf16[256,128]{1,0:T(8,128)(2,1)S(1)}, bf16[256,128]{1,0:T(8,128)(2,1)S(1)}, u32[]{:S(2)}, u32[]{:S(2)}) collective-permute-start(bf16[256,128]{1,0:T(8,128)(2,1)S(1)} %get-tuple-element.43), channel_id=1, source_target_pairs={{0,24},{1,25},{2,26},{3,27},{4,28},{5,29},{6,30},{7,31},{8,16},{9,... | collective-permute-start | bytes 196616 | tf_op jit(solution)/shard_map/ppermute | solution.py:40
  28.0 1.3 %collective-permute-done.8.refs_1_ = bf16[256,128]{1,0:T(8,128)(2,1)S(1)} collective-permute-done((bf16[256,128]{1,0:T(8,128)(2,1)S(1)}, bf16[256,128]{1,0:T(8,128)(2,1)S(1)}, u32[]{:S(2)}, u32[]{:S(2)}) %collective-permute-start.8) | collective-permute-done | bytes 65568 | tf_op jit(solution)/shard_map/ppermute | solution.py:40
  29.3 0.0 collective-permute-start.13
  29.3 0.0 collective-permute-done.9.refs_2_
  29.3 3.2 %collective-permute-start.7 = (bf16[256,128]{1,0:T(8,128)(2,1)S(1)}, bf16[256,128]{1,0:T(8,128)(2,1)S(1)}, u32[]{:S(2)}, u32[]{:S(2)}) collective-permute-start(bf16[256,128]{1,0:T(8,128)(2,1)S(1)} %get-tuple-element.37), channel_id=1, source_target_pairs={{0,20},{1,21},{2,22},{3,23},{4,16},{5,17},{6,18},{7,19},{8,28},{9,... | collective-permute-start | bytes 196616 | tf_op jit(solution)/shard_map/ppermute | solution.py:40
  32.4 0.0 collective-permute-done.10.refs_3_
  32.4 0.0 collective-permute-done.11.refs_4_
  32.4 0.9 %collective-permute-done.12.refs_5_ = bf16[256,128]{1,0:T(8,128)(2,1)S(1)} collective-permute-done((bf16[256,128]{1,0:T(8,128)(2,1)S(1)}, bf16[256,128]{1,0:T(8,128)(2,1)S(1)}, u32[]{:S(2)}, u32[]{:S(2)}) %collective-permute-start.12) | collective-permute-done | bytes 65568 | tf_op jit(solution)/shard_map/ppermute | solution.py:40
  33.4 1.1 %collective-permute-done.13.refs_6_ = bf16[256,128]{1,0:T(8,128)(2,1)S(1)} collective-permute-done((bf16[256,128]{1,0:T(8,128)(2,1)S(1)}, bf16[256,128]{1,0:T(8,128)(2,1)S(1)}, u32[]{:S(2)}, u32[]{:S(2)}) %collective-permute-start.13) | collective-permute-done | bytes 65568 | tf_op jit(solution)/shard_map/ppermute | solution.py:40
  34.4 0.0 copy-done
  34.4 0.0 copy-done.1
  34.4 1.0 %shard_map.58.refs_1_ = bf16[128,2048]{1,0:T(8,128)(2,1)} custom-call(bf16[128,2048]{1,0:T(8,128)(2,1)S(1)} %copy-done, f32[1,2048]{1,0:T(1,128)S(1)} %bitcast.1, bf16[128,2048]{1,0:T(8,128)(2,1)S(1)} %get-tuple-element.25.mixed_ref, bf16[2048,128]{1,0:T(8,128)(2,1)S(1)} %get-tuple-element.26.home_ref, bf16[256,128]{1,0:T(8,128)(2,1)S(1)} %get-tuple-element.38.refs_0_, ...), custom_call_target="tpu_custom_call" | custom-call | tf_op jit(solution)/shard_map/pallas_call | solution.py:276
  35.4 0.0 collective-permute-done.7.refs_0_
  35.4 0.1 shard_map.59
Async XLA Ops:
  0.0 34.4 %copy-start = (bf16[128,2048]{1,0:T(8,128)(2,1)S(1)}, bf16[128,2048]{1,0:T(8,128)(2,1)}, u32[]{:S(2)}) copy-start(bf16[128,2048]{1,0:T(8,128)(2,1)} %query_ref.3) | copy-start | bytes 1572868
  0.0 34.4 %copy-start.1 = (f32[2048]{0:T(1024)S(1)}, f32[2048]{0:T(1024)}, u32[]{:S(2)}) copy-start(f32[2048]{0:T(1024)} %param.9) | copy-start | bytes 24580
  2.9 8.2 %collective-permute-start.1 = (bf16[272,128]{1,0:T(8,128)(2,1)S(1)}, bf16[272,128]{1,0:T(8,128)(2,1)S(1)}, u32[]{:S(2)}, u32[]{:S(2)}) collective-permute-start(bf16[272,128]{1,0:T(8,128)(2,1)S(1)} %get-tuple-element.29), channel_id=1, source_target_pairs={{0,24},{1,25},{2,26},{3,27},{4,28},{5,29},{6,30},{7,31},{8,16},{9,... | collective-permute-start | bytes 208904 | tf_op jit(solution)/shard_map/ppermute | solution.py:40
  6.7 7.3 %collective-permute-start.2 = (bf16[272,128]{1,0:T(8,128)(2,1)S(1)}, bf16[272,128]{1,0:T(8,128)(2,1)S(1)}, u32[]{:S(2)}, u32[]{:S(2)}) collective-permute-start(bf16[272,128]{1,0:T(8,128)(2,1)S(1)} %get-tuple-element.30), channel_id=1, source_target_pairs={{0,4},{1,5},{2,6},{3,7},{4,0},{5,1},{6,2},{7,3},{8,12},{9,13},{10,... | collective-permute-start | bytes 208904 | tf_op jit(solution)/shard_map/ppermute | solution.py:40
  8.2 6.6 %collective-permute-start.3 = (bf16[272,128]{1,0:T(8,128)(2,1)S(1)}, bf16[272,128]{1,0:T(8,128)(2,1)S(1)}, u32[]{:S(2)}, u32[]{:S(2)}) collective-permute-start(bf16[272,128]{1,0:T(8,128)(2,1)S(1)} %get-tuple-element.31), channel_id=1, source_target_pairs={{0,16},{1,17},{2,18},{3,19},{4,20},{5,21},{6,22},{7,23},{8,24},{9,... | collective-permute-start | bytes 208904 | tf_op jit(solution)/shard_map/ppermute | solution.py:40
  8.2 6.6 %collective-permute-start.4 = (bf16[272,128]{1,0:T(8,128)(2,1)S(1)}, bf16[272,128]{1,0:T(8,128)(2,1)S(1)}, u32[]{:S(2)}, u32[]{:S(2)}) collective-permute-start(bf16[272,128]{1,0:T(8,128)(2,1)S(1)} %get-tuple-element.32), channel_id=1, source_target_pairs={{0,8},{1,9},{2,10},{3,11},{4,12},{5,13},{6,14},{7,15},{8,0},{9,1},... | collective-permute-start | bytes 208904 | tf_op jit(solution)/shard_map/ppermute | solution.py:40
  9.0 7.9 %collective-permute-start.5 = (bf16[272,128]{1,0:T(8,128)(2,1)S(1)}, bf16[272,128]{1,0:T(8,128)(2,1)S(1)}, u32[]{:S(2)}, u32[]{:S(2)}) collective-permute-start(bf16[272,128]{1,0:T(8,128)(2,1)S(1)} %get-tuple-element.33), channel_id=1, source_target_pairs={{0,20},{1,21},{2,22},{3,23},{4,16},{5,17},{6,18},{7,19},{8,28},{9,... | collective-permute-start | bytes 208904 | tf_op jit(solution)/shard_map/ppermute | solution.py:40
  11.1 5.8 %collective-permute-start.6 = (bf16[272,128]{1,0:T(8,128)(2,1)S(1)}, bf16[272,128]{1,0:T(8,128)(2,1)S(1)}, u32[]{:S(2)}, u32[]{:S(2)}) collective-permute-start(bf16[272,128]{1,0:T(8,128)(2,1)S(1)} %get-tuple-element.34), channel_id=1, source_target_pairs={{0,12},{1,13},{2,14},{3,15},{4,8},{5,9},{6,10},{7,11},{8,4},{9,5},... | collective-permute-start | bytes 208904 | tf_op jit(solution)/shard_map/ppermute | solution.py:40
  14.0 7.0 %collective-permute-start = (bf16[272,128]{1,0:T(8,128)(2,1)S(1)}, bf16[272,128]{1,0:T(8,128)(2,1)S(1)}, u32[]{:S(2)}, u32[]{:S(2)}) collective-permute-start(bf16[272,128]{1,0:T(8,128)(2,1)S(1)} %get-tuple-element.27), channel_id=1, source_target_pairs={{0,28},{1,29},{2,30},{3,31},{4,24},{5,25},{6,26},{7,27},{8,20},{9,... | collective-permute-start | bytes 208904 | tf_op jit(solution)/shard_map/ppermute | solution.py:40
  22.1 7.1 %collective-permute-start.8 = (bf16[256,128]{1,0:T(8,128)(2,1)S(1)}, bf16[256,128]{1,0:T(8,128)(2,1)S(1)}, u32[]{:S(2)}, u32[]{:S(2)}) collective-permute-start(bf16[256,128]{1,0:T(8,128)(2,1)S(1)} %get-tuple-element.39), channel_id=1, source_target_pairs={{0,16},{1,17},{2,18},{3,19},{4,20},{5,21},{6,22},{7,23},{8,24},{9,... | collective-permute-start | bytes 196616 | tf_op jit(solution)/shard_map/ppermute | solution.py:40
  22.5 6.8 %collective-permute-start.9 = (bf16[256,128]{1,0:T(8,128)(2,1)S(1)}, bf16[256,128]{1,0:T(8,128)(2,1)S(1)}, u32[]{:S(2)}, u32[]{:S(2)}) collective-permute-start(bf16[256,128]{1,0:T(8,128)(2,1)S(1)} %get-tuple-element.40), channel_id=1, source_target_pairs={{0,4},{1,5},{2,6},{3,7},{4,0},{5,1},{6,2},{7,3},{8,12},{9,13},{10,... | collective-permute-start | bytes 196616 | tf_op jit(solution)/shard_map/ppermute | solution.py:40
  23.1 9.4 %collective-permute-start.10 = (bf16[256,128]{1,0:T(8,128)(2,1)S(1)}, bf16[256,128]{1,0:T(8,128)(2,1)S(1)}, u32[]{:S(2)}, u32[]{:S(2)}) collective-permute-start(bf16[256,128]{1,0:T(8,128)(2,1)S(1)} %get-tuple-element.41), channel_id=1, source_target_pairs={{0,28},{1,29},{2,30},{3,31},{4,24},{5,25},{6,26},{7,27},{8,20},{9,... | collective-permute-start | bytes 196616 | tf_op jit(solution)/shard_map/ppermute | solution.py:40
  24.7 7.7 %collective-permute-start.11 = (bf16[256,128]{1,0:T(8,128)(2,1)S(1)}, bf16[256,128]{1,0:T(8,128)(2,1)S(1)}, u32[]{:S(2)}, u32[]{:S(2)}) collective-permute-start(bf16[256,128]{1,0:T(8,128)(2,1)S(1)} %get-tuple-element.42), channel_id=1, source_target_pairs={{0,8},{1,9},{2,10},{3,11},{4,12},{5,13},{6,14},{7,15},{8,0},{9,1},... | collective-permute-start | bytes 196616 | tf_op jit(solution)/shard_map/ppermute | solution.py:40
  27.1 6.2 %collective-permute-start.12 = (bf16[256,128]{1,0:T(8,128)(2,1)S(1)}, bf16[256,128]{1,0:T(8,128)(2,1)S(1)}, u32[]{:S(2)}, u32[]{:S(2)}) collective-permute-start(bf16[256,128]{1,0:T(8,128)(2,1)S(1)} %get-tuple-element.43), channel_id=1, source_target_pairs={{0,24},{1,25},{2,26},{3,27},{4,28},{5,29},{6,30},{7,31},{8,16},{9,... | collective-permute-start | bytes 196616 | tf_op jit(solution)/shard_map/ppermute | solution.py:40
  29.3 5.2 %collective-permute-start.13 = (bf16[256,128]{1,0:T(8,128)(2,1)S(1)}, bf16[256,128]{1,0:T(8,128)(2,1)S(1)}, u32[]{:S(2)}, u32[]{:S(2)}) collective-permute-start(bf16[256,128]{1,0:T(8,128)(2,1)S(1)} %get-tuple-element.44), channel_id=1, source_target_pairs={{0,12},{1,13},{2,14},{3,15},{4,8},{5,9},{6,10},{7,11},{8,4},{9,5},... | collective-permute-start | bytes 196616 | tf_op jit(solution)/shard_map/ppermute | solution.py:40
  29.3 6.2 %collective-permute-start.7 = (bf16[256,128]{1,0:T(8,128)(2,1)S(1)}, bf16[256,128]{1,0:T(8,128)(2,1)S(1)}, u32[]{:S(2)}, u32[]{:S(2)}) collective-permute-start(bf16[256,128]{1,0:T(8,128)(2,1)S(1)} %get-tuple-element.37), channel_id=1, source_target_pairs={{0,20},{1,21},{2,22},{3,23},{4,16},{5,17},{6,18},{7,19},{8,28},{9,... | collective-permute-start | bytes 196616 | tf_op jit(solution)/shard_map/ppermute | solution.py:40
